TPU v7x, 32 devices: a whole 2x2x4 slice. The times are simulated.
32 devices in a mesh: wide: 16 (over z, y, x), narrow: 2 (over core).
Axes of the slice: x: 2, y: 2, z: 4, core: 2. Of those that a mesh axis runs over, the one named last changes fastest.
Arguments:
- tokens: bfloat16 [2048, 2048], P('wide', 'narrow'), may hold values from -6 to 6
- expert_ids: int32 [2048, 6], P('wide'), may hold values from 0 to 15, all different within a row; in each aligned block of 128 rows (0 to 127, 128 to 255, ...) at most 54 rows name the same one
- route_gates: float32 [2048, 6], P('wide'), may hold values from 0.05 to 0.6
- expert_gate: bfloat16 [16, 1408, 2048], P('wide', 'narrow'), may hold values from -0.125 to 0.125
- expert_up: bfloat16 [16, 1408, 2048], P('wide', 'narrow'), may hold values from -0.125 to 0.125
- expert_down: bfloat16 [16, 1408, 2048], P('wide', 'narrow'), may hold values from -0.21875 to 0.21875
- shared_gate: bfloat16 [2048, 2816], P('wide', 'narrow'), may hold values from -0.125 to 0.125
- shared_up: bfloat16 [2048, 2816], P('wide', 'narrow'), may hold values from -0.125 to 0.125
- shared_down: bfloat16 [2816, 2048], P('narrow', 'wide'), may hold values from -0.15625 to 0.15625
Outputs:
- mixed: bfloat16 [2048, 2048], P('wide', 'narrow')
Inputs may be any that keep to these rules, and one draw needn't show every extreme that they name: `expert_ids`: each row names 6 different experts. Among the rows of one index of wide no expert is named by more than 54 rows, a bound that some block reaches of them.
All inputs are finite; a program needn't handle non-finite values.
Results may differ from a plain program's by a relative error of at most 0.019.
Values may be sent and summed in bfloat16 or wider, within the bound.
No kernel may reach another device: no remote copies, remote signals or barrier semaphores. Data moves between devices by JAX's collectives and lax.ppermute only.
A program may use at most 64 MiB of HBM per device.

v0:
```python
import functools
import jax
import jax.numpy as jnp
from jax import lax
from jax.experimental import pallas as pl
from jax.experimental.pallas import tpu as pltpu
from jax.sharding import PartitionSpec as P

PLANE = 4
TILE = 256
OUT_TILE = 512
VMEM_BYTES = 60 * 1024 * 1024


def dot_t(rows, weight):
    return lax.dot_general(rows, weight, (((1,), (1,)), ((), ())), preferred_element_type=jnp.float32)


def launch(copies, sems, src, dst):
    copy = pltpu.make_async_copy(src, dst, sems.at[len(copies)])
    copy.start()
    copies.append(copy)


def row_chunks(count):
    size = count // 4 if count % 64 == 0 else count
    return [(first, size) for first in range(0, count, size)]


def fill(rows, blocks):
    step = blocks[0].shape[0]
    for k, block in enumerate(blocks):
        rows[k * step : (k + 1) * step, :] = block[...]


def gated(rows, w_gate, w_up, lower, upper):
    pre = dot_t(rows[...], w_gate[lower:upper, :])
    return jax.nn.silu(pre) * dot_t(rows[...], w_up[lower:upper, :])


def tiles(first, end):
    return [(lower, min(end, lower + TILE)) for lower in range(first, end, TILE)]


def gate_column(gates, plane, expert):
    line = gates[plane, expert : expert + 1, :]
    return jnp.broadcast_to(line, (128, line.shape[1])).T[:, 0:1]


def launch_projections(copies, sems, sources, w_gate, w_up):
    firsts, base = [], 0
    for gate, up in sources:
        for first, size in row_chunks(gate.shape[0]):
            into = pl.ds(base + first, size)
            launch(copies, sems, gate.at[pl.ds(first, size)], w_gate.at[into])
            launch(copies, sems, up.at[pl.ds(first, size)], w_up.at[into])
            firsts.append(base + first)
        base += gate.shape[0]
    return firsts


def wait_rows(copies, firsts, ready, upper):
    while ready < len(firsts) and firsts[ready] < upper:
        copies[2 * ready].wait()
        copies[2 * ready + 1].wait()
        ready += 1
    return ready


def hidden_kernel(count, *refs):
    blocks = refs[: -2 * count - 5]
    sources = refs[-2 * count - 5 : -5]
    out, rows, w_gate, w_up, sems = refs[-5:]
    copies = []
    sources = [(sources[2 * i], sources[2 * i + 1]) for i in range(count)]
    firsts = launch_projections(copies, sems, sources, w_gate, w_up)
    fill(rows, blocks)
    ready = 0
    for lower, upper in tiles(0, w_gate.shape[0]):
        ready = wait_rows(copies, firsts, ready, upper)
        out[:, lower:upper] = gated(rows, w_gate, w_up, lower, upper).astype(jnp.bfloat16)


def expert_hidden(blocks, pieces):
    step, width = blocks[0].shape
    depth = step * len(blocks)
    total = sum(piece[0].shape[0] for piece in pieces)
    held = pltpu.VMEM((total, width), jnp.bfloat16)
    sems = 2 * sum(len(row_chunks(piece[0].shape[0])) for piece in pieces)
    return pl.pallas_call(
        functools.partial(hidden_kernel, len(pieces)),
        out_shape=jax.ShapeDtypeStruct((depth, total), jnp.bfloat16),
        in_specs=[pl.BlockSpec(memory_space=pltpu.VMEM)] * len(blocks)
        + [pl.BlockSpec(memory_space=pl.ANY)] * (2 * len(pieces)),
        out_specs=pl.BlockSpec(memory_space=pltpu.VMEM),
        scratch_shapes=[
            pltpu.VMEM((depth, width), jnp.bfloat16),
            held,
            held,
            pltpu.SemaphoreType.DMA((sems,)),
        ],
        compiler_params=pltpu.CompilerParams(vmem_limit_bytes=VMEM_BYTES),
        cost_estimate=pl.CostEstimate(
            flops=4 * depth * width * total,
            bytes_accessed=4 * total * width,
            transcendentals=depth * total,
        ),
    )(*blocks, *[w for piece in pieces for w in piece[:2]])


def layer_kernel(plan, *refs):
    experts, plane, x_first, ties, count, skip = plan
    blocks, gates, shared = refs[:4], refs[4], refs[5]
    refs = refs[6:]
    acts = None
    if skip is not None:
        acts, refs = refs[0], refs[1:]
    pieces = [refs[3 * i : 3 * i + 3] for i in range(count)]
    keep, send, rows, w_gate, w_up, w_down, hidden, sems = refs[3 * count + ties :]
    step, width = blocks[0].shape
    size, units = pieces[0][0].shape[0], shared.shape[1]
    base = size * count
    copies = []
    sources = [piece[:2] for piece in pieces] if acts is None else []
    sources.append((shared.at[0], shared.at[1]))
    firsts = launch_projections(copies, sems, sources, w_gate, w_up)
    head = len(copies)
    for lower in range(0, width, OUT_TILE):
        columns = pl.ds(lower, OUT_TILE)
        for i, piece in enumerate(pieces):
            part = w_down.at[pl.ds(i * size, size), columns]
            launch(copies, sems, piece[2].at[:, columns], part)
        launch(copies, sems, shared.at[2].at[:, columns], w_down.at[pl.ds(base, units), columns])
    fill(rows, blocks)
    ready = 0
    for e in range(experts):
        column = gate_column(gates, plane, e)
        for lower, upper in tiles(e * base // experts, (e + 1) * base // experts):
            if acts is None:
                ready = wait_rows(copies, firsts, ready, upper)
                value = gated(rows, w_gate, w_up, lower, upper)
            else:
                value = acts[skip : skip + PLANE * step, lower:upper].astype(jnp.float32)
            hidden[:, lower:upper] = (value * column).astype(jnp.bfloat16)
    wait_rows(copies, firsts, ready, base + units)
    offset = 0 if acts is not None else base
    value = gated(rows, w_gate, w_up, offset, offset + units)
    hidden[:, base:] = value.astype(jnp.bfloat16)
    kept, sent = ((0, 2), (1, 3)) if x_first else ((0, 1), (2, 3))
    for n in range(width // OUT_TILE):
        lower, upper = n * OUT_TILE, (n + 1) * OUT_TILE
        for copy in copies[head + n * (count + 1) : head + (n + 1) * (count + 1)]:
            copy.wait()
        part = jnp.dot(hidden[...], w_down[:, lower:upper], preferred_element_type=jnp.float32)
        part = part.astype(jnp.bfloat16)
        for ref, which in ((keep, kept), (send, sent)):
            for j, k in enumerate(which):
                ref[j, :, lower:upper] = part[k * step : (k + 1) * step]


def layer(blocks, gates, shared, acts, skip, pieces, experts, plane, x_first, after):
    step, width = blocks[0].shape
    units, count = shared.shape[1], len(pieces)
    total = count * pieces[0][0].shape[0] + units
    worked = total if acts is None else units
    depth = PLANE * step
    pair = jax.ShapeDtypeStruct((2, step, width), jnp.bfloat16)
    held = pltpu.VMEM((worked, width), jnp.bfloat16)
    sems = 2 * count * len(row_chunks(pieces[0][0].shape[0])) + 2 * len(row_chunks(units))
    sems += (width // OUT_TILE) * (count + 1)
    given = [] if acts is None else [acts]
    plan = (experts, plane, x_first, len(after), count, None if acts is None else skip)
    return pl.pallas_call(
        functools.partial(layer_kernel, plan),
        out_shape=[pair] * 2,
        in_specs=[pl.BlockSpec(memory_space=pltpu.VMEM)] * 5
        + [pl.BlockSpec(memory_space=pl.ANY)]
        + [pl.BlockSpec(memory_space=pltpu.VMEM)] * len(given)
        + [pl.BlockSpec(memory_space=pl.ANY)] * (3 * count + len(after)),
        out_specs=[pl.BlockSpec(memory_space=pltpu.VMEM)] * 2,
        scratch_shapes=[
            pltpu.VMEM((depth, width), jnp.bfloat16),
            held,
            held,
            pltpu.VMEM((total, width), jnp.bfloat16),
            pltpu.VMEM((depth, total), jnp.bfloat16),
            pltpu.SemaphoreType.DMA((sems,)),
        ],
        compiler_params=pltpu.CompilerParams(vmem_limit_bytes=VMEM_BYTES),
        cost_estimate=pl.CostEstimate(
            flops=2 * depth * width * (total + 2 * worked),
            bytes_accessed=2 * (total + 2 * worked) * width,
            transcendentals=depth * worked,
        ),
    )(*blocks, gates, shared, *given, *[w for piece in pieces for w in piece], *after)


def cut_kernel(units, padded, gate, up, down, coded, out):
    wide, chunk = out.shape[0], out.shape[2]
    gate_t, up_t = gate[...].T, up[...].T
    blank = jnp.zeros((padded - units, chunk), jnp.bfloat16)
    for w in range(wide):
        part = slice(w * units, (w + 1) * units)
        out[w, 0:units, :] = gate_t[part]
        out[w, units:padded, :] = coded[w]
        out[w, padded : padded + units, :] = up_t[part]
        out[w, padded + units : 2 * padded, :] = blank
        out[w, 2 * padded : 2 * padded + units, :] = down[part, :]
        out[w, 2 * padded + units : 3 * padded, :] = blank


def cut(gate, up, down, coded, units, padded):
    wide, chunk = coded.shape[0], down.shape[1]
    coded = coded.reshape(wide, padded - units, chunk)
    if chunk % 128 == 0 and units % 8 == 0 and units * wide == gate.shape[1]:
        return pl.pallas_call(
            functools.partial(cut_kernel, units, padded),
            out_shape=jax.ShapeDtypeStruct((wide, 3 * padded, chunk), jnp.bfloat16),
            in_specs=[pl.BlockSpec(memory_space=pltpu.VMEM)] * 4,
            out_specs=pl.BlockSpec(memory_space=pltpu.VMEM),
            compiler_params=pltpu.CompilerParams(vmem_limit_bytes=VMEM_BYTES),
            cost_estimate=pl.CostEstimate(
                flops=0, bytes_accessed=16 * down.size, transcendentals=0
            ),
        )(gate, up, down, coded)
    parts = []
    blank = jnp.zeros((wide, padded - units, chunk), jnp.bfloat16)
    for weight, tail in ((gate.T, coded), (up.T, blank), (down, blank)):
        weight = jnp.pad(weight, ((0, units * wide - weight.shape[0]), (0, 0)))
        parts += [weight.reshape(wide, units, chunk), tail]
    return jnp.concatenate(parts, axis=1)


def lay_out_kernel(units, *refs):
    parts, out = refs[:-1], refs[-1]
    for s, part in enumerate(parts):
        wide, _, chunk = part.shape
        for kind in range(3):
            for w in range(wide):
                out[kind, s * units : (s + 1) * units, w * chunk : (w + 1) * chunk] = part[
                    w, kind * units : (kind + 1) * units, :
                ]


def lay_out(parts, units, width):
    if parts[0].shape[2] % 128:
        shaped = [p.reshape(p.shape[0], 3, units, p.shape[2]) for p in parts]
        shaped = [jnp.transpose(p, (1, 2, 0, 3)).reshape(3, units, width) for p in shaped]
        return jnp.concatenate(shaped, axis=1)
    return pl.pallas_call(
        functools.partial(lay_out_kernel, units),
        out_shape=jax.ShapeDtypeStruct((3, units * len(parts), width), jnp.bfloat16),
        in_specs=[pl.BlockSpec(memory_space=pltpu.VMEM)] * len(parts),
        out_specs=pl.BlockSpec(memory_space=pltpu.VMEM),
        compiler_params=pltpu.CompilerParams(vmem_limit_bytes=VMEM_BYTES),
        cost_estimate=pl.CostEstimate(
            flops=0, bytes_accessed=12 * units * len(parts) * width, transcendentals=0
        ),
    )(*parts)


def body(
    tokens,
    expert_ids,
    route_gates,
    expert_gate,
    expert_up,
    expert_down,
    shared_gate,
    shared_up,
    shared_down,
):
    wide = lax.axis_size("wide")
    narrow = lax.axis_size("narrow")
    lines = wide // PLANE
    tok_rows = tokens.shape[0]
    own_rows = tok_rows // narrow
    local_experts = expert_gate.shape[0]
    width = expert_gate.shape[2]
    experts_all = local_experts * wide
    here = lax.axis_index("wide")
    core = lax.axis_index("narrow")

    def flip(value, bits):
        return lax.ppermute(value, "wide", [(w, w ^ bits) for w in range(wide)])

    def shift(value, by):
        return lax.ppermute(
            value, "wide", [(w, (w + PLANE * by) % wide) for w in range(wide)]
        )

    def turn(value, by):
        return lax.ppermute(value, "narrow", [(c, (c + by) % narrow) for c in range(narrow)])

    mine = lax.all_to_all(tokens, "narrow", split_axis=0, concat_axis=1, tiled=True)

    own_ids = lax.dynamic_slice_in_dim(expert_ids, core * own_rows, own_rows, 0)
    own_gates = lax.dynamic_slice_in_dim(route_gates, core * own_rows, own_rows, 0)
    numbers = jnp.arange(experts_all, dtype=jnp.int32)
    chosen = own_ids.T[:, None, :] == numbers[None, :, None]
    table = jnp.sum(jnp.where(chosen, own_gates.T[:, None, :], 0.0), axis=0)
    table = table.reshape(wide, local_experts * own_rows)
    high = table.astype(jnp.bfloat16)
    low = (table - high.astype(jnp.float32)).astype(jnp.bfloat16)
    coded = jnp.concatenate([high, low], axis=1)

    hidden_local = shared_gate.shape[1]
    units = -(-hidden_local // wide)
    chunk = shared_down.shape[1]
    gate_rows = -(-coded.shape[1] // chunk)
    padded = -(-(units + gate_rows) // 16) * 16
    coded = jnp.pad(coded, ((0, 0), (0, (padded - units) * chunk - coded.shape[1])))
    stacked = cut(shared_gate, shared_up, shared_down, coded, units, padded)

    near = sorted({1, lines - 1} - {0, lines})
    rest = [d for d in range(1, lines) if d not in near]
    planes = rest + near + [0]
    x_first = {d: n % 2 == 0 for n, d in enumerate(planes)}
    lined, by_x, by_y = {0: mine}, {}, {}
    for d in near:
        lined[d] = shift(mine, d)
    by_x[0], by_y[0] = flip(mine, 1), flip(mine, 2)
    pieces = []
    for e in range(local_experts):
        for t in range(narrow):
            piece = (expert_gate[e], expert_up[e], expert_down[e])
            pieces.append(tuple(turn(w, t) for w in piece) if t else piece)
    lined, by_x, by_y, stacked, pieces = lax.optimization_barrier(
        (lined, by_x, by_y, stacked, pieces)
    )
    for d in rest:
        lined[d] = shift(lined[0], d)
    for d in near:
        by_x[d], by_y[d] = flip(lined[d], 1), flip(lined[d], 2)
    lined, by_x, by_y, stacked = lax.optimization_barrier((lined, by_x, by_y, stacked))
    recut = lax.all_to_all(stacked, "wide", split_axis=0, concat_axis=0, tiled=True)
    for d in rest:
        by_x[d], by_y[d] = flip(lined[d], 1), flip(lined[d], 2)
    blocks = {}
    for d in near[1:] + [0] + near[:1] + rest:
        far = flip(by_x[d], 2) if x_first[d] else flip(by_y[d], 1)
        blocks[d] = (lined[d], by_x[d], by_y[d], far)
    early = planes[-2:]
    acts = expert_hidden([block for d in early for block in blocks[d]], pieces)
    recut, blocks, acts = lax.optimization_barrier((recut, blocks, acts))
    shared = lay_out([recut] + [turn(recut, s) for s in range(1, narrow)], padded, width)
    coded = recut[:, units : units + gate_rows].reshape(wide, gate_rows * chunk)
    coded = coded.astype(jnp.float32)
    size = local_experts * own_rows
    table = (coded[:, :size] + coded[:, size : 2 * size]).reshape(wide, local_experts, own_rows)

    order = jnp.arange(wide, dtype=jnp.int32)
    line, place = here // PLANE, here % PLANE
    source = ((line - order // PLANE) % lines) * PLANE + (place ^ (order % PLANE))
    picks = source[:, None] == jnp.arange(wide, dtype=jnp.int32)[None, :]
    gates = jnp.sum(jnp.where(picks[:, :, None, None], table[None], 0.0), axis=1)
    gates = jnp.transpose(gates.reshape(lines, PLANE, local_experts, own_rows), (0, 2, 1, 3))
    gates = gates.reshape(lines, local_experts, PLANE * own_rows)

    kept, came, onwards = [], [], {}

    def pass_on(m, later):
        came[m], kept[later] = lax.optimization_barrier((came[m], kept[later]))
        got = came[m].astype(jnp.float32)
        onwards[m] = (kept[m][1].astype(jnp.float32) + got[1]).astype(jnp.bfloat16)

    for n, d in enumerate(planes):
        after = [kept[n - 1]] if n else []
        if 2 <= n < lines - 1:
            after.append(onwards[n - 2])
        ready = acts if d in early else None
        skip = early.index(d) * PLANE * own_rows if d in early else None
        keep, send = layer(
            blocks[d], gates, shared, ready, skip, pieces, local_experts, d, x_first[d], after
        )
        kept.append(keep)
        came.append(flip(send, 1 if x_first[d] else 2))
        if 1 <= n < lines - 2:
            pass_on(n - 1, n)
    for m in range(max(0, lines - 3), lines):
        pass_on(m, lines - 1)
    out = None
    for n, d in enumerate(planes):
        total = kept[n][0].astype(jnp.float32) + came[n][0].astype(jnp.float32)
        total = total + flip(onwards[n], 2 if x_first[d] else 1).astype(jnp.float32)
        if d:
            total = shift(total.astype(jnp.bfloat16), -d).astype(jnp.float32)
        out = total if out is None else out + total
    return lax.all_to_all(
        out.astype(jnp.bfloat16), "narrow", split_axis=1, concat_axis=0, tiled=True
    )


def solution(mesh):
    return jax.shard_map(
        body,
        mesh=mesh,
        in_specs=(
            P("wide", "narrow"),
            P("wide", None),
            P("wide", None),
            P("wide", "narrow", None),
            P("wide", "narrow", None),
            P("wide", "narrow", None),
            P("wide", "narrow"),
            P("wide", "narrow"),
            P("narrow", "wide"),
        ),
        out_specs=P("wide", "narrow"),
        check_vma=False,
    )
```

profile of v0, /device:TPU:0, one launch (start us, length us, event | category | flops | bytes accessed | tf_op | source)
XLA Modules:
  0.0 185.6 jit_solution(303513460323106451)
XLA Ops:
  1.0 9.0 %all_to_all.43 = bf16[2,64,1024]{2,1,0:T(8,128)(2,1)S(1)} all-to-all(bf16[2,64,1024]{2,1,0:T(8,128)(2,1)} %bitcast.76), channel_id=1, replica_groups=mesh['wide'=16,'narrow'=2] {'narrow'}, dimensions={0} | all-to-all | bytes 524288 | tf_op jit(solution)/shard_map/all_to_all | solution.py:295
  10.0 2.4 %collective-permute-start = (bf16[64,2048]{1,0:T(8,128)(2,1)S(1)}, bf16[64,2048]{1,0:T(8,128)(2,1)}, u32[]{:S(2)}, u32[]{:S(2)}) collective-permute-start(bf16[64,2048]{1,0:T(8,128)(2,1)S(1)} %bitcast.65), channel_id=1, source_target_pairs={{0,8},{2,10},{4,12},{6,14},{8,16},{10,18},{12,20},{14,22},{16,24},... | collective-permute-start | bytes 786440 | tf_op jit(solution)/shard_map/ppermute | solution.py:288
  12.4 2.1 %collective-permute-start.1 = (bf16[64,2048]{1,0:T(8,128)(2,1)S(1)}, bf16[64,2048]{1,0:T(8,128)(2,1)S(1)}, u32[]{:S(2)}, u32[]{:S(2)}) collective-permute-start(bf16[64,2048]{1,0:T(8,128)(2,1)S(1)} %bitcast.66), channel_id=1, source_target_pairs={{0,24},{2,26},{4,28},{6,30},{8,0},{10,2},{12,4},{14,6},{16,8},{18,... | collective-permute-start | bytes 786440 | tf_op jit(solution)/shard_map/ppermute | solution.py:288
  14.6 0.8 dynamic-slice_bitcast_fusion.1
  15.3 6.3 %collective-permute-done.refs_0_ = bf16[64,2048]{1,0:T(8,128)(2,1)} collective-permute-done((bf16[64,2048]{1,0:T(8,128)(2,1)S(1)}, bf16[64,2048]{1,0:T(8,128)(2,1)}, u32[]{:S(2)}, u32[]{:S(2)}) %collective-permute-start) | collective-permute-done | bytes 262176 | tf_op jit(solution)/shard_map/ppermute | solution.py:288
  21.7 1.7 collective-permute-start.2
  23.4 2.7 %collective-permute-done.1.refs_0_ = bf16[64,2048]{1,0:T(8,128)(2,1)S(1)} collective-permute-done((bf16[64,2048]{1,0:T(8,128)(2,1)S(1)}, bf16[64,2048]{1,0:T(8,128)(2,1)S(1)}, u32[]{:S(2)}, u32[]{:S(2)}) %collective-permute-start.1) | collective-permute-done | bytes 262176 | tf_op jit(solution)/shard_map/ppermute | solution.py:288
  26.1 1.5 collective-permute-start.3
  28.3 2.4 %shard_map.91 = bf16[16,288,128]{2,1,0:T(8,128)(2,1)} custom-call(bf16[128,1408]{1,0:T(8,128)(2,1)} %gate.1, bf16[128,1408]{1,0:T(8,128)(2,1)} %up.1, bf16[1408,128]{1,0:T(8,128)(2,1)} %down.1, bf16[16,8,128]{2,1,0:T(8,128)(2,1)} %bitcast.77), custom_call_target="tpu_custom_call" | custom-call | bytes 2883584 | tf_op jit(solution)/shard_map/pallas_call | solution.py:216
  30.8 3.0 %collective-permute-done.3.refs_6_.refs_2_ = bf16[64,2048]{1,0:T(8,128)(2,1)S(1)} collective-permute-done((bf16[64,2048]{1,0:T(8,128)(2,1)S(1)}, bf16[64,2048]{1,0:T(8,128)(2,1)S(1)}, u32[]{:S(2)}, u32[]{:S(2)}) %collective-permute-start.3) | collective-permute-done | bytes 262176 | tf_op jit(solution)/shard_map/ppermute | solution.py:285
  33.8 1.6 collective-permute-start.10
  35.3 1.5 collective-permute-start.8
  37.9 1.6 collective-permute-start.7
  39.5 3.8 %collective-permute-done.10.refs_2_ = bf16[64,2048]{1,0:T(8,128)(2,1)S(1)} collective-permute-done((bf16[64,2048]{1,0:T(8,128)(2,1)}, bf16[64,2048]{1,0:T(8,128)(2,1)S(1)}, u32[]{:S(2)}, u32[]{:S(2)}) %collective-permute-start.10) | collective-permute-done | bytes 262176 | tf_op jit(solution)/shard_map/ppermute | solution.py:285
  43.3 3.1 %collective-permute-done.11.refs_2_ = bf16[64,2048]{1,0:T(8,128)(2,1)S(1)} collective-permute-done((bf16[64,2048]{1,0:T(8,128)(2,1)S(1)}, bf16[64,2048]{1,0:T(8,128)(2,1)S(1)}, u32[]{:S(2)}, u32[]{:S(2)}) %collective-permute-start.11) | collective-permute-done | bytes 262176 | tf_op jit(solution)/shard_map/ppermute | solution.py:285
  46.4 1.2 collective-permute-done.9.refs_1_
  47.7 0.7 copy-done.13
  48.4 1.8 collective-permute-done.7.refs_0_
  50.1 4.7 %all-to-all-start.1 = ((bf16[16,288,128]{2,1,0:T(8,128)(2,1)}), bf16[16,288,128]{2,1,0:T(8,128)(2,1)}, u32[]{:S(2)}, u32[]{:S(2)}) async-start(bf16[16,288,128]{2,1,0:T(8,128)(2,1)} %shard_map.91), calls=%async_computation.1 | async-start | bytes 2359296 | tf_op jit(solution)/shard_map/all_to_all | solution.py:336
  54.8 1.9 %collective-permute-start.14 = (bf16[64,2048]{1,0:T(8,128)(2,1)}, bf16[64,2048]{1,0:T(8,128)(2,1)}, u32[]{:S(2)}, u32[]{:S(2)}) collective-permute-start(bf16[64,2048]{1,0:T(8,128)(2,1)} %collective-permute-done.7.refs_0_), channel_id=1, source_target_pairs={{0,2},{2,0},{4,6},{6,4},{8,10},{10,8},{12,14},{14,12},{16,18},{18,... | collective-permute-start | bytes 786440 | tf_op jit(solution)/shard_map/ppermute | solution.py:285
  56.9 1.8 collective-permute-start.17
  58.9 1.8 collective-permute-start.13
  60.8 12.7 %collective-permute-done.14.refs_1_ = bf16[64,2048]{1,0:T(8,128)(2,1)} collective-permute-done((bf16[64,2048]{1,0:T(8,128)(2,1)}, bf16[64,2048]{1,0:T(8,128)(2,1)}, u32[]{:S(2)}, u32[]{:S(2)}) %collective-permute-start.14) | collective-permute-done | bytes 262176 | tf_op jit(solution)/shard_map/ppermute | solution.py:285
  73.5 1.7 collective-permute-start.16
  75.2 7.2 %collective-permute-done.12.refs_7_.refs_3_ = bf16[64,2048]{1,0:T(8,128)(2,1)S(1)} collective-permute-done((bf16[64,2048]{1,0:T(8,128)(2,1)}, bf16[64,2048]{1,0:T(8,128)(2,1)S(1)}, u32[]{:S(2)}, u32[]{:S(2)}) %collective-permute-start.12) | collective-permute-done | bytes 262176 | tf_op jit(solution)/shard_map/ppermute | solution.py:285
  83.8 12.1 %shard_map.92.refs_6_ = bf16[512,1408]{1,0:T(8,128)(2,1)} custom-call(bf16[64,2048]{1,0:T(8,128)(2,1)} %copy-done.9, bf16[64,2048]{1,0:T(8,128)(2,1)} %copy-done.13, bf16[64,2048]{1,0:T(8,128)(2,1)} %copy-done.12, bf16[64,2048]{1,0:T(8,128)(2,1)} %copy-done.17, bf16[64,2048]{1,0:T(8,128)(2,1)} %bitcast.70, bf16[64,2048]{1,0:T(8,128)(2,1)} %copy-done.10, ...), custom_call_target="tpu_custom_call" | custom-call | flops 5905580032 | bytes 11534336 | tf_op jit(solution)/shard_map/pallas_call | solution.py:90
  96.2 0.8 slice_convert_fusion
  97.8 1.3 collective-permute-done.18.refs_1_
  99.1 1.0 copy-done.5
  100.1 3.6 %shard_map.93.refs_5_ = bf16[3,192,2048]{2,1,0:T(8,128)(2,1)} custom-call(bf16[16,288,128]{2,1,0:T(8,128)(2,1)} %all-to-all-done.1.refs_0_, bf16[16,288,128]{2,1,0:T(8,128)(2,1)} %copy-done.5), custom_call_target="tpu_custom_call" | custom-call | bytes 4718592 | tf_op jit(solution)/shard_map/pallas_call | solution.py:250
  103.7 11.9 %shard_map.94 = (bf16[2,64,2048]{2,1,0:T(8,128)(2,1)}, bf16[2,64,2048]{2,1,0:T(8,128)(2,1)}) custom-call(bf16[64,2048]{1,0:T(8,128)(2,1)} %collective-permute-done.7.refs_0_, bf16[64,2048]{1,0:T(8,128)(2,1)} %collective-permute-done.14.refs_1_, bf16[64,2048]{1,0:T(8,128)(2,1)} %collective-permute-done.15.refs_2_, ...), custom_call_target="tpu_custom_call" | custom-call | flops 5033164800 | bytes 19660800 | tf_op jit(solution)/shard_map/pallas_call | solution.py:173
  115.9 11.9 %shard_map.95 = (bf16[2,64,2048]{2,1,0:T(8,128)(2,1)}, bf16[2,64,2048]{2,1,0:T(8,128)(2,1)}) custom-call(bf16[64,2048]{1,0:T(8,128)(2,1)} %collective-permute-done.refs_0_, bf16[64,2048]{1,0:T(8,128)(2,1)} %copy-done.15, bf16[64,2048]{1,0:T(8,128)(2,1)} %copy-done.14, bf16[64,2048]{1,0:T(8,128)(2,1)} %collective-permute-done.13.refs_3_, ...), custom_call_target="tpu_custom_call" | custom-call | flops 5033164800 | bytes 19660800 | tf_op jit(solution)/shard_map/pallas_call | solution.py:173
  127.8 2.0 %collective-permute-start.22 = (bf16[2,64,2048]{2,1,0:T(8,128)(2,1)}, bf16[2,64,2048]{2,1,0:T(8,128)(2,1)S(1)}, u32[]{:S(2)}, u32[]{:S(2)}) collective-permute-start(bf16[2,64,2048]{2,1,0:T(8,128)(2,1)} %get-tuple-element.99), channel_id=1, source_target_pairs={{0,4},{2,6},{4,0},{6,2},{8,12},{10,14},{12,8},{14,10},{16,20},{18,... | collective-permute-start | bytes 1572872 | tf_op jit(solution)/shard_map/ppermute | solution.py:285
  130.1 1.5 collective-permute-start.20
  131.6 7.8 %shard_map.96 = (bf16[2,64,2048]{2,1,0:T(8,128)(2,1)}, bf16[2,64,2048]{2,1,0:T(8,128)(2,1)}) custom-call(bf16[64,2048]{1,0:T(8,128)(2,1)} %copy-done.9, bf16[64,2048]{1,0:T(8,128)(2,1)} %copy-done.13, bf16[64,2048]{1,0:T(8,128)(2,1)} %copy-done.12, bf16[64,2048]{1,0:T(8,128)(2,1)} %copy-done.17, f32[4,1,256]{2,1,0:T(1,128)} %reshape_transpose_reshape.3.refs_4_, ...), custom_call_target="tpu_custom_call" | custom-call | flops 2080374784 | bytes 8126464 | tf_op jit(solution)/shard_map/pallas_call | solution.py:173
  139.4 7.8 %shard_map.97 = (bf16[2,64,2048]{2,1,0:T(8,128)(2,1)}, bf16[2,64,2048]{2,1,0:T(8,128)(2,1)}) custom-call(bf16[64,2048]{1,0:T(8,128)(2,1)} %bitcast.71, bf16[64,2048]{1,0:T(8,128)(2,1)} %copy-done.10, bf16[64,2048]{1,0:T(8,128)(2,1)} %copy-done.11, bf16[64,2048]{1,0:T(8,128)(2,1)} %copy-done.16, f32[4,1,256]{2,1,0:T(1,128)} %reshape_transpose_reshape.3.refs_4_, ...), custom_call_target="tpu_custom_call" | custom-call | flops 2080374784 | bytes 8126464 | tf_op jit(solution)/shard_map/pallas_call | solution.py:173
  148.0 1.5 collective-permute-start.25
  150.2 2.4 %collective-permute-start.21 = (bf16[64,2048]{1,0:T(8,128)(2,1)S(1)}, bf16[64,2048]{1,0:T(8,128)(2,1)S(1)}, u32[]{:S(2)}, u32[]{:S(2)}) collective-permute-start(bf16[64,2048]{1,0:T(8,128)(2,1)S(1)} %fusion.4), channel_id=1, source_target_pairs={{0,16},{2,18},{4,20},{6,22},{8,24},{10,26},{12,28},{14,30},{16,0},... | collective-permute-start | bytes 786440 | tf_op jit(solution)/shard_map/ppermute | solution.py:288
  152.6 4.0 %collective-permute-done.23 = bf16[64,2048]{1,0:T(8,128)(2,1)S(1)} collective-permute-done((bf16[64,2048]{1,0:T(8,128)(2,1)S(1)}, bf16[64,2048]{1,0:T(8,128)(2,1)S(1)}, u32[]{:S(2)}, u32[]{:S(2)}) %collective-permute-start.23) | collective-permute-done | bytes 262176 | tf_op jit(solution)/shard_map/ppermute | solution.py:285
  156.8 1.7 collective-permute-start.24
  158.5 7.4 %collective-permute-done.25 = bf16[2,64,2048]{2,1,0:T(8,128)(2,1)S(1)} collective-permute-done((bf16[2,64,2048]{2,1,0:T(8,128)(2,1)S(1)}, bf16[2,64,2048]{2,1,0:T(8,128)(2,1)S(1)}, u32[]{:S(2)}, u32[]{:S(2)}) %collective-permute-start.25) | collective-permute-done | bytes 524320 | tf_op jit(solution)/shard_map/ppermute | solution.py:285
  166.0 1.0 collective-permute-start.26
  167.0 1.3 collective-permute-start.29
  168.3 4.1 %collective-permute-done.26 = bf16[64,2048]{1,0:T(8,128)(2,1)S(1)} collective-permute-done((bf16[64,2048]{1,0:T(8,128)(2,1)S(1)}, bf16[64,2048]{1,0:T(8,128)(2,1)S(1)}, u32[]{:S(2)}, u32[]{:S(2)}) %collective-permute-start.26) | collective-permute-done | bytes 262176 | tf_op jit(solution)/shard_map/ppermute | solution.py:285
  172.5 1.2 collective-permute-start.27
  173.7 7.0 %collective-permute-done.27 = bf16[64,2048]{1,0:T(8,128)(2,1)S(1)} collective-permute-done((bf16[64,2048]{1,0:T(8,128)(2,1)S(1)}, bf16[64,2048]{1,0:T(8,128)(2,1)S(1)}, u32[]{:S(2)}, u32[]{:S(2)}) %collective-permute-start.27) | collective-permute-done | bytes 262176 | tf_op jit(solution)/shard_map/ppermute | solution.py:288
  181.0 3.9 %all_to_all.44 = bf16[64,2,1024]{2,0,1:T(8,128)(2,1)S(1)} all-to-all(bf16[64,2,1024]{2,0,1:T(8,128)(2,1)S(1)} %bitcast.73), channel_id=1, replica_groups=mesh['wide'=16,'narrow'=2] {'narrow'}, dimensions={1} | all-to-all | bytes 524288 | tf_op jit(solution)/shard_map/all_to_all | solution.py:389
  184.9 0.7 copy.22
  (84 shorter events, 8.3 us)
Async XLA Ops:
  0.0 14.5 %copy-start = (f32[128,6]{0,1:T(8,128)S(1)}, f32[128,6]{0,1:T(8,128)}, u32[]{:S(2)}) copy-start(f32[128,6]{0,1:T(8,128)} %param.11) | copy-start | bytes 9220
  0.0 33.7 %collective-permute-start.4 = (bf16[704,2048]{1,0:T(8,128)(2,1)}, bf16[704,2048]{1,0:T(8,128)(2,1)S(1)}, u32[]{:S(2)}, u32[]{:S(2)}) collective-permute-start(bf16[704,2048]{1,0:T(8,128)(2,1)} %bitcast.48), channel_id=1, source_target_pairs={{0,1},{1,0},{2,3},{3,2},{4,5},{5,4},{6,7},{7,6},{8,9},{9,8},{10,11... | collective-permute-start | bytes 8650760 | tf_op jit(solution)/shard_map/ppermute | solution.py:293
  0.5 33.3 %collective-permute-start.5 = (bf16[704,2048]{1,0:T(8,128)(2,1)}, bf16[704,2048]{1,0:T(8,128)(2,1)}, u32[]{:S(2)}, u32[]{:S(2)}) collective-permute-start(bf16[704,2048]{1,0:T(8,128)(2,1)} %bitcast.54), channel_id=1, source_target_pairs={{0,1},{1,0},{2,3},{3,2},{4,5},{5,4},{6,7},{7,6},{8,9},{9,8},{10,11... | collective-permute-start | bytes 8650760 | tf_op jit(solution)/shard_map/ppermute | solution.py:293
  0.5 33.2 %collective-permute-start.6 = (bf16[704,2048]{1,0:T(8,128)(2,1)}, bf16[704,2048]{1,0:T(8,128)(2,1)}, u32[]{:S(2)}, u32[]{:S(2)}) collective-permute-start(bf16[704,2048]{1,0:T(8,128)(2,1)} %bitcast.60), channel_id=1, source_target_pairs={{0,1},{1,0},{2,3},{3,2},{4,5},{5,4},{6,7},{7,6},{8,9},{9,8},{10,11... | collective-permute-start | bytes 8650760 | tf_op jit(solution)/shard_map/ppermute | solution.py:293
  10.0 72.4 %copy-start.7 = (bf16[2,8,8,1024]{3,2,0,1:T(8,128)(2,1)}, bf16[2,8,8,1024]{3,2,0,1:T(8,128)(2,1)S(1)}, u32[]{:S(2)}) copy-start(bf16[2,8,8,1024]{3,2,0,1:T(8,128)(2,1)S(1)} %copy.17) | copy-start | bytes 786436
  10.0 11.6 %collective-permute-start = (bf16[64,2048]{1,0:T(8,128)(2,1)S(1)}, bf16[64,2048]{1,0:T(8,128)(2,1)}, u32[]{:S(2)}, u32[]{:S(2)}) collective-permute-start(bf16[64,2048]{1,0:T(8,128)(2,1)S(1)} %bitcast.65), channel_id=1, source_target_pairs={{0,8},{2,10},{4,12},{6,14},{8,16},{10,18},{12,20},{14,22},{16,24},... | collective-permute-start | bytes 786440 | tf_op jit(solution)/shard_map/ppermute | solution.py:288
  12.4 13.7 %collective-permute-start.1 = (bf16[64,2048]{1,0:T(8,128)(2,1)S(1)}, bf16[64,2048]{1,0:T(8,128)(2,1)S(1)}, u32[]{:S(2)}, u32[]{:S(2)}) collective-permute-start(bf16[64,2048]{1,0:T(8,128)(2,1)S(1)} %bitcast.66), channel_id=1, source_target_pairs={{0,24},{2,26},{4,28},{6,30},{8,0},{10,2},{12,4},{14,6},{16,8},{18,... | collective-permute-start | bytes 786440 | tf_op jit(solution)/shard_map/ppermute | solution.py:288
  21.7 9.1 %collective-permute-start.2 = (bf16[64,2048]{1,0:T(8,128)(2,1)S(1)}, bf16[64,2048]{1,0:T(8,128)(2,1)S(1)}, u32[]{:S(2)}, u32[]{:S(2)}) collective-permute-start(bf16[64,2048]{1,0:T(8,128)(2,1)S(1)} %bitcast.67), channel_id=1, source_target_pairs={{0,2},{2,0},{4,6},{6,4},{8,10},{10,8},{12,14},{14,12},{16,18},{18,... | collective-permute-start | bytes 786440 | tf_op jit(solution)/shard_map/ppermute | solution.py:285
  26.1 56.3 %copy-start.9 = (bf16[64,2048]{1,0:T(8,128)(2,1)}, bf16[64,2048]{1,0:T(8,128)(2,1)S(1)}, u32[]{:S(2)}) copy-start(bf16[64,2048]{1,0:T(8,128)(2,1)S(1)} %collective-permute-done.1.refs_0_) | copy-start | bytes 786436
  26.1 7.6 %collective-permute-start.3 = (bf16[64,2048]{1,0:T(8,128)(2,1)S(1)}, bf16[64,2048]{1,0:T(8,128)(2,1)S(1)}, u32[]{:S(2)}, u32[]{:S(2)}) collective-permute-start(bf16[64,2048]{1,0:T(8,128)(2,1)S(1)} %bitcast.68), channel_id=1, source_target_pairs={{0,4},{2,6},{4,0},{6,2},{8,12},{10,14},{12,8},{14,10},{16,20},{18,... | collective-permute-start | bytes 786440 | tf_op jit(solution)/shard_map/ppermute | solution.py:285
  30.8 16.9 %copy-start.10 = (bf16[64,2048]{1,0:T(8,128)(2,1)}, bf16[64,2048]{1,0:T(8,128)(2,1)S(1)}, u32[]{:S(2)}) copy-start(bf16[64,2048]{1,0:T(8,128)(2,1)S(1)} %collective-permute-done.2.refs_5_.refs_1_) | copy-start | bytes 786436
  33.7 13.9 %copy-start.11 = (bf16[64,2048]{1,0:T(8,128)(2,1)}, bf16[64,2048]{1,0:T(8,128)(2,1)S(1)}, u32[]{:S(2)}) copy-start(bf16[64,2048]{1,0:T(8,128)(2,1)S(1)} %collective-permute-done.3.refs_6_.refs_2_) | copy-start | bytes 786436
  33.7 48.7 %copy-start.1 = (bf16[704,2048]{1,0:T(8,128)(2,1)}, bf16[704,2048]{1,0:T(8,128)(2,1)S(1)}, u32[]{:S(2)}) copy-start(bf16[704,2048]{1,0:T(8,128)(2,1)S(1)} %collective-permute-done.4.refs_10_.refs_9_) | copy-start | bytes 8650756
  33.8 9.5 %collective-permute-start.10 = (bf16[64,2048]{1,0:T(8,128)(2,1)}, bf16[64,2048]{1,0:T(8,128)(2,1)S(1)}, u32[]{:S(2)}, u32[]{:S(2)}) collective-permute-start(bf16[64,2048]{1,0:T(8,128)(2,1)} %collective-permute-done.refs_0_), channel_id=1, source_target_pairs={{0,4},{2,6},{4,0},{6,2},{8,12},{10,14},{12,8},{14,10},{16,20},{18,... | collective-permute-start | bytes 786440 | tf_op jit(solution)/shard_map/ppermute | solution.py:285
  35.3 11.0 %collective-permute-start.8 = (bf16[64,2048]{1,0:T(8,128)(2,1)}, bf16[64,2048]{1,0:T(8,128)(2,1)S(1)}, u32[]{:S(2)}, u32[]{:S(2)}) collective-permute-start(bf16[64,2048]{1,0:T(8,128)(2,1)} %collective-permute-done.refs_0_), channel_id=1, source_target_pairs={{0,2},{2,0},{4,6},{6,4},{8,10},{10,8},{12,14},{14,12},{16,18},{18,... | collective-permute-start | bytes 786440 | tf_op jit(solution)/shard_map/ppermute | solution.py:285
  36.8 9.5 %collective-permute-start.11 = (bf16[64,2048]{1,0:T(8,128)(2,1)S(1)}, bf16[64,2048]{1,0:T(8,128)(2,1)S(1)}, u32[]{:S(2)}, u32[]{:S(2)}) collective-permute-start(bf16[64,2048]{1,0:T(8,128)(2,1)S(1)} %collective-permute-done.1.refs_0_), channel_id=1, source_target_pairs={{0,4},{2,6},{4,0},{6,2},{8,12},{10,14},{12,8},{14,10},{16,20},{18,... | collective-permute-start | bytes 786440 | tf_op jit(solution)/shard_map/ppermute | solution.py:285
  37.3 10.3 %collective-permute-start.9 = (bf16[64,2048]{1,0:T(8,128)(2,1)S(1)}, bf16[64,2048]{1,0:T(8,128)(2,1)S(1)}, u32[]{:S(2)}, u32[]{:S(2)}) collective-permute-start(bf16[64,2048]{1,0:T(8,128)(2,1)S(1)} %collective-permute-done.1.refs_0_), channel_id=1, source_target_pairs={{0,2},{2,0},{4,6},{6,4},{8,10},{10,8},{12,14},{14,12},{16,18},{18,... | collective-permute-start | bytes 786440 | tf_op jit(solution)/shard_map/ppermute | solution.py:285
  37.9 12.2 %collective-permute-start.7 = (bf16[64,2048]{1,0:T(8,128)(2,1)S(1)}, bf16[64,2048]{1,0:T(8,128)(2,1)}, u32[]{:S(2)}, u32[]{:S(2)}) collective-permute-start(bf16[64,2048]{1,0:T(8,128)(2,1)S(1)} %bitcast.69), channel_id=1, source_target_pairs={{0,16},{2,18},{4,20},{6,22},{8,24},{10,26},{12,28},{14,30},{16,0},... | collective-permute-start | bytes 786440 | tf_op jit(solution)/shard_map/ppermute | solution.py:288
  43.3 4.3 %copy-start.14 = (bf16[64,2048]{1,0:T(8,128)(2,1)}, bf16[64,2048]{1,0:T(8,128)(2,1)S(1)}, u32[]{:S(2)}) copy-start(bf16[64,2048]{1,0:T(8,128)(2,1)S(1)} %collective-permute-done.10.refs_2_) | copy-start | bytes 786436
  46.4 1.3 copy-start.12
  46.4 1.3 copy-start.15
  50.1 45.9 %all-to-all-start.1 = ((bf16[16,288,128]{2,1,0:T(8,128)(2,1)}), bf16[16,288,128]{2,1,0:T(8,128)(2,1)}, u32[]{:S(2)}, u32[]{:S(2)}) async-start(bf16[16,288,128]{2,1,0:T(8,128)(2,1)} %shard_map.91), calls=%async_computation.1 | async-start | bytes 2359296 | tf_op jit(solution)/shard_map/all_to_all | solution.py:336
  54.8 18.6 %collective-permute-start.14 = (bf16[64,2048]{1,0:T(8,128)(2,1)}, bf16[64,2048]{1,0:T(8,128)(2,1)}, u32[]{:S(2)}, u32[]{:S(2)}) collective-permute-start(bf16[64,2048]{1,0:T(8,128)(2,1)} %collective-permute-done.7.refs_0_), channel_id=1, source_target_pairs={{0,2},{2,0},{4,6},{6,4},{8,10},{10,8},{12,14},{14,12},{16,18},{18,... | collective-permute-start | bytes 786440 | tf_op jit(solution)/shard_map/ppermute | solution.py:285
  56.7 25.7 %collective-permute-start.12 = (bf16[64,2048]{1,0:T(8,128)(2,1)}, bf16[64,2048]{1,0:T(8,128)(2,1)S(1)}, u32[]{:S(2)}, u32[]{:S(2)}) collective-permute-start(bf16[64,2048]{1,0:T(8,128)(2,1)} %copy-done.11), channel_id=1, source_target_pairs={{0,2},{2,0},{4,6},{6,4},{8,10},{10,8},{12,14},{14,12},{16,18},{18,... | collective-permute-start | bytes 786440 | tf_op jit(solution)/shard_map/ppermute | solution.py:285
  56.9 25.5 %collective-permute-start.17 = (bf16[64,2048]{1,0:T(8,128)(2,1)}, bf16[64,2048]{1,0:T(8,128)(2,1)S(1)}, u32[]{:S(2)}, u32[]{:S(2)}) collective-permute-start(bf16[64,2048]{1,0:T(8,128)(2,1)} %copy-done.13), channel_id=1, source_target_pairs={{0,4},{2,6},{4,0},{6,2},{8,12},{10,14},{12,8},{14,10},{16,20},{18,... | collective-permute-start | bytes 786440 | tf_op jit(solution)/shard_map/ppermute | solution.py:285
  58.7 37.2 %collective-permute-start.15 = (bf16[64,2048]{1,0:T(8,128)(2,1)}, bf16[64,2048]{1,0:T(8,128)(2,1)}, u32[]{:S(2)}, u32[]{:S(2)}) collective-permute-start(bf16[64,2048]{1,0:T(8,128)(2,1)} %collective-permute-done.7.refs_0_), channel_id=1, source_target_pairs={{0,4},{2,6},{4,0},{6,2},{8,12},{10,14},{12,8},{14,10},{16,20},{18,... | collective-permute-start | bytes 786440 | tf_op jit(solution)/shard_map/ppermute | solution.py:285
  58.9 37.0 %collective-permute-start.13 = (bf16[64,2048]{1,0:T(8,128)(2,1)}, bf16[64,2048]{1,0:T(8,128)(2,1)}, u32[]{:S(2)}, u32[]{:S(2)}) collective-permute-start(bf16[64,2048]{1,0:T(8,128)(2,1)} %copy-done.14), channel_id=1, source_target_pairs={{0,2},{2,0},{4,6},{6,4},{8,10},{10,8},{12,14},{14,12},{16,18},{18,... | collective-permute-start | bytes 786440 | tf_op jit(solution)/shard_map/ppermute | solution.py:285
  73.5 22.5 %collective-permute-start.16 = (bf16[64,2048]{1,0:T(8,128)(2,1)}, bf16[64,2048]{1,0:T(8,128)(2,1)}, u32[]{:S(2)}, u32[]{:S(2)}) collective-permute-start(bf16[64,2048]{1,0:T(8,128)(2,1)} %collective-permute-done.14.refs_1_), channel_id=1, source_target_pairs={{0,4},{2,6},{4,0},{6,2},{8,12},{10,14},{12,8},{14,10},{16,20},{18,... | collective-permute-start | bytes 786440 | tf_op jit(solution)/shard_map/ppermute | solution.py:285
  82.4 0.7 copy-start.16
  96.0 3.1 %collective-permute-start.18 = (bf16[16,288,128]{2,1,0:T(8,128)(2,1)}, bf16[16,288,128]{2,1,0:T(8,128)(2,1)S(1)}, u32[]{:S(2)}, u32[]{:S(2)}) collective-permute-start(bf16[16,288,128]{2,1,0:T(8,128)(2,1)} %all-to-all-done.1.refs_0_), channel_id=1, source_target_pairs={{0,1},{1,0},{2,3},{3,2},{4,5},{5,4},{6,7},{7,6},{8,9},{9,8},{10,11... | collective-permute-start | bytes 3538952 | tf_op jit(solution)/shard_map/ppermute | solution.py:293
  99.1 1.0 copy-start.5
  115.6 14.4 %collective-permute-start.19 = (bf16[2,64,2048]{2,1,0:T(8,128)(2,1)}, bf16[2,64,2048]{2,1,0:T(8,128)(2,1)S(1)}, u32[]{:S(2)}, u32[]{:S(2)}) collective-permute-start(bf16[2,64,2048]{2,1,0:T(8,128)(2,1)} %get-tuple-element.91), channel_id=1, source_target_pairs={{0,2},{2,0},{4,6},{6,4},{8,10},{10,8},{12,14},{14,12},{16,18},{18,... | collective-permute-start | bytes 1572872 | tf_op jit(solution)/shard_map/ppermute | solution.py:285
  115.9 14.1 %copy-start.3 = (bf16[2,64,2048]{2,1,0:T(8,128)(2,1)S(1)}, bf16[2,64,2048]{2,1,0:T(8,128)(2,1)}, u32[]{:S(2)}) copy-start(bf16[2,64,2048]{2,1,0:T(8,128)(2,1)} %get-tuple-element.90.refs_12_) | copy-start | bytes 1572868
  127.8 19.5 %collective-permute-start.22 = (bf16[2,64,2048]{2,1,0:T(8,128)(2,1)}, bf16[2,64,2048]{2,1,0:T(8,128)(2,1)S(1)}, u32[]{:S(2)}, u32[]{:S(2)}) collective-permute-start(bf16[2,64,2048]{2,1,0:T(8,128)(2,1)} %get-tuple-element.99), channel_id=1, source_target_pairs={{0,4},{2,6},{4,0},{6,2},{8,12},{10,14},{12,8},{14,10},{16,20},{18,... | collective-permute-start | bytes 1572872 | tf_op jit(solution)/shard_map/ppermute | solution.py:285
  130.1 1.5 copy-start.6
  130.1 20.0 %collective-permute-start.20 = (bf16[64,2048]{1,0:T(8,128)(2,1)S(1)}, bf16[64,2048]{1,0:T(8,128)(2,1)S(1)}, u32[]{:S(2)}, u32[]{:S(2)}) collective-permute-start(bf16[64,2048]{1,0:T(8,128)(2,1)S(1)} %fusion.5.refs_14_), channel_id=1, source_target_pairs={{0,4},{2,6},{4,0},{6,2},{8,12},{10,14},{12,8},{14,10},{16,20},{18,... | collective-permute-start | bytes 786440 | tf_op jit(solution)/shard_map/ppermute | solution.py:285
  139.4 7.9 %copy-start.4 = (bf16[2,64,2048]{2,1,0:T(8,128)(2,1)S(1)}, bf16[2,64,2048]{2,1,0:T(8,128)(2,1)}, u32[]{:S(2)}) copy-start(bf16[2,64,2048]{2,1,0:T(8,128)(2,1)} %get-tuple-element.98.refs_13_) | copy-start | bytes 1572868
  139.4 8.6 %copy-start.18 = (bf16[2,64,2048]{2,1,0:T(8,128)(2,1)S(1)}, bf16[2,64,2048]{2,1,0:T(8,128)(2,1)}, u32[]{:S(2)}) copy-start(bf16[2,64,2048]{2,1,0:T(8,128)(2,1)} %get-tuple-element.112) | copy-start | bytes 1572868
  147.2 18.7 %copy-start.2 = (bf16[2,64,2048]{2,1,0:T(8,128)(2,1)S(1)}, bf16[2,64,2048]{2,1,0:T(8,128)(2,1)}, u32[]{:S(2)}) copy-start(bf16[2,64,2048]{2,1,0:T(8,128)(2,1)} %get-tuple-element.109.refs_13_) | copy-start | bytes 1572868
  147.2 19.7 %copy-start.8 = (bf16[2,64,2048]{2,1,0:T(8,128)(2,1)S(1)}, bf16[2,64,2048]{2,1,0:T(8,128)(2,1)}, u32[]{:S(2)}) copy-start(bf16[2,64,2048]{2,1,0:T(8,128)(2,1)} %get-tuple-element.117) | copy-start | bytes 1572868
  147.3 9.3 %collective-permute-start.23 = (bf16[64,2048]{1,0:T(8,128)(2,1)S(1)}, bf16[64,2048]{1,0:T(8,128)(2,1)S(1)}, u32[]{:S(2)}, u32[]{:S(2)}) collective-permute-start(bf16[64,2048]{1,0:T(8,128)(2,1)S(1)} %fusion.6), channel_id=1, source_target_pairs={{0,2},{2,0},{4,6},{6,4},{8,10},{10,8},{12,14},{14,12},{16,18},{18,... | collective-permute-start | bytes 786440 | tf_op jit(solution)/shard_map/ppermute | solution.py:285
  148.0 17.9 %collective-permute-start.25 = (bf16[2,64,2048]{2,1,0:T(8,128)(2,1)S(1)}, bf16[2,64,2048]{2,1,0:T(8,128)(2,1)S(1)}, u32[]{:S(2)}, u32[]{:S(2)}) collective-permute-start(bf16[2,64,2048]{2,1,0:T(8,128)(2,1)S(1)} %copy-done.18), channel_id=1, source_target_pairs={{0,2},{2,0},{4,6},{6,4},{8,10},{10,8},{12,14},{14,12},{16,18},{18,... | collective-permute-start | bytes 1572872 | tf_op jit(solution)/shard_map/ppermute | solution.py:285
  149.4 17.5 %collective-permute-start.28 = (bf16[2,64,2048]{2,1,0:T(8,128)(2,1)}, bf16[2,64,2048]{2,1,0:T(8,128)(2,1)S(1)}, u32[]{:S(2)}, u32[]{:S(2)}) collective-permute-start(bf16[2,64,2048]{2,1,0:T(8,128)(2,1)} %get-tuple-element.115), channel_id=1, source_target_pairs={{0,4},{2,6},{4,0},{6,2},{8,12},{10,14},{12,8},{14,10},{16,20},{18,... | collective-permute-start | bytes 1572872 | tf_op jit(solution)/shard_map/ppermute | solution.py:285
  150.2 23.5 %collective-permute-start.21 = (bf16[64,2048]{1,0:T(8,128)(2,1)S(1)}, bf16[64,2048]{1,0:T(8,128)(2,1)S(1)}, u32[]{:S(2)}, u32[]{:S(2)}) collective-permute-start(bf16[64,2048]{1,0:T(8,128)(2,1)S(1)} %fusion.4), channel_id=1, source_target_pairs={{0,16},{2,18},{4,20},{6,22},{8,24},{10,26},{12,28},{14,30},{16,0},... | collective-permute-start | bytes 786440 | tf_op jit(solution)/shard_map/ppermute | solution.py:288
  156.8 16.9 %collective-permute-start.24 = (bf16[64,2048]{1,0:T(8,128)(2,1)S(1)}, bf16[64,2048]{1,0:T(8,128)(2,1)S(1)}, u32[]{:S(2)}, u32[]{:S(2)}) collective-permute-start(bf16[64,2048]{1,0:T(8,128)(2,1)S(1)} %fusion.3), channel_id=1, source_target_pairs={{0,24},{2,26},{4,28},{6,30},{8,0},{10,2},{12,4},{14,6},{16,8},{18,... | collective-permute-start | bytes 786440 | tf_op jit(solution)/shard_map/ppermute | solution.py:288
  166.0 6.4 %collective-permute-start.26 = (bf16[64,2048]{1,0:T(8,128)(2,1)S(1)}, bf16[64,2048]{1,0:T(8,128)(2,1)S(1)}, u32[]{:S(2)}, u32[]{:S(2)}) collective-permute-start(bf16[64,2048]{1,0:T(8,128)(2,1)S(1)} %fusion.7), channel_id=1, source_target_pairs={{0,4},{2,6},{4,0},{6,2},{8,12},{10,14},{12,8},{14,10},{16,20},{18,... | collective-permute-start | bytes 786440 | tf_op jit(solution)/shard_map/ppermute | solution.py:285
  167.0 6.7 %collective-permute-start.29 = (bf16[64,2048]{1,0:T(8,128)(2,1)S(1)}, bf16[64,2048]{1,0:T(8,128)(2,1)S(1)}, u32[]{:S(2)}, u32[]{:S(2)}) collective-permute-start(bf16[64,2048]{1,0:T(8,128)(2,1)S(1)} %fusion.8), channel_id=1, source_target_pairs={{0,2},{2,0},{4,6},{6,4},{8,10},{10,8},{12,14},{14,12},{16,18},{18,... | collective-permute-start | bytes 786440 | tf_op jit(solution)/shard_map/ppermute | solution.py:285
  172.5 8.2 %collective-permute-start.27 = (bf16[64,2048]{1,0:T(8,128)(2,1)S(1)}, bf16[64,2048]{1,0:T(8,128)(2,1)S(1)}, u32[]{:S(2)}, u32[]{:S(2)}) collective-permute-start(bf16[64,2048]{1,0:T(8,128)(2,1)S(1)} %fusion.2), channel_id=1, source_target_pairs={{0,8},{2,10},{4,12},{6,14},{8,16},{10,18},{12,20},{14,22},{16,24},... | collective-permute-start | bytes 786440 | tf_op jit(solution)/shard_map/ppermute | solution.py:288
  (2 other events, 1.4 us)
where the time goes:
time: 186 us
  waiting for transfers between devices  65.8 us (35%)
  Pallas kernels  57.5 us (31%)
  starting transfers between devices  41.1 us (22%)
  blocking collectives  13 us (7%)
  local copies, waits for them, and re-layouts  6 us (3%)
  other arithmetic  1.92 us (1%)
    ppermute x20, waiting for transfers between devices, flip(): return lax.ppermute(value, 'wide', [(w, w ^ bits) for w in range(wide)])  46.7 us
    pallas_call x4, Pallas kernels, layer(): pl.pallas_call(functools.partial(layer_kernel, plan), out_shape=[pair] *...  39.4 us
    ppermute x20, starting transfers between devices, flip(): return lax.ppermute(value, 'wide', [(w, w ^ bits) for w in range(wide)])  23.9 us
    ppermute x6, waiting for transfers between devices, shift(): lax.ppermute(value, 'wide', [(w, (w + PLANE * by) % wide) for w in range(...  17.8 us
    pallas_call x1, Pallas kernels, expert_hidden(): pl.pallas_call(functools.partial(hidden_kernel, len(pieces)), out_shape=j...  12.1 us
    ppermute x6, starting transfers between devices, shift(): lax.ppermute(value, 'wide', [(w, (w + PLANE * by) % wide) for w in range(...  11.4 us
    all_to_all x1, blocking collectives, body(): lax.all_to_all(tokens, 'narrow', split_axis=0, concat_axis=1, tiled=True)  9.03 us
    all_to_all x1, starting transfers between devices, body(): lax.all_to_all(stacked, 'wide', split_axis=0, concat_axis=0, tiled=True)  4.71 us
  transfers between devices with their start and end apart: 31, of which 15 were waited for; matrix products, arithmetic and copies ran while one was open for 2% of the time, Pallas kernels for 23%

commit v1 on v0

--- a/solution.py
+++ b/solution.py
@@ -23,8 +23,9 @@
 
 
 def row_chunks(count):
-    size = count // 4 if count % 64 == 0 else count
-    return [(first, size) for first in range(0, count, size)]
+    if count <= 3 * TILE:
+        return [(0, count)]
+    return [(0, TILE), (TILE, 2 * TILE), (3 * TILE, count - 3 * TILE)]
 
 
 def fill(rows, blocks):
@@ -67,90 +68,38 @@
     return ready
 
 
-def hidden_kernel(count, *refs):
-    blocks = refs[: -2 * count - 5]
-    sources = refs[-2 * count - 5 : -5]
-    out, rows, w_gate, w_up, sems = refs[-5:]
+def layer_kernel(plan, *refs):
+    experts, plane, x_first, ties = plan
+    blocks, gates, shared = refs[:4], refs[4], refs[5]
+    trios = [refs[6 + 3 * i : 9 + 3 * i] for i in range(experts)]
+    keep, send, rows, w_gate, w_up, w_shared, w_down, hidden, sems = refs[6 + 3 * experts + ties :]
+    step, width = blocks[0].shape
+    size, units = trios[0][0].shape[0], shared.shape[1]
+    base = size * experts
     copies = []
-    sources = [(sources[2 * i], sources[2 * i + 1]) for i in range(count)]
-    firsts = launch_projections(copies, sems, sources, w_gate, w_up)
-    fill(rows, blocks)
-    ready = 0
-    for lower, upper in tiles(0, w_gate.shape[0]):
-        ready = wait_rows(copies, firsts, ready, upper)
-        out[:, lower:upper] = gated(rows, w_gate, w_up, lower, upper).astype(jnp.bfloat16)
-
-
-def expert_hidden(blocks, pieces):
-    step, width = blocks[0].shape
-    depth = step * len(blocks)
-    total = sum(piece[0].shape[0] for piece in pieces)
-    held = pltpu.VMEM((total, width), jnp.bfloat16)
-    sems = 2 * sum(len(row_chunks(piece[0].shape[0])) for piece in pieces)
-    return pl.pallas_call(
-        functools.partial(hidden_kernel, len(pieces)),
-        out_shape=jax.ShapeDtypeStruct((depth, total), jnp.bfloat16),
-        in_specs=[pl.BlockSpec(memory_space=pltpu.VMEM)] * len(blocks)
-        + [pl.BlockSpec(memory_space=pl.ANY)] * (2 * len(pieces)),
-        out_specs=pl.BlockSpec(memory_space=pltpu.VMEM),
-        scratch_shapes=[
-            pltpu.VMEM((depth, width), jnp.bfloat16),
-            held,
-            held,
-            pltpu.SemaphoreType.DMA((sems,)),
-        ],
-        compiler_params=pltpu.CompilerParams(vmem_limit_bytes=VMEM_BYTES),
-        cost_estimate=pl.CostEstimate(
-            flops=4 * depth * width * total,
-            bytes_accessed=4 * total * width,
-            transcendentals=depth * total,
-        ),
-    )(*blocks, *[w for piece in pieces for w in piece[:2]])
-
-
-def layer_kernel(plan, *refs):
-    experts, plane, x_first, ties, count, skip = plan
-    blocks, gates, shared = refs[:4], refs[4], refs[5]
-    refs = refs[6:]
-    acts = None
-    if skip is not None:
-        acts, refs = refs[0], refs[1:]
-    pieces = [refs[3 * i : 3 * i + 3] for i in range(count)]
-    keep, send, rows, w_gate, w_up, w_down, hidden, sems = refs[3 * count + ties :]
-    step, width = blocks[0].shape
-    size, units = pieces[0][0].shape[0], shared.shape[1]
-    base = size * count
-    copies = []
-    sources = [piece[:2] for piece in pieces] if acts is None else []
-    sources.append((shared.at[0], shared.at[1]))
-    firsts = launch_projections(copies, sems, sources, w_gate, w_up)
+    firsts = launch_projections(copies, sems, [trio[:2] for trio in trios], w_gate, w_up)
+    launch(copies, sems, shared.at[pl.ds(0, 2)], w_shared)
     head = len(copies)
-    for lower in range(0, width, OUT_TILE):
-        columns = pl.ds(lower, OUT_TILE)
-        for i, piece in enumerate(pieces):
-            part = w_down.at[pl.ds(i * size, size), columns]
-            launch(copies, sems, piece[2].at[:, columns], part)
-        launch(copies, sems, shared.at[2].at[:, columns], w_down.at[pl.ds(base, units), columns])
+    for e, trio in enumerate(trios):
+        launch(copies, sems, trio[2], w_down.at[pl.ds(e * size, size)])
+    launch(copies, sems, shared.at[2], w_down.at[pl.ds(base, units)])
     fill(rows, blocks)
     ready = 0
     for e in range(experts):
         column = gate_column(gates, plane, e)
-        for lower, upper in tiles(e * base // experts, (e + 1) * base // experts):
-            if acts is None:
-                ready = wait_rows(copies, firsts, ready, upper)
-                value = gated(rows, w_gate, w_up, lower, upper)
-            else:
-                value = acts[skip : skip + PLANE * step, lower:upper].astype(jnp.float32)
-            hidden[:, lower:upper] = (value * column).astype(jnp.bfloat16)
-    wait_rows(copies, firsts, ready, base + units)
-    offset = 0 if acts is not None else base
-    value = gated(rows, w_gate, w_up, offset, offset + units)
+        for lower, upper in tiles(e * size, (e + 1) * size):
+            ready = wait_rows(copies, firsts, ready, upper)
+            value = gated(rows, w_gate, w_up, lower, upper) * column
+            hidden[:, lower:upper] = value.astype(jnp.bfloat16)
+    copies[head - 1].wait()
+    pre = dot_t(rows[...], w_shared[0])
+    value = jax.nn.silu(pre) * dot_t(rows[...], w_shared[1])
     hidden[:, base:] = value.astype(jnp.bfloat16)
+    for copy in copies[head:]:
+        copy.wait()
     kept, sent = ((0, 2), (1, 3)) if x_first else ((0, 1), (2, 3))
-    for n in range(width // OUT_TILE):
-        lower, upper = n * OUT_TILE, (n + 1) * OUT_TILE
-        for copy in copies[head + n * (count + 1) : head + (n + 1) * (count + 1)]:
-            copy.wait()
+    for lower in range(0, width, OUT_TILE):
+        upper = lower + OUT_TILE
         part = jnp.dot(hidden[...], w_down[:, lower:upper], preferred_element_type=jnp.float32)
         part = part.astype(jnp.bfloat16)
         for ref, which in ((keep, kept), (send, sent)):
@@ -158,41 +107,37 @@
                 ref[j, :, lower:upper] = part[k * step : (k + 1) * step]
 
 
-def layer(blocks, gates, shared, acts, skip, pieces, experts, plane, x_first, after):
+def layer(blocks, gates, shared, trios, plane, x_first, after):
     step, width = blocks[0].shape
-    units, count = shared.shape[1], len(pieces)
-    total = count * pieces[0][0].shape[0] + units
-    worked = total if acts is None else units
+    units, experts = shared.shape[1], len(trios)
+    size = trios[0][0].shape[0]
+    total = experts * size + units
     depth = PLANE * step
     pair = jax.ShapeDtypeStruct((2, step, width), jnp.bfloat16)
-    held = pltpu.VMEM((worked, width), jnp.bfloat16)
-    sems = 2 * count * len(row_chunks(pieces[0][0].shape[0])) + 2 * len(row_chunks(units))
-    sems += (width // OUT_TILE) * (count + 1)
-    given = [] if acts is None else [acts]
-    plan = (experts, plane, x_first, len(after), count, None if acts is None else skip)
+    held = pltpu.VMEM((experts * size, width), jnp.bfloat16)
+    sems = 2 * experts * len(row_chunks(size)) + experts + 2
     return pl.pallas_call(
-        functools.partial(layer_kernel, plan),
+        functools.partial(layer_kernel, (experts, plane, x_first, len(after))),
         out_shape=[pair] * 2,
         in_specs=[pl.BlockSpec(memory_space=pltpu.VMEM)] * 5
-        + [pl.BlockSpec(memory_space=pl.ANY)]
-        + [pl.BlockSpec(memory_space=pltpu.VMEM)] * len(given)
-        + [pl.BlockSpec(memory_space=pl.ANY)] * (3 * count + len(after)),
+        + [pl.BlockSpec(memory_space=pl.ANY)] * (1 + 3 * experts + len(after)),
         out_specs=[pl.BlockSpec(memory_space=pltpu.VMEM)] * 2,
         scratch_shapes=[
             pltpu.VMEM((depth, width), jnp.bfloat16),
             held,
             held,
+            pltpu.VMEM((2, units, width), jnp.bfloat16),
             pltpu.VMEM((total, width), jnp.bfloat16),
             pltpu.VMEM((depth, total), jnp.bfloat16),
             pltpu.SemaphoreType.DMA((sems,)),
         ],
         compiler_params=pltpu.CompilerParams(vmem_limit_bytes=VMEM_BYTES),
         cost_estimate=pl.CostEstimate(
-            flops=2 * depth * width * (total + 2 * worked),
-            bytes_accessed=2 * (total + 2 * worked) * width,
-            transcendentals=depth * worked,
+            flops=6 * depth * width * total,
+            bytes_accessed=6 * total * width,
+            transcendentals=depth * total,
         ),
-    )(*blocks, gates, shared, *given, *[w for piece in pieces for w in piece], *after)
+    )(*blocks, gates, shared, *[w for trio in trios for w in trio], *after)
 
 
 def cut_kernel(units, padded, gate, up, down, coded, out):
@@ -320,14 +265,14 @@
     for d in near:
         lined[d] = shift(mine, d)
     by_x[0], by_y[0] = flip(mine, 1), flip(mine, 2)
-    pieces = []
-    for e in range(local_experts):
-        for t in range(narrow):
-            piece = (expert_gate[e], expert_up[e], expert_down[e])
-            pieces.append(tuple(turn(w, t) for w in piece) if t else piece)
-    lined, by_x, by_y, stacked, pieces = lax.optimization_barrier(
-        (lined, by_x, by_y, stacked, pieces)
+    experts = (expert_gate, expert_up, expert_down)
+    lined, by_x, by_y, stacked, experts = lax.optimization_barrier(
+        (lined, by_x, by_y, stacked, experts)
     )
+    trios = [
+        tuple(lax.all_gather(weight[e], "narrow", axis=0, tiled=True) for weight in experts)
+        for e in range(local_experts)
+    ]
     for d in rest:
         lined[d] = shift(lined[0], d)
     for d in near:
@@ -340,9 +285,7 @@
     for d in near[1:] + [0] + near[:1] + rest:
         far = flip(by_x[d], 2) if x_first[d] else flip(by_y[d], 1)
         blocks[d] = (lined[d], by_x[d], by_y[d], far)
-    early = planes[-2:]
-    acts = expert_hidden([block for d in early for block in blocks[d]], pieces)
-    recut, blocks, acts = lax.optimization_barrier((recut, blocks, acts))
+    recut, blocks = lax.optimization_barrier((recut, blocks))
     shared = lay_out([recut] + [turn(recut, s) for s in range(1, narrow)], padded, width)
     coded = recut[:, units : units + gate_rows].reshape(wide, gate_rows * chunk)
     coded = coded.astype(jnp.float32)
@@ -357,28 +300,21 @@
     gates = jnp.transpose(gates.reshape(lines, PLANE, local_experts, own_rows), (0, 2, 1, 3))
     gates = gates.reshape(lines, local_experts, PLANE * own_rows)
 
-    kept, came, onwards = [], [], {}
+    kept, came, onwards = [], [], []
 
     def pass_on(m, later):
         came[m], kept[later] = lax.optimization_barrier((came[m], kept[later]))
         got = came[m].astype(jnp.float32)
-        onwards[m] = (kept[m][1].astype(jnp.float32) + got[1]).astype(jnp.bfloat16)
+        onwards.append((kept[m][1].astype(jnp.float32) + got[1]).astype(jnp.bfloat16))
 
     for n, d in enumerate(planes):
-        after = [kept[n - 1]] if n else []
-        if 2 <= n < lines - 1:
-            after.append(onwards[n - 2])
-        ready = acts if d in early else None
-        skip = early.index(d) * PLANE * own_rows if d in early else None
-        keep, send = layer(
-            blocks[d], gates, shared, ready, skip, pieces, local_experts, d, x_first[d], after
-        )
+        after = kept[-1:] + onwards[-1:]
+        keep, send = layer(blocks[d], gates, shared, trios, d, x_first[d], after)
         kept.append(keep)
         came.append(flip(send, 1 if x_first[d] else 2))
-        if 1 <= n < lines - 2:
+        if n:
             pass_on(n - 1, n)
-    for m in range(max(0, lines - 3), lines):
-        pass_on(m, lines - 1)
+    pass_on(lines - 1, lines - 1)
     out = None
     for n, d in enumerate(planes):
         total = kept[n][0].astype(jnp.float32) + came[n][0].astype(jnp.float32)

time: 186 us -> 182 us (0.978)
  between operations: 0.34 us -> 13.4 us
  waiting for transfers between devices: 65.8 us -> 57.3 us
  Pallas kernels: 57.5 us -> 51.1 us
  blocking collectives: 13 us -> 9.06 us
  starting transfers between devices: 41.1 us -> 44.8 us
  local copies, waits for them, and re-layouts: 6 us -> 3.99 us
    pallas_call x5 -> x4, Pallas kernels: 51.5 us -> 45 us  [layer(): pl.pallas_call(functools.partial(layer_kernel, (experts, plane, x_first,...]
    ppermute x6, waiting for transfers between devices: 17.8 us -> 11.7 us  [shift(): lax.ppermute(value, 'wide', [(w, (w + PLANE * by) % wide) for w in range(...]
    ppermute x20, waiting for transfers between devices: 46.7 us -> 42.4 us  [flip(): return lax.ppermute(value, 'wide', [(w, w ^ bits) for w in range(wide)])]
    all_to_all x1, blocking collectives: 9.03 us -> 5.11 us  [body(): lax.all_to_all(tokens, 'narrow', split_axis=0, concat_axis=1, tiled=True)]
    ppermute x20, starting transfers between devices: 23.9 us -> 27.5 us  [flip(): return lax.ppermute(value, 'wide', [(w, w ^ bits) for w in range(wide)])]
    unnamed x40 -> x50, local copies, waits for them, and re-layouts: 4.47 us -> 2.45 us
  transfers between devices with their start and end apart: 31 -> 31, of which waited for: 15 -> 16; matrix products, arithmetic and copies ran while one was open for 2% -> 2% of each run, Pallas kernels for 23% -> 22%
where the time goes in v1:
time: 182 us
  waiting for transfers between devices  57.3 us (31%)
  Pallas kernels  51.1 us (28%)
  starting transfers between devices  44.8 us (25%)
  between operations  13.4 us (7%)
  blocking collectives  9.06 us (5%)
  local copies, waits for them, and re-layouts  3.99 us (2%)
  other arithmetic  2.13 us (1%)
    pallas_call x4, Pallas kernels, layer(): pl.pallas_call(functools.partial(layer_kernel, (experts, plane, x_first,...  45 us
    ppermute x20, waiting for transfers between devices, flip(): return lax.ppermute(value, 'wide', [(w, w ^ bits) for w in range(wide)])  42.4 us
    ppermute x20, starting transfers between devices, flip(): return lax.ppermute(value, 'wide', [(w, w ^ bits) for w in range(wide)])  27.5 us
    ppermute x6, starting transfers between devices, shift(): lax.ppermute(value, 'wide', [(w, (w + PLANE * by) % wide) for w in range(...  11.9 us
    ppermute x6, waiting for transfers between devices, shift(): lax.ppermute(value, 'wide', [(w, (w + PLANE * by) % wide) for w in range(...  11.7 us
    all_to_all x1, starting transfers between devices, body(): lax.all_to_all(stacked, 'wide', split_axis=0, concat_axis=0, tiled=True)  5.27 us
    all_to_all x1, blocking collectives, body(): lax.all_to_all(tokens, 'narrow', split_axis=0, concat_axis=1, tiled=True)  5.11 us
    all_to_all x1, blocking collectives, body(): lax.all_to_all(out.astype(jnp.bfloat16), 'narrow', split_axis=1, concat_a...  3.94 us
  transfers between devices with their start and end apart: 31, of which 16 were waited for; matrix products, arithmetic and copies ran while one was open for 2% of the time, Pallas kernels for 22%

profile of v1, /device:TPU:0, one launch (start us, length us, event | category | flops | bytes accessed | tf_op | source)
XLA Modules:
  0.0 181.8 jit_solution(16115899826013860035)
XLA Ops:
  6.5 5.1 %all_to_all.43 = bf16[2,64,1024]{2,1,0:T(8,128)(2,1)S(1)} all-to-all(bf16[2,64,1024]{2,1,0:T(8,128)(2,1)} %bitcast.70), channel_id=1, replica_groups=mesh['wide'=16,'narrow'=2] {'narrow'}, dimensions={0} | all-to-all | bytes 524288 | tf_op jit(solution)/shard_map/all_to_all | solution.py:240
  11.7 3.1 %collective-permute-start = (bf16[64,2048]{1,0:T(8,128)(2,1)S(1)}, bf16[64,2048]{1,0:T(8,128)(2,1)S(1)}, u32[]{:S(2)}, u32[]{:S(2)}) collective-permute-start(bf16[64,2048]{1,0:T(8,128)(2,1)S(1)} %bitcast.60), channel_id=1, source_target_pairs={{0,8},{2,10},{4,12},{6,14},{8,16},{10,18},{12,20},{14,22},{16,24},... | collective-permute-start | bytes 786440 | tf_op jit(solution)/shard_map/ppermute | solution.py:233
  14.8 2.1 %collective-permute-start.1 = (bf16[64,2048]{1,0:T(8,128)(2,1)S(1)}, bf16[64,2048]{1,0:T(8,128)(2,1)S(1)}, u32[]{:S(2)}, u32[]{:S(2)}) collective-permute-start(bf16[64,2048]{1,0:T(8,128)(2,1)S(1)} %bitcast.61), channel_id=1, source_target_pairs={{0,24},{2,26},{4,28},{6,30},{8,0},{10,2},{12,4},{14,6},{16,8},{18,... | collective-permute-start | bytes 786440 | tf_op jit(solution)/shard_map/ppermute | solution.py:233
  16.9 1.6 collective-permute-start.2
  18.5 1.5 collective-permute-start.3
  20.1 0.8 dynamic-slice_bitcast_fusion.1
  21.6 2.5 %shard_map.91 = bf16[16,288,128]{2,1,0:T(8,128)(2,1)} custom-call(bf16[128,1408]{1,0:T(8,128)(2,1)} %gate.1, bf16[128,1408]{1,0:T(8,128)(2,1)} %up.1, bf16[1408,128]{1,0:T(8,128)(2,1)} %down.1, bf16[16,8,128]{2,1,0:T(8,128)(2,1)} %bitcast.71), custom_call_target="tpu_custom_call" | custom-call | bytes 2883584 | tf_op jit(solution)/shard_map/pallas_call | solution.py:161
  24.0 4.4 %collective-permute-done.1.refs_0_ = bf16[64,2048]{1,0:T(8,128)(2,1)S(1)} collective-permute-done((bf16[64,2048]{1,0:T(8,128)(2,1)S(1)}, bf16[64,2048]{1,0:T(8,128)(2,1)S(1)}, u32[]{:S(2)}, u32[]{:S(2)}) %collective-permute-start.1) | collective-permute-done | bytes 262176 | tf_op jit(solution)/shard_map/ppermute | solution.py:233
  30.0 1.6 collective-permute-start.5
  31.6 1.5 collective-permute-start.7
  34.1 1.3 collective-permute-start.4
  35.4 3.9 %collective-permute-done.5.refs_1_ = bf16[64,2048]{1,0:T(8,128)(2,1)S(1)} collective-permute-done((bf16[64,2048]{1,0:T(8,128)(2,1)S(1)}, bf16[64,2048]{1,0:T(8,128)(2,1)S(1)}, u32[]{:S(2)}, u32[]{:S(2)}) %collective-permute-start.5) | collective-permute-done | bytes 262176 | tf_op jit(solution)/shard_map/ppermute | solution.py:230
  39.3 4.0 %collective-permute-done.6.refs_1_ = bf16[64,2048]{1,0:T(8,128)(2,1)S(1)} collective-permute-done((bf16[64,2048]{1,0:T(8,128)(2,1)S(1)}, bf16[64,2048]{1,0:T(8,128)(2,1)S(1)}, u32[]{:S(2)}, u32[]{:S(2)}) %collective-permute-start.6) | collective-permute-done | bytes 262176 | tf_op jit(solution)/shard_map/ppermute | solution.py:230
  43.4 1.2 collective-permute-done.8.refs_2_
  44.6 2.6 %collective-permute-done.4.refs_0_ = bf16[64,2048]{1,0:T(8,128)(2,1)S(1)} collective-permute-done((bf16[64,2048]{1,0:T(8,128)(2,1)S(1)}, bf16[64,2048]{1,0:T(8,128)(2,1)S(1)}, u32[]{:S(2)}, u32[]{:S(2)}) %collective-permute-start.4) | collective-permute-done | bytes 262176 | tf_op jit(solution)/shard_map/ppermute | solution.py:233
  47.2 5.3 %all-to-all-start.1 = ((bf16[16,288,128]{2,1,0:T(8,128)(2,1)}), bf16[16,288,128]{2,1,0:T(8,128)(2,1)S(1)}, u32[]{:S(2)}, u32[]{:S(2)}) async-start(bf16[16,288,128]{2,1,0:T(8,128)(2,1)} %shard_map.91), calls=%async_computation.1 | async-start | bytes 2359296 | tf_op jit(solution)/shard_map/all_to_all | solution.py:281
  52.5 1.9 %collective-permute-start.11 = (bf16[64,2048]{1,0:T(8,128)(2,1)S(1)}, bf16[64,2048]{1,0:T(8,128)(2,1)S(1)}, u32[]{:S(2)}, u32[]{:S(2)}) collective-permute-start(bf16[64,2048]{1,0:T(8,128)(2,1)S(1)} %collective-permute-done.4.refs_0_), channel_id=1, source_target_pairs={{0,2},{2,0},{4,6},{6,4},{8,10},{10,8},{12,14},{14,12},{16,18},{18,... | collective-permute-start | bytes 786440 | tf_op jit(solution)/shard_map/ppermute | solution.py:230
  54.4 1.5 collective-permute-start.12
  56.6 1.9 %collective-permute-start.9 = (bf16[64,2048]{1,0:T(8,128)(2,1)S(1)}, bf16[64,2048]{1,0:T(8,128)(2,1)S(1)}, u32[]{:S(2)}, u32[]{:S(2)}) collective-permute-start(bf16[64,2048]{1,0:T(8,128)(2,1)S(1)} %collective-permute-done.3.refs_2_), channel_id=1, source_target_pairs={{0,2},{2,0},{4,6},{6,4},{8,10},{10,8},{12,14},{14,12},{16,18},{18,... | collective-permute-start | bytes 786440 | tf_op jit(solution)/shard_map/ppermute | solution.py:230
  58.5 8.8 %collective-permute-done.11.refs_1_ = bf16[64,2048]{1,0:T(8,128)(2,1)S(1)} collective-permute-done((bf16[64,2048]{1,0:T(8,128)(2,1)S(1)}, bf16[64,2048]{1,0:T(8,128)(2,1)S(1)}, u32[]{:S(2)}, u32[]{:S(2)}) %collective-permute-start.11) | collective-permute-done | bytes 262176 | tf_op jit(solution)/shard_map/ppermute | solution.py:230
  67.2 5.5 %collective-permute-start.13 = (bf16[64,2048]{1,0:T(8,128)(2,1)S(1)}, bf16[64,2048]{1,0:T(8,128)(2,1)}, u32[]{:S(2)}, u32[]{:S(2)}) collective-permute-start(bf16[64,2048]{1,0:T(8,128)(2,1)S(1)} %collective-permute-done.11.refs_1_), channel_id=1, source_target_pairs={{0,4},{2,6},{4,0},{6,2},{8,12},{10,14},{12,8},{14,10},{16,20},{18,... | collective-permute-start | bytes 786440 | tf_op jit(solution)/shard_map/ppermute | solution.py:230
  72.7 7.3 %collective-permute-done.10.refs_3_ = bf16[64,2048]{1,0:T(8,128)(2,1)S(1)} collective-permute-done((bf16[64,2048]{1,0:T(8,128)(2,1)S(1)}, bf16[64,2048]{1,0:T(8,128)(2,1)S(1)}, u32[]{:S(2)}, u32[]{:S(2)}) %collective-permute-start.10) | collective-permute-done | bytes 262176 | tf_op jit(solution)/shard_map/ppermute | solution.py:230
  80.1 4.3 %collective-permute-done.9.refs_3_ = bf16[64,2048]{1,0:T(8,128)(2,1)S(1)} collective-permute-done((bf16[64,2048]{1,0:T(8,128)(2,1)S(1)}, bf16[64,2048]{1,0:T(8,128)(2,1)S(1)}, u32[]{:S(2)}, u32[]{:S(2)}) %collective-permute-start.9) | collective-permute-done | bytes 262176 | tf_op jit(solution)/shard_map/ppermute | solution.py:230
  85.7 1.8 %collective-permute-done.15.refs_1_ = bf16[16,288,128]{2,1,0:T(8,128)(2,1)S(1)} collective-permute-done((bf16[16,288,128]{2,1,0:T(8,128)(2,1)S(1)}, bf16[16,288,128]{2,1,0:T(8,128)(2,1)S(1)}, u32[]{:S(2)}, u32[]{:S(2)}) %collective-permute-start.15) | collective-permute-done | bytes 1179680 | tf_op jit(solution)/shard_map/ppermute | solution.py:238
  87.6 1.0 copy-done.5
  88.6 3.6 %shard_map.92.refs_5_ = bf16[3,192,2048]{2,1,0:T(8,128)(2,1)} custom-call(bf16[16,288,128]{2,1,0:T(8,128)(2,1)} %copy-done.1, bf16[16,288,128]{2,1,0:T(8,128)(2,1)} %copy-done.5), custom_call_target="tpu_custom_call" | custom-call | bytes 4718592 | tf_op jit(solution)/shard_map/pallas_call | solution.py:195
  92.2 11.2 %shard_map.93 = (bf16[2,64,2048]{2,1,0:T(8,128)(2,1)}, bf16[2,64,2048]{2,1,0:T(8,128)(2,1)}) custom-call(bf16[64,2048]{1,0:T(8,128)(2,1)} %copy-done.19, bf16[64,2048]{1,0:T(8,128)(2,1)} %copy-done.22, bf16[64,2048]{1,0:T(8,128)(2,1)} %copy-done.23, bf16[64,2048]{1,0:T(8,128)(2,1)} %collective-permute-done.13.refs_3_, ...), custom_call_target="tpu_custom_call" | custom-call | flops 5033164800 | bytes 19660800 | tf_op jit(solution)/shard_map/pallas_call | solution.py:119
  103.5 1.4 collective-permute-start.16
  104.9 11.3 %shard_map.94 = (bf16[2,64,2048]{2,1,0:T(8,128)(2,1)}, bf16[2,64,2048]{2,1,0:T(8,128)(2,1)}) custom-call(bf16[64,2048]{1,0:T(8,128)(2,1)} %copy-done.13, bf16[64,2048]{1,0:T(8,128)(2,1)} %copy-done.16, bf16[64,2048]{1,0:T(8,128)(2,1)} %copy-done.17, bf16[64,2048]{1,0:T(8,128)(2,1)} %copy-done.21, f32[4,1,256]{2,1,0:T(1,128)} %reshape_transpose_reshape.3.refs_4_, ...), custom_call_target="tpu_custom_call" | custom-call | flops 5033164800 | bytes 19660800 | tf_op jit(solution)/shard_map/pallas_call | solution.py:119
  116.9 0.9 collective-permute-done.16
  117.8 1.3 collective-permute-start.17
  119.2 11.2 %shard_map.95 = (bf16[2,64,2048]{2,1,0:T(8,128)(2,1)}, bf16[2,64,2048]{2,1,0:T(8,128)(2,1)}) custom-call(bf16[64,2048]{1,0:T(8,128)(2,1)} %copy-done.12, bf16[64,2048]{1,0:T(8,128)(2,1)} %copy-done.14, bf16[64,2048]{1,0:T(8,128)(2,1)} %copy-done.15, bf16[64,2048]{1,0:T(8,128)(2,1)} %copy-done.20, f32[4,1,256]{2,1,0:T(1,128)} %reshape_transpose_reshape.3.refs_4_, ...), custom_call_target="tpu_custom_call" | custom-call | flops 5033164800 | bytes 19660800 | tf_op jit(solution)/shard_map/pallas_call | solution.py:119
  130.4 0.9 collective-permute-done.19
  131.4 0.7 collective-permute-start.20
  132.1 1.4 collective-permute-start.22
  133.5 11.2 %shard_map.96 = (bf16[2,64,2048]{2,1,0:T(8,128)(2,1)}, bf16[2,64,2048]{2,1,0:T(8,128)(2,1)}) custom-call(bf16[64,2048]{1,0:T(8,128)(2,1)} %bitcast.65, bf16[64,2048]{1,0:T(8,128)(2,1)} %copy-done.10, bf16[64,2048]{1,0:T(8,128)(2,1)} %copy-done.11, bf16[64,2048]{1,0:T(8,128)(2,1)} %copy-done.18, f32[4,1,256]{2,1,0:T(1,128)} %reshape_transpose_reshape.3.refs_4_, ...), custom_call_target="tpu_custom_call" | custom-call | flops 5033164800 | bytes 19660800 | tf_op jit(solution)/shard_map/pallas_call | solution.py:119
  145.5 2.4 %collective-permute-start.18 = (bf16[64,2048]{1,0:T(8,128)(2,1)S(1)}, bf16[64,2048]{1,0:T(8,128)(2,1)S(1)}, u32[]{:S(2)}, u32[]{:S(2)}) collective-permute-start(bf16[64,2048]{1,0:T(8,128)(2,1)S(1)} %fusion.4), channel_id=1, source_target_pairs={{0,16},{2,18},{4,20},{6,22},{8,24},{10,26},{12,28},{14,30},{16,0},... | collective-permute-start | bytes 786440 | tf_op jit(solution)/shard_map/ppermute | solution.py:233
  147.9 1.1 fusion.3
  149.0 1.5 collective-permute-start.21
  150.6 1.5 collective-permute-start.23
  152.1 7.2 %collective-permute-done.25 = bf16[2,64,2048]{2,1,0:T(8,128)(2,1)S(1)} collective-permute-done((bf16[2,64,2048]{2,1,0:T(8,128)(2,1)}, bf16[2,64,2048]{2,1,0:T(8,128)(2,1)S(1)}, u32[]{:S(2)}, u32[]{:S(2)}) %collective-permute-start.25) | collective-permute-done | bytes 524320 | tf_op jit(solution)/shard_map/ppermute | solution.py:230
  159.3 1.0 collective-permute-start.26
  160.4 1.7 collective-permute-done.23
  162.2 1.5 collective-permute-start.24
  163.7 2.1 %collective-permute-done.26 = bf16[64,2048]{1,0:T(8,128)(2,1)S(1)} collective-permute-done((bf16[64,2048]{1,0:T(8,128)(2,1)S(1)}, bf16[64,2048]{1,0:T(8,128)(2,1)S(1)}, u32[]{:S(2)}, u32[]{:S(2)}) %collective-permute-start.26) | collective-permute-done | bytes 262176 | tf_op jit(solution)/shard_map/ppermute | solution.py:230
  165.8 4.6 %collective-permute-done.24 = bf16[64,2048]{1,0:T(8,128)(2,1)S(1)} collective-permute-done((bf16[64,2048]{1,0:T(8,128)(2,1)S(1)}, bf16[64,2048]{1,0:T(8,128)(2,1)S(1)}, u32[]{:S(2)}, u32[]{:S(2)}) %collective-permute-start.24) | collective-permute-done | bytes 262176 | tf_op jit(solution)/shard_map/ppermute | solution.py:233
  170.6 3.9 %all_to_all.44 = bf16[64,2,1024]{2,0,1:T(8,128)(2,1)S(1)} all-to-all(bf16[64,2,1024]{2,0,1:T(8,128)(2,1)S(1)} %bitcast.67), channel_id=1, replica_groups=mesh['wide'=16,'narrow'=2] {'narrow'}, dimensions={1} | all-to-all | bytes 524288 | tf_op jit(solution)/shard_map/all_to_all | solution.py:325
  174.6 0.7 copy.22
  (96 shorter events, 7.4 us)
Async XLA Ops:
  6.5 13.5 %copy-start = (f32[128,6]{0,1:T(8,128)S(1)}, f32[128,6]{0,1:T(8,128)}, u32[]{:S(2)}) copy-start(f32[128,6]{0,1:T(8,128)} %param.11) | copy-start | bytes 9220
  6.5 85.7 %all-gather.7.cloned.1.call-start = ((), (), s32[]{:S(2)}) async-start(), calls=%async_computation.3 | async-start | bytes 8650752 | tf_op jit(solution)/shard_map/all_gather | solution.py:273
  11.7 22.5 %copy-start.8 = (bf16[2,8,8,1024]{3,2,0,1:T(8,128)(2,1)}, bf16[2,8,8,1024]{3,2,0,1:T(8,128)(2,1)S(1)}, u32[]{:S(2)}) copy-start(bf16[2,8,8,1024]{3,2,0,1:T(8,128)(2,1)S(1)} %copy.17) | copy-start | bytes 786436
  11.7 12.3 %collective-permute-start = (bf16[64,2048]{1,0:T(8,128)(2,1)S(1)}, bf16[64,2048]{1,0:T(8,128)(2,1)S(1)}, u32[]{:S(2)}, u32[]{:S(2)}) collective-permute-start(bf16[64,2048]{1,0:T(8,128)(2,1)S(1)} %bitcast.60), channel_id=1, source_target_pairs={{0,8},{2,10},{4,12},{6,14},{8,16},{10,18},{12,20},{14,22},{16,24},... | collective-permute-start | bytes 786440 | tf_op jit(solution)/shard_map/ppermute | solution.py:233
  14.8 13.7 %collective-permute-start.1 = (bf16[64,2048]{1,0:T(8,128)(2,1)S(1)}, bf16[64,2048]{1,0:T(8,128)(2,1)S(1)}, u32[]{:S(2)}, u32[]{:S(2)}) collective-permute-start(bf16[64,2048]{1,0:T(8,128)(2,1)S(1)} %bitcast.61), channel_id=1, source_target_pairs={{0,24},{2,26},{4,28},{6,30},{8,0},{10,2},{12,4},{14,6},{16,8},{18,... | collective-permute-start | bytes 786440 | tf_op jit(solution)/shard_map/ppermute | solution.py:233
  16.9 11.6 %collective-permute-start.2 = (bf16[64,2048]{1,0:T(8,128)(2,1)S(1)}, bf16[64,2048]{1,0:T(8,128)(2,1)S(1)}, u32[]{:S(2)}, u32[]{:S(2)}) collective-permute-start(bf16[64,2048]{1,0:T(8,128)(2,1)S(1)} %bitcast.62), channel_id=1, source_target_pairs={{0,2},{2,0},{4,6},{6,4},{8,10},{10,8},{12,14},{14,12},{16,18},{18,... | collective-permute-start | bytes 786440 | tf_op jit(solution)/shard_map/ppermute | solution.py:230
  18.5 10.0 %collective-permute-start.3 = (bf16[64,2048]{1,0:T(8,128)(2,1)S(1)}, bf16[64,2048]{1,0:T(8,128)(2,1)S(1)}, u32[]{:S(2)}, u32[]{:S(2)}) collective-permute-start(bf16[64,2048]{1,0:T(8,128)(2,1)S(1)} %bitcast.63), channel_id=1, source_target_pairs={{0,4},{2,6},{4,0},{6,2},{8,12},{10,14},{12,8},{14,10},{16,20},{18,... | collective-permute-start | bytes 786440 | tf_op jit(solution)/shard_map/ppermute | solution.py:230
  24.0 7.5 %copy-start.13 = (bf16[64,2048]{1,0:T(8,128)(2,1)}, bf16[64,2048]{1,0:T(8,128)(2,1)S(1)}, u32[]{:S(2)}) copy-start(bf16[64,2048]{1,0:T(8,128)(2,1)S(1)} %collective-permute-done.refs_0_) | copy-start | bytes 786436
  28.5 5.2 %copy-start.12 = (bf16[64,2048]{1,0:T(8,128)(2,1)}, bf16[64,2048]{1,0:T(8,128)(2,1)S(1)}, u32[]{:S(2)}) copy-start(bf16[64,2048]{1,0:T(8,128)(2,1)S(1)} %collective-permute-done.1.refs_0_) | copy-start | bytes 786436
  28.5 28.1 %copy-start.11 = (bf16[64,2048]{1,0:T(8,128)(2,1)}, bf16[64,2048]{1,0:T(8,128)(2,1)S(1)}, u32[]{:S(2)}) copy-start(bf16[64,2048]{1,0:T(8,128)(2,1)S(1)} %collective-permute-done.3.refs_2_) | copy-start | bytes 786436
  28.5 63.7 %all-gather.9.cloned.1.call-start = ((), (), s32[]{:S(2)}) async-start(), calls=%async_computation.4 | async-start | bytes 8650752 | tf_op jit(solution)/shard_map/all_gather | solution.py:273
  29.3 62.9 %all-gather.11.cloned.1.call-start = ((), (), s32[]{:S(2)}) async-start(), calls=%async_computation.5 | async-start | bytes 8650752 | tf_op jit(solution)/shard_map/all_gather | solution.py:273
  30.0 9.3 %collective-permute-start.5 = (bf16[64,2048]{1,0:T(8,128)(2,1)S(1)}, bf16[64,2048]{1,0:T(8,128)(2,1)S(1)}, u32[]{:S(2)}, u32[]{:S(2)}) collective-permute-start(bf16[64,2048]{1,0:T(8,128)(2,1)S(1)} %collective-permute-done.refs_0_), channel_id=1, source_target_pairs={{0,2},{2,0},{4,6},{6,4},{8,10},{10,8},{12,14},{14,12},{16,18},{18,... | collective-permute-start | bytes 786440 | tf_op jit(solution)/shard_map/ppermute | solution.py:230
  31.6 11.8 %collective-permute-start.7 = (bf16[64,2048]{1,0:T(8,128)(2,1)S(1)}, bf16[64,2048]{1,0:T(8,128)(2,1)S(1)}, u32[]{:S(2)}, u32[]{:S(2)}) collective-permute-start(bf16[64,2048]{1,0:T(8,128)(2,1)S(1)} %collective-permute-done.refs_0_), channel_id=1, source_target_pairs={{0,4},{2,6},{4,0},{6,2},{8,12},{10,14},{12,8},{14,10},{16,20},{18,... | collective-permute-start | bytes 786440 | tf_op jit(solution)/shard_map/ppermute | solution.py:230
  33.1 10.3 %collective-permute-start.6 = (bf16[64,2048]{1,0:T(8,128)(2,1)S(1)}, bf16[64,2048]{1,0:T(8,128)(2,1)S(1)}, u32[]{:S(2)}, u32[]{:S(2)}) collective-permute-start(bf16[64,2048]{1,0:T(8,128)(2,1)S(1)} %collective-permute-done.1.refs_0_), channel_id=1, source_target_pairs={{0,2},{2,0},{4,6},{6,4},{8,10},{10,8},{12,14},{14,12},{16,18},{18,... | collective-permute-start | bytes 786440 | tf_op jit(solution)/shard_map/ppermute | solution.py:230
  33.6 10.9 %collective-permute-start.8 = (bf16[64,2048]{1,0:T(8,128)(2,1)S(1)}, bf16[64,2048]{1,0:T(8,128)(2,1)S(1)}, u32[]{:S(2)}, u32[]{:S(2)}) collective-permute-start(bf16[64,2048]{1,0:T(8,128)(2,1)S(1)} %collective-permute-done.1.refs_0_), channel_id=1, source_target_pairs={{0,4},{2,6},{4,0},{6,2},{8,12},{10,14},{12,8},{14,10},{16,20},{18,... | collective-permute-start | bytes 786440 | tf_op jit(solution)/shard_map/ppermute | solution.py:230
  34.1 13.0 %collective-permute-start.4 = (bf16[64,2048]{1,0:T(8,128)(2,1)S(1)}, bf16[64,2048]{1,0:T(8,128)(2,1)S(1)}, u32[]{:S(2)}, u32[]{:S(2)}) collective-permute-start(bf16[64,2048]{1,0:T(8,128)(2,1)S(1)} %bitcast.64), channel_id=1, source_target_pairs={{0,16},{2,18},{4,20},{6,22},{8,24},{10,26},{12,28},{14,30},{16,0},... | collective-permute-start | bytes 786440 | tf_op jit(solution)/shard_map/ppermute | solution.py:233
  39.3 7.9 %copy-start.16 = (bf16[64,2048]{1,0:T(8,128)(2,1)}, bf16[64,2048]{1,0:T(8,128)(2,1)S(1)}, u32[]{:S(2)}) copy-start(bf16[64,2048]{1,0:T(8,128)(2,1)S(1)} %collective-permute-done.5.refs_1_) | copy-start | bytes 786436
  43.3 48.9 %copy-start.14 = (bf16[64,2048]{1,0:T(8,128)(2,1)}, bf16[64,2048]{1,0:T(8,128)(2,1)S(1)}, u32[]{:S(2)}) copy-start(bf16[64,2048]{1,0:T(8,128)(2,1)S(1)} %collective-permute-done.6.refs_1_) | copy-start | bytes 786436
  43.3 41.2 %copy-start.17 = (bf16[64,2048]{1,0:T(8,128)(2,1)}, bf16[64,2048]{1,0:T(8,128)(2,1)S(1)}, u32[]{:S(2)}) copy-start(bf16[64,2048]{1,0:T(8,128)(2,1)S(1)} %collective-permute-done.7.refs_2_) | copy-start | bytes 786436
  47.2 37.4 %copy-start.19 = (bf16[64,2048]{1,0:T(8,128)(2,1)}, bf16[64,2048]{1,0:T(8,128)(2,1)S(1)}, u32[]{:S(2)}) copy-start(bf16[64,2048]{1,0:T(8,128)(2,1)S(1)} %collective-permute-done.4.refs_0_) | copy-start | bytes 786436
  47.2 37.4 %all-to-all-start.1 = ((bf16[16,288,128]{2,1,0:T(8,128)(2,1)}), bf16[16,288,128]{2,1,0:T(8,128)(2,1)S(1)}, u32[]{:S(2)}, u32[]{:S(2)}) async-start(bf16[16,288,128]{2,1,0:T(8,128)(2,1)} %shard_map.91), calls=%async_computation.1 | async-start | bytes 2359296 | tf_op jit(solution)/shard_map/all_to_all | solution.py:281
  52.5 14.8 %collective-permute-start.11 = (bf16[64,2048]{1,0:T(8,128)(2,1)S(1)}, bf16[64,2048]{1,0:T(8,128)(2,1)S(1)}, u32[]{:S(2)}, u32[]{:S(2)}) collective-permute-start(bf16[64,2048]{1,0:T(8,128)(2,1)S(1)} %collective-permute-done.4.refs_0_), channel_id=1, source_target_pairs={{0,2},{2,0},{4,6},{6,4},{8,10},{10,8},{12,14},{14,12},{16,18},{18,... | collective-permute-start | bytes 786440 | tf_op jit(solution)/shard_map/ppermute | solution.py:230
  54.4 25.7 %collective-permute-start.12 = (bf16[64,2048]{1,0:T(8,128)(2,1)S(1)}, bf16[64,2048]{1,0:T(8,128)(2,1)S(1)}, u32[]{:S(2)}, u32[]{:S(2)}) collective-permute-start(bf16[64,2048]{1,0:T(8,128)(2,1)S(1)} %collective-permute-done.4.refs_0_), channel_id=1, source_target_pairs={{0,4},{2,6},{4,0},{6,2},{8,12},{10,14},{12,8},{14,10},{16,20},{18,... | collective-permute-start | bytes 786440 | tf_op jit(solution)/shard_map/ppermute | solution.py:230
  55.9 24.2 %collective-permute-start.10 = (bf16[64,2048]{1,0:T(8,128)(2,1)S(1)}, bf16[64,2048]{1,0:T(8,128)(2,1)S(1)}, u32[]{:S(2)}, u32[]{:S(2)}) collective-permute-start(bf16[64,2048]{1,0:T(8,128)(2,1)S(1)} %collective-permute-done.7.refs_2_), channel_id=1, source_target_pairs={{0,2},{2,0},{4,6},{6,4},{8,10},{10,8},{12,14},{14,12},{16,18},{18,... | collective-permute-start | bytes 786440 | tf_op jit(solution)/shard_map/ppermute | solution.py:230
  56.4 23.6 %collective-permute-start.14 = (bf16[64,2048]{1,0:T(8,128)(2,1)S(1)}, bf16[64,2048]{1,0:T(8,128)(2,1)S(1)}, u32[]{:S(2)}, u32[]{:S(2)}) collective-permute-start(bf16[64,2048]{1,0:T(8,128)(2,1)S(1)} %collective-permute-done.6.refs_1_), channel_id=1, source_target_pairs={{0,4},{2,6},{4,0},{6,2},{8,12},{10,14},{12,8},{14,10},{16,20},{18,... | collective-permute-start | bytes 786440 | tf_op jit(solution)/shard_map/ppermute | solution.py:230
  56.6 27.8 %collective-permute-start.9 = (bf16[64,2048]{1,0:T(8,128)(2,1)S(1)}, bf16[64,2048]{1,0:T(8,128)(2,1)S(1)}, u32[]{:S(2)}, u32[]{:S(2)}) collective-permute-start(bf16[64,2048]{1,0:T(8,128)(2,1)S(1)} %collective-permute-done.3.refs_2_), channel_id=1, source_target_pairs={{0,2},{2,0},{4,6},{6,4},{8,10},{10,8},{12,14},{14,12},{16,18},{18,... | collective-permute-start | bytes 786440 | tf_op jit(solution)/shard_map/ppermute | solution.py:230
  67.2 17.4 %copy-start.22 = (bf16[64,2048]{1,0:T(8,128)(2,1)}, bf16[64,2048]{1,0:T(8,128)(2,1)S(1)}, u32[]{:S(2)}) copy-start(bf16[64,2048]{1,0:T(8,128)(2,1)S(1)} %collective-permute-done.11.refs_1_) | copy-start | bytes 786436
  67.2 17.4 %collective-permute-start.13 = (bf16[64,2048]{1,0:T(8,128)(2,1)S(1)}, bf16[64,2048]{1,0:T(8,128)(2,1)}, u32[]{:S(2)}, u32[]{:S(2)}) collective-permute-start(bf16[64,2048]{1,0:T(8,128)(2,1)S(1)} %collective-permute-done.11.refs_1_), channel_id=1, source_target_pairs={{0,4},{2,6},{4,0},{6,2},{8,12},{10,14},{12,8},{14,10},{16,20},{18,... | collective-permute-start | bytes 786440 | tf_op jit(solution)/shard_map/ppermute | solution.py:230
  80.0 23.4 %copy-start.21 = (bf16[64,2048]{1,0:T(8,128)(2,1)}, bf16[64,2048]{1,0:T(8,128)(2,1)S(1)}, u32[]{:S(2)}) copy-start(bf16[64,2048]{1,0:T(8,128)(2,1)S(1)} %collective-permute-done.10.refs_3_) | copy-start | bytes 786436
  80.1 4.5 %copy-start.20 = (bf16[64,2048]{1,0:T(8,128)(2,1)}, bf16[64,2048]{1,0:T(8,128)(2,1)S(1)}, u32[]{:S(2)}) copy-start(bf16[64,2048]{1,0:T(8,128)(2,1)S(1)} %collective-permute-done.14.refs_3_) | copy-start | bytes 786436
  84.4 19.1 %copy-start.18 = (bf16[64,2048]{1,0:T(8,128)(2,1)}, bf16[64,2048]{1,0:T(8,128)(2,1)S(1)}, u32[]{:S(2)}) copy-start(bf16[64,2048]{1,0:T(8,128)(2,1)S(1)} %collective-permute-done.9.refs_3_) | copy-start | bytes 786436
  84.6 2.9 %collective-permute-start.15 = (bf16[16,288,128]{2,1,0:T(8,128)(2,1)S(1)}, bf16[16,288,128]{2,1,0:T(8,128)(2,1)S(1)}, u32[]{:S(2)}, u32[]{:S(2)}) collective-permute-start(bf16[16,288,128]{2,1,0:T(8,128)(2,1)S(1)} %all-to-all-done.1.refs_0_), channel_id=1, source_target_pairs={{0,1},{1,0},{2,3},{3,2},{4,5},{5,4},{6,7},{7,6},{8,9},{9,8},{10,11... | collective-permute-start | bytes 3538952 | tf_op jit(solution)/shard_map/ppermute | solution.py:238
  103.5 14.2 %collective-permute-start.16 = (bf16[2,64,2048]{2,1,0:T(8,128)(2,1)}, bf16[2,64,2048]{2,1,0:T(8,128)(2,1)S(1)}, u32[]{:S(2)}, u32[]{:S(2)}) collective-permute-start(bf16[2,64,2048]{2,1,0:T(8,128)(2,1)} %get-tuple-element.84), channel_id=1, source_target_pairs={{0,2},{2,0},{4,6},{6,4},{8,10},{10,8},{12,14},{14,12},{16,18},{18,... | collective-permute-start | bytes 1572872 | tf_op jit(solution)/shard_map/ppermute | solution.py:230
  104.9 12.8 %copy-start.3 = (bf16[2,64,2048]{2,1,0:T(8,128)(2,1)S(1)}, bf16[2,64,2048]{2,1,0:T(8,128)(2,1)}, u32[]{:S(2)}) copy-start(bf16[2,64,2048]{2,1,0:T(8,128)(2,1)} %get-tuple-element.83.refs_9_) | copy-start | bytes 1572868
  116.2 15.1 %collective-permute-start.19 = (bf16[2,64,2048]{2,1,0:T(8,128)(2,1)}, bf16[2,64,2048]{2,1,0:T(8,128)(2,1)S(1)}, u32[]{:S(2)}, u32[]{:S(2)}) collective-permute-start(bf16[2,64,2048]{2,1,0:T(8,128)(2,1)} %get-tuple-element.92), channel_id=1, source_target_pairs={{0,4},{2,6},{4,0},{6,2},{8,12},{10,14},{12,8},{14,10},{16,20},{18,... | collective-permute-start | bytes 1572872 | tf_op jit(solution)/shard_map/ppermute | solution.py:230
  117.8 13.5 %copy-start.4 = (bf16[2,64,2048]{2,1,0:T(8,128)(2,1)S(1)}, bf16[2,64,2048]{2,1,0:T(8,128)(2,1)}, u32[]{:S(2)}) copy-start(bf16[2,64,2048]{2,1,0:T(8,128)(2,1)} %get-tuple-element.91.refs_9_) | copy-start | bytes 1572868
  117.8 27.6 %collective-permute-start.17 = (bf16[64,2048]{1,0:T(8,128)(2,1)S(1)}, bf16[64,2048]{1,0:T(8,128)(2,1)S(1)}, u32[]{:S(2)}, u32[]{:S(2)}) collective-permute-start(bf16[64,2048]{1,0:T(8,128)(2,1)S(1)} %fusion.5.refs_10_), channel_id=1, source_target_pairs={{0,4},{2,6},{4,0},{6,2},{8,12},{10,14},{12,8},{14,10},{16,20},{18,... | collective-permute-start | bytes 786440 | tf_op jit(solution)/shard_map/ppermute | solution.py:230
  131.4 16.5 %collective-permute-start.20 = (bf16[64,2048]{1,0:T(8,128)(2,1)S(1)}, bf16[64,2048]{1,0:T(8,128)(2,1)}, u32[]{:S(2)}, u32[]{:S(2)}) collective-permute-start(bf16[64,2048]{1,0:T(8,128)(2,1)S(1)} %fusion.6.refs_10_), channel_id=1, source_target_pairs={{0,2},{2,0},{4,6},{6,4},{8,10},{10,8},{12,14},{14,12},{16,18},{18,... | collective-permute-start | bytes 786440 | tf_op jit(solution)/shard_map/ppermute | solution.py:230
  132.1 18.4 %copy-start.2 = (bf16[2,64,2048]{2,1,0:T(8,128)(2,1)S(1)}, bf16[2,64,2048]{2,1,0:T(8,128)(2,1)}, u32[]{:S(2)}) copy-start(bf16[2,64,2048]{2,1,0:T(8,128)(2,1)} %get-tuple-element.99.refs_9_) | copy-start | bytes 1572868
  132.1 18.4 %collective-permute-start.22 = (bf16[2,64,2048]{2,1,0:T(8,128)(2,1)}, bf16[2,64,2048]{2,1,0:T(8,128)(2,1)S(1)}, u32[]{:S(2)}, u32[]{:S(2)}) collective-permute-start(bf16[2,64,2048]{2,1,0:T(8,128)(2,1)} %get-tuple-element.100), channel_id=1, source_target_pairs={{0,2},{2,0},{4,6},{6,4},{8,10},{10,8},{12,14},{14,12},{16,18},{18,... | collective-permute-start | bytes 1572872 | tf_op jit(solution)/shard_map/ppermute | solution.py:230
  144.7 14.5 %copy-start.9 = (bf16[2,64,2048]{2,1,0:T(8,128)(2,1)S(1)}, bf16[2,64,2048]{2,1,0:T(8,128)(2,1)}, u32[]{:S(2)}) copy-start(bf16[2,64,2048]{2,1,0:T(8,128)(2,1)} %get-tuple-element.109) | copy-start | bytes 1572868
  144.7 14.5 %collective-permute-start.25 = (bf16[2,64,2048]{2,1,0:T(8,128)(2,1)}, bf16[2,64,2048]{2,1,0:T(8,128)(2,1)S(1)}, u32[]{:S(2)}, u32[]{:S(2)}) collective-permute-start(bf16[2,64,2048]{2,1,0:T(8,128)(2,1)} %get-tuple-element.107), channel_id=1, source_target_pairs={{0,4},{2,6},{4,0},{6,2},{8,12},{10,14},{12,8},{14,10},{16,20},{18,... | collective-permute-start | bytes 1572872 | tf_op jit(solution)/shard_map/ppermute | solution.py:230
  145.5 18.2 %collective-permute-start.18 = (bf16[64,2048]{1,0:T(8,128)(2,1)S(1)}, bf16[64,2048]{1,0:T(8,128)(2,1)S(1)}, u32[]{:S(2)}, u32[]{:S(2)}) collective-permute-start(bf16[64,2048]{1,0:T(8,128)(2,1)S(1)} %fusion.4), channel_id=1, source_target_pairs={{0,16},{2,18},{4,20},{6,22},{8,24},{10,26},{12,28},{14,30},{16,0},... | collective-permute-start | bytes 786440 | tf_op jit(solution)/shard_map/ppermute | solution.py:233
  149.0 14.7 %collective-permute-start.21 = (bf16[64,2048]{1,0:T(8,128)(2,1)S(1)}, bf16[64,2048]{1,0:T(8,128)(2,1)S(1)}, u32[]{:S(2)}, u32[]{:S(2)}) collective-permute-start(bf16[64,2048]{1,0:T(8,128)(2,1)S(1)} %fusion.3), channel_id=1, source_target_pairs={{0,24},{2,26},{4,28},{6,30},{8,0},{10,2},{12,4},{14,6},{16,8},{18,... | collective-permute-start | bytes 786440 | tf_op jit(solution)/shard_map/ppermute | solution.py:233
  150.6 11.5 %collective-permute-start.23 = (bf16[64,2048]{1,0:T(8,128)(2,1)S(1)}, bf16[64,2048]{1,0:T(8,128)(2,1)S(1)}, u32[]{:S(2)}, u32[]{:S(2)}) collective-permute-start(bf16[64,2048]{1,0:T(8,128)(2,1)S(1)} %fusion.7), channel_id=1, source_target_pairs={{0,4},{2,6},{4,0},{6,2},{8,12},{10,14},{12,8},{14,10},{16,20},{18,... | collective-permute-start | bytes 786440 | tf_op jit(solution)/shard_map/ppermute | solution.py:230
  159.3 6.4 %collective-permute-start.26 = (bf16[64,2048]{1,0:T(8,128)(2,1)S(1)}, bf16[64,2048]{1,0:T(8,128)(2,1)S(1)}, u32[]{:S(2)}, u32[]{:S(2)}) collective-permute-start(bf16[64,2048]{1,0:T(8,128)(2,1)S(1)} %fusion.8), channel_id=1, source_target_pairs={{0,2},{2,0},{4,6},{6,4},{8,10},{10,8},{12,14},{14,12},{16,18},{18,... | collective-permute-start | bytes 786440 | tf_op jit(solution)/shard_map/ppermute | solution.py:230
  162.2 8.2 %collective-permute-start.24 = (bf16[64,2048]{1,0:T(8,128)(2,1)S(1)}, bf16[64,2048]{1,0:T(8,128)(2,1)S(1)}, u32[]{:S(2)}, u32[]{:S(2)}) collective-permute-start(bf16[64,2048]{1,0:T(8,128)(2,1)S(1)} %fusion.2), channel_id=1, source_target_pairs={{0,8},{2,10},{4,12},{6,14},{8,16},{10,18},{12,20},{14,22},{16,24},... | collective-permute-start | bytes 786440 | tf_op jit(solution)/shard_map/ppermute | solution.py:233
  (7 other events, 15.2 us)
Sparse Core Ops, SparseCore 0:
  28.6 15.9 all-gather.6
  46.2 17.1 all-gather.8
  64.9 17.1 all-gather.10

commit v2 on v1

--- a/solution.py
+++ b/solution.py
@@ -257,35 +257,38 @@
     coded = jnp.pad(coded, ((0, 0), (0, (padded - units) * chunk - coded.shape[1])))
     stacked = cut(shared_gate, shared_up, shared_down, coded, units, padded)
 
+    trios = [
+        tuple(
+            lax.all_gather(weight[e], "narrow", axis=0, tiled=True)
+            for weight in (expert_gate, expert_up, expert_down)
+        )
+        for e in range(local_experts)
+    ]
+
     near = sorted({1, lines - 1} - {0, lines})
     rest = [d for d in range(1, lines) if d not in near]
-    planes = rest + near + [0]
+    planes = [0] + near[:1] + rest + near[1:]
     x_first = {d: n % 2 == 0 for n, d in enumerate(planes)}
-    lined, by_x, by_y = {0: mine}, {}, {}
+    lined, by_x, by_y, far = {0: mine}, {}, {}, {}
     for d in near:
         lined[d] = shift(mine, d)
     by_x[0], by_y[0] = flip(mine, 1), flip(mine, 2)
-    experts = (expert_gate, expert_up, expert_down)
-    lined, by_x, by_y, stacked, experts = lax.optimization_barrier(
-        (lined, by_x, by_y, stacked, experts)
-    )
-    trios = [
-        tuple(lax.all_gather(weight[e], "narrow", axis=0, tiled=True) for weight in experts)
-        for e in range(local_experts)
-    ]
+    lined, by_x, by_y, stacked = lax.optimization_barrier((lined, by_x, by_y, stacked))
+    recut = lax.all_to_all(stacked, "wide", split_axis=0, concat_axis=0, tiled=True)
     for d in rest:
         lined[d] = shift(lined[0], d)
     for d in near:
-        by_x[d], by_y[d] = flip(lined[d], 1), flip(lined[d], 2)
-    lined, by_x, by_y, stacked = lax.optimization_barrier((lined, by_x, by_y, stacked))
-    recut = lax.all_to_all(stacked, "wide", split_axis=0, concat_axis=0, tiled=True)
+        by_x[d] = flip(lined[d], 1)
+    for d in near[:1]:
+        by_y[d] = flip(lined[d], 2)
+    far[0] = flip(by_x[0], 2)
+    recut, lined, by_x, by_y, far = lax.optimization_barrier((recut, lined, by_x, by_y, far))
+    for d in near[:1]:
+        far[d] = flip(by_y[d], 1)
+    for d in near[1:]:
+        by_y[d], far[d] = flip(lined[d], 2), flip(by_x[d], 2)
     for d in rest:
         by_x[d], by_y[d] = flip(lined[d], 1), flip(lined[d], 2)
-    blocks = {}
-    for d in near[1:] + [0] + near[:1] + rest:
-        far = flip(by_x[d], 2) if x_first[d] else flip(by_y[d], 1)
-        blocks[d] = (lined[d], by_x[d], by_y[d], far)
-    recut, blocks = lax.optimization_barrier((recut, blocks))
     shared = lay_out([recut] + [turn(recut, s) for s in range(1, narrow)], padded, width)
     coded = recut[:, units : units + gate_rows].reshape(wide, gate_rows * chunk)
     coded = coded.astype(jnp.float32)
@@ -309,7 +312,14 @@
 
     for n, d in enumerate(planes):
         after = kept[-1:] + onwards[-1:]
-        keep, send = layer(blocks[d], gates, shared, trios, d, x_first[d], after)
+        blocks = (lined[d], by_x[d], by_y[d], far[d])
+        keep, send = layer(blocks, gates, shared, trios, d, x_first[d], after)
+        if n == 0:
+            keep, send, by_x, by_y, far = lax.optimization_barrier((keep, send, by_x, by_y, far))
+            for k in rest:
+                far[k] = flip(by_x[k], 2) if x_first[k] else flip(by_y[k], 1)
+        elif n == 1:
+            keep, send, far = lax.optimization_barrier((keep, send, far))
         kept.append(keep)
         came.append(flip(send, 1 if x_first[d] else 2))
         if n:

time: 182 us -> 184 us (1.011)
  waiting for transfers between devices: 57.3 us -> 66.4 us
  starting transfers between devices: 44.8 us -> 37.5 us
    ppermute x6, waiting for transfers between devices: 11.7 us -> 36.4 us  [shift(): lax.ppermute(value, 'wide', [(w, (w + PLANE * by) % wide) for w in range(...]
    ppermute x20, waiting for transfers between devices: 42.4 us -> 27.8 us  [flip(): return lax.ppermute(value, 'wide', [(w, w ^ bits) for w in range(wide)])]
    ppermute x20, starting transfers between devices: 27.5 us -> 23.1 us  [flip(): return lax.ppermute(value, 'wide', [(w, w ^ bits) for w in range(wide)])]
    ppermute x6, starting transfers between devices: 11.9 us -> 8.67 us  [shift(): lax.ppermute(value, 'wide', [(w, (w + PLANE * by) % wide) for w in range(...]
    ppermute x1, waiting for transfers between devices: 1.85 us -> 0.01 us  [turn(): lax.ppermute(value, 'narrow', [(c, (c + by) % narrow) for c in range(narr...]
  transfers between devices with their start and end apart: 31 -> 31, of which waited for: 16 -> 10; matrix products, arithmetic and copies ran while one was open for 2% -> 2% of each run, Pallas kernels for 22% -> 28%
where the time goes in v2:
time: 184 us; the launch traced here: 183 us
  waiting for transfers between devices  66.4 us (36%)
  Pallas kernels  51.2 us (28%)
  starting transfers between devices  37.5 us (20%)
  between operations  13.5 us (7%)
  blocking collectives  7.89 us (4%)
  local copies, waits for them, and re-layouts  3.68 us (2%)
  other arithmetic  3.09 us (2%)
    pallas_call x4, Pallas kernels, layer(): pl.pallas_call(functools.partial(layer_kernel, (experts, plane, x_first,...  45 us
    ppermute x6, waiting for transfers between devices, shift(): lax.ppermute(value, 'wide', [(w, (w + PLANE * by) % wide) for w in range(...  36.4 us
    ppermute x20, waiting for transfers between devices, flip(): return lax.ppermute(value, 'wide', [(w, w ^ bits) for w in range(wide)])  27.8 us
    ppermute x20, starting transfers between devices, flip(): return lax.ppermute(value, 'wide', [(w, w ^ bits) for w in range(wide)])  23.1 us
    ppermute x6, starting transfers between devices, shift(): lax.ppermute(value, 'wide', [(w, (w + PLANE * by) % wide) for w in range(...  8.67 us
    all_to_all x1, starting transfers between devices, body(): lax.all_to_all(stacked, 'wide', split_axis=0, concat_axis=0, tiled=True)  5.62 us
    all_to_all x1, blocking collectives, body(): lax.all_to_all(tokens, 'narrow', split_axis=0, concat_axis=1, tiled=True)  3.94 us
    all_to_all x1, blocking collectives, body(): lax.all_to_all(out.astype(jnp.bfloat16), 'narrow', split_axis=1, concat_a...  3.94 us
  transfers between devices with their start and end apart: 31, of which 10 were waited for; matrix products, arithmetic and copies ran while one was open for 2% of the time, Pallas kernels for 28%

profile of v2, /device:TPU:0, one launch (start us, length us, event | category | flops | bytes accessed | tf_op | source)
XLA Modules:
  0.0 183.2 jit_solution(8324330977127824683)
XLA Ops:
  6.5 0.7 all-gather.7.cloned.1.call-update
  7.3 0.7 all-gather.9.cloned.1.call-update
  8.1 0.7 all-gather.11.cloned.1.call-update
  8.8 3.9 %all_to_all.43 = bf16[2,64,1024]{2,1,0:T(8,128)(2,1)S(1)} all-to-all(bf16[2,64,1024]{2,1,0:T(8,128)(2,1)S(1)} %bitcast.74), channel_id=1, replica_groups=mesh['wide'=16,'narrow'=2] {'narrow'}, dimensions={0} | all-to-all | bytes 524288 | tf_op jit(solution)/shard_map/all_to_all | solution.py:240
  12.7 3.1 %collective-permute-start = (bf16[64,2048]{1,0:T(8,128)(2,1)S(1)}, bf16[64,2048]{1,0:T(8,128)(2,1)S(1)}, u32[]{:S(2)}, u32[]{:S(2)}) collective-permute-start(bf16[64,2048]{1,0:T(8,128)(2,1)S(1)} %bitcast.64), channel_id=1, source_target_pairs={{0,8},{2,10},{4,12},{6,14},{8,16},{10,18},{12,20},{14,22},{16,24},... | collective-permute-start | bytes 786440 | tf_op jit(solution)/shard_map/ppermute | solution.py:233
  15.8 2.1 %collective-permute-start.1 = (bf16[64,2048]{1,0:T(8,128)(2,1)S(1)}, bf16[64,2048]{1,0:T(8,128)(2,1)S(1)}, u32[]{:S(2)}, u32[]{:S(2)}) collective-permute-start(bf16[64,2048]{1,0:T(8,128)(2,1)S(1)} %bitcast.65), channel_id=1, source_target_pairs={{0,24},{2,26},{4,28},{6,30},{8,0},{10,2},{12,4},{14,6},{16,8},{18,... | collective-permute-start | bytes 786440 | tf_op jit(solution)/shard_map/ppermute | solution.py:233
  17.9 1.6 collective-permute-start.2
  19.6 1.5 collective-permute-start.3
  21.3 0.6 copy.18
  22.0 2.6 %shard_map.91 = bf16[16,288,128]{2,1,0:T(8,128)(2,1)} custom-call(bf16[128,1408]{1,0:T(8,128)(2,1)} %gate.1, bf16[128,1408]{1,0:T(8,128)(2,1)} %up.1, bf16[1408,128]{1,0:T(8,128)(2,1)} %down.1, bf16[16,8,128]{2,1,0:T(8,128)(2,1)} %bitcast.75), custom_call_target="tpu_custom_call" | custom-call | bytes 2883584 | tf_op jit(solution)/shard_map/pallas_call | solution.py:161
  25.0 4.5 %collective-permute-done.1.refs_0_ = bf16[64,2048]{1,0:T(8,128)(2,1)S(1)} collective-permute-done((bf16[64,2048]{1,0:T(8,128)(2,1)S(1)}, bf16[64,2048]{1,0:T(8,128)(2,1)S(1)}, u32[]{:S(2)}, u32[]{:S(2)}) %collective-permute-start.1) | collective-permute-done | bytes 262176 | tf_op jit(solution)/shard_map/ppermute | solution.py:233
  29.5 0.7 copy-done.14
  30.3 5.6 %all-to-all-start.1 = ((bf16[16,288,128]{2,1,0:T(8,128)(2,1)}), bf16[16,288,128]{2,1,0:T(8,128)(2,1)S(1)}, u32[]{:S(2)}, u32[]{:S(2)}) async-start(bf16[16,288,128]{2,1,0:T(8,128)(2,1)} %shard_map.91), calls=%async_computation.1 | async-start | bytes 2359296 | tf_op jit(solution)/shard_map/all_to_all | solution.py:277
  35.9 1.9 %collective-permute-start.5 = (bf16[64,2048]{1,0:T(8,128)(2,1)S(1)}, bf16[64,2048]{1,0:T(8,128)(2,1)S(1)}, u32[]{:S(2)}, u32[]{:S(2)}) collective-permute-start(bf16[64,2048]{1,0:T(8,128)(2,1)S(1)} %collective-permute-done.refs_0_), channel_id=1, source_target_pairs={{0,2},{2,0},{4,6},{6,4},{8,10},{10,8},{12,14},{14,12},{16,18},{18,... | collective-permute-start | bytes 786440 | tf_op jit(solution)/shard_map/ppermute | solution.py:230
  37.8 1.5 collective-permute-start.7
  39.3 2.4 %collective-permute-start.4 = (bf16[64,2048]{1,0:T(8,128)(2,1)S(1)}, bf16[64,2048]{1,0:T(8,128)(2,1)S(1)}, u32[]{:S(2)}, u32[]{:S(2)}) collective-permute-start(bf16[64,2048]{1,0:T(8,128)(2,1)S(1)} %bitcast.68), channel_id=1, source_target_pairs={{0,16},{2,18},{4,20},{6,22},{8,24},{10,26},{12,28},{14,30},{16,0},... | collective-permute-start | bytes 786440 | tf_op jit(solution)/shard_map/ppermute | solution.py:233
  42.8 11.7 %collective-permute-done.5.refs_1_ = bf16[64,2048]{1,0:T(8,128)(2,1)S(1)} collective-permute-done((bf16[64,2048]{1,0:T(8,128)(2,1)S(1)}, bf16[64,2048]{1,0:T(8,128)(2,1)S(1)}, u32[]{:S(2)}, u32[]{:S(2)}) %collective-permute-start.5) | collective-permute-done | bytes 262176 | tf_op jit(solution)/shard_map/ppermute | solution.py:230
  54.5 20.4 %collective-permute-done.4.refs_0_ = bf16[64,2048]{1,0:T(8,128)(2,1)S(1)} collective-permute-done((bf16[64,2048]{1,0:T(8,128)(2,1)S(1)}, bf16[64,2048]{1,0:T(8,128)(2,1)S(1)}, u32[]{:S(2)}, u32[]{:S(2)}) %collective-permute-start.4) | collective-permute-done | bytes 262176 | tf_op jit(solution)/shard_map/ppermute | solution.py:233
  75.0 0.7 copy-done.15
  75.8 1.5 collective-permute-start.10
  77.3 1.9 %collective-permute-start.11 = (bf16[64,2048]{1,0:T(8,128)(2,1)}, bf16[64,2048]{1,0:T(8,128)(2,1)}, u32[]{:S(2)}, u32[]{:S(2)}) collective-permute-start(bf16[64,2048]{1,0:T(8,128)(2,1)} %copy-done.15), channel_id=1, source_target_pairs={{0,4},{2,6},{4,0},{6,2},{8,12},{10,14},{12,8},{14,10},{16,20},{18,... | collective-permute-start | bytes 786440 | tf_op jit(solution)/shard_map/ppermute | solution.py:230
  79.4 0.7 reshape_transpose_reshape.3.refs_4_
  80.8 1.9 %collective-permute-start.14 = (bf16[64,2048]{1,0:T(8,128)(2,1)S(1)}, bf16[64,2048]{1,0:T(8,128)(2,1)}, u32[]{:S(2)}, u32[]{:S(2)}) collective-permute-start(bf16[64,2048]{1,0:T(8,128)(2,1)S(1)} %collective-permute-done.6.refs_1_), channel_id=1, source_target_pairs={{0,4},{2,6},{4,0},{6,2},{8,12},{10,14},{12,8},{14,10},{16,20},{18,... | collective-permute-start | bytes 786440 | tf_op jit(solution)/shard_map/ppermute | solution.py:230
  82.7 3.6 %shard_map.92.refs_5_ = bf16[3,192,2048]{2,1,0:T(8,128)(2,1)} custom-call(bf16[16,288,128]{2,1,0:T(8,128)(2,1)} %copy-done.1, bf16[16,288,128]{2,1,0:T(8,128)(2,1)} %copy-done.5), custom_call_target="tpu_custom_call" | custom-call | bytes 4718592 | tf_op jit(solution)/shard_map/pallas_call | solution.py:195
  86.3 11.3 %shard_map.93 = (bf16[2,64,2048]{2,1,0:T(8,128)(2,1)}, bf16[2,64,2048]{2,1,0:T(8,128)(2,1)}) custom-call(bf16[64,2048]{1,0:T(8,128)(2,1)} %bitcast.69, bf16[64,2048]{1,0:T(8,128)(2,1)} %copy-done.13, bf16[64,2048]{1,0:T(8,128)(2,1)} %copy-done.14, bf16[64,2048]{1,0:T(8,128)(2,1)} %collective-permute-done.8.refs_3_, ...), custom_call_target="tpu_custom_call" | custom-call | flops 5033164800 | bytes 19660800 | tf_op jit(solution)/shard_map/pallas_call | solution.py:119
  97.7 1.5 collective-permute-start.15
  99.2 1.0 collective-permute-start.16
  100.2 11.2 %shard_map.94 = (bf16[2,64,2048]{2,1,0:T(8,128)(2,1)}, bf16[2,64,2048]{2,1,0:T(8,128)(2,1)}) custom-call(bf16[64,2048]{1,0:T(8,128)(2,1)} %copy-done.11, bf16[64,2048]{1,0:T(8,128)(2,1)} %copy-done.16, bf16[64,2048]{1,0:T(8,128)(2,1)} %copy-done.17, bf16[64,2048]{1,0:T(8,128)(2,1)} %collective-permute-done.13.refs_3_, ...), custom_call_target="tpu_custom_call" | custom-call | flops 5033164800 | bytes 19660800 | tf_op jit(solution)/shard_map/pallas_call | solution.py:119
  111.5 1.1 collective-permute-start.18
  112.7 1.1 collective-permute-start.17
  113.8 11.2 %shard_map.95 = (bf16[2,64,2048]{2,1,0:T(8,128)(2,1)}, bf16[2,64,2048]{2,1,0:T(8,128)(2,1)}) custom-call(bf16[64,2048]{1,0:T(8,128)(2,1)} %copy-done.15, bf16[64,2048]{1,0:T(8,128)(2,1)} %collective-permute-done.10.refs_1_, bf16[64,2048]{1,0:T(8,128)(2,1)} %collective-permute-done.11.refs_2_, bf16[64,2048]{1,0:T(8,128)(2,1)} %copy-done.18, ...), custom_call_target="tpu_custom_call" | custom-call | flops 5033164800 | bytes 19660800 | tf_op jit(solution)/shard_map/pallas_call | solution.py:119
  125.0 1.0 collective-permute-start.21
  126.0 0.6 collective-permute-done.18
  126.7 1.0 collective-permute-start.19
  127.7 11.3 %shard_map.96 = (bf16[2,64,2048]{2,1,0:T(8,128)(2,1)}, bf16[2,64,2048]{2,1,0:T(8,128)(2,1)}) custom-call(bf16[64,2048]{1,0:T(8,128)(2,1)} %copy-done.10, bf16[64,2048]{1,0:T(8,128)(2,1)} %copy-done.12, bf16[64,2048]{1,0:T(8,128)(2,1)} %collective-permute-done.12.refs_2_, bf16[64,2048]{1,0:T(8,128)(2,1)} %collective-permute-done.14.refs_3_, ...), custom_call_target="tpu_custom_call" | custom-call | flops 5033164800 | bytes 19660800 | tf_op jit(solution)/shard_map/pallas_call | solution.py:119
  139.0 0.8 collective-permute-start.24
  139.8 3.3 %collective-permute-done.19 = bf16[64,2048]{1,0:T(8,128)(2,1)} collective-permute-done((bf16[64,2048]{1,0:T(8,128)(2,1)S(1)}, bf16[64,2048]{1,0:T(8,128)(2,1)}, u32[]{:S(2)}, u32[]{:S(2)}) %collective-permute-start.19) | collective-permute-done | bytes 262176 | tf_op jit(solution)/shard_map/ppermute | solution.py:230
  143.1 1.1 fusion.2
  144.2 1.0 collective-permute-start.20
  145.3 1.0 collective-permute-start.22
  146.2 6.9 %collective-permute-done.24 = bf16[2,64,2048]{2,1,0:T(8,128)(2,1)S(1)} collective-permute-done((bf16[2,64,2048]{2,1,0:T(8,128)(2,1)}, bf16[2,64,2048]{2,1,0:T(8,128)(2,1)S(1)}, u32[]{:S(2)}, u32[]{:S(2)}) %collective-permute-start.24) | collective-permute-done | bytes 524320 | tf_op jit(solution)/shard_map/ppermute | solution.py:230
  153.1 1.0 fusion.10
  154.1 1.0 collective-permute-start.25
  155.2 0.8 collective-permute-done.22
  156.1 4.5 %collective-permute-done.25 = bf16[64,2048]{1,0:T(8,128)(2,1)S(1)} collective-permute-done((bf16[64,2048]{1,0:T(8,128)(2,1)S(1)}, bf16[64,2048]{1,0:T(8,128)(2,1)S(1)}, u32[]{:S(2)}, u32[]{:S(2)}) %collective-permute-start.25) | collective-permute-done | bytes 262176 | tf_op jit(solution)/shard_map/ppermute | solution.py:230
  160.8 11.0 %collective-permute-done.23 = bf16[64,2048]{1,0:T(8,128)(2,1)S(1)} collective-permute-done((bf16[64,2048]{1,0:T(8,128)(2,1)S(1)}, bf16[64,2048]{1,0:T(8,128)(2,1)S(1)}, u32[]{:S(2)}, u32[]{:S(2)}) %collective-permute-start.23) | collective-permute-done | bytes 262176 | tf_op jit(solution)/shard_map/ppermute | solution.py:233
  172.0 3.9 %all_to_all.44 = bf16[64,2,1024]{2,0,1:T(8,128)(2,1)S(1)} all-to-all(bf16[64,2,1024]{2,0,1:T(8,128)(2,1)S(1)} %bitcast.71), channel_id=1, replica_groups=mesh['wide'=16,'narrow'=2] {'narrow'}, dimensions={1} | all-to-all | bytes 524288 | tf_op jit(solution)/shard_map/all_to_all | solution.py:335
  176.0 0.7 copy.22
  (90 shorter events, 3.9 us)
Async XLA Ops:
  6.5 14.6 %copy-start = (f32[128,6]{0,1:T(8,128)S(1)}, f32[128,6]{0,1:T(8,128)}, u32[]{:S(2)}) copy-start(f32[128,6]{0,1:T(8,128)} %param.11) | copy-start | bytes 9220
  6.5 79.7 %all-gather.7.cloned.1.call-start = ((), (), s32[]{:S(2)}) async-start(), calls=%async_computation.3 | async-start | bytes 8650752 | tf_op jit(solution)/shard_map/all_gather | solution.py:262
  7.3 1.5 copy-start.19
  7.3 13.9 %copy-start.20 = (s32[128,6]{0,1:T(8,128)S(1)}, s32[128,6]{0,1:T(8,128)}, u32[]{:S(2)}) copy-start(s32[128,6]{0,1:T(8,128)} %param.10) | copy-start | bytes 9220
  7.3 79.0 %all-gather.9.cloned.1.call-start = ((), (), s32[]{:S(2)}) async-start(), calls=%async_computation.4 | async-start | bytes 8650752 | tf_op jit(solution)/shard_map/all_gather | solution.py:262
  8.0 78.3 %all-gather.11.cloned.1.call-start = ((), (), s32[]{:S(2)}) async-start(), calls=%async_computation.5 | async-start | bytes 8650752 | tf_op jit(solution)/shard_map/all_gather | solution.py:262
  12.7 73.5 %copy-start.8 = (bf16[2,8,8,1024]{3,2,0,1:T(8,128)(2,1)}, bf16[2,8,8,1024]{3,2,0,1:T(8,128)(2,1)S(1)}, u32[]{:S(2)}) copy-start(bf16[2,8,8,1024]{3,2,0,1:T(8,128)(2,1)S(1)} %copy.17) | copy-start | bytes 786436
  12.7 12.2 %collective-permute-start = (bf16[64,2048]{1,0:T(8,128)(2,1)S(1)}, bf16[64,2048]{1,0:T(8,128)(2,1)S(1)}, u32[]{:S(2)}, u32[]{:S(2)}) collective-permute-start(bf16[64,2048]{1,0:T(8,128)(2,1)S(1)} %bitcast.64), channel_id=1, source_target_pairs={{0,8},{2,10},{4,12},{6,14},{8,16},{10,18},{12,20},{14,22},{16,24},... | collective-permute-start | bytes 786440 | tf_op jit(solution)/shard_map/ppermute | solution.py:233
  15.8 13.7 %collective-permute-start.1 = (bf16[64,2048]{1,0:T(8,128)(2,1)S(1)}, bf16[64,2048]{1,0:T(8,128)(2,1)S(1)}, u32[]{:S(2)}, u32[]{:S(2)}) collective-permute-start(bf16[64,2048]{1,0:T(8,128)(2,1)S(1)} %bitcast.65), channel_id=1, source_target_pairs={{0,24},{2,26},{4,28},{6,30},{8,0},{10,2},{12,4},{14,6},{16,8},{18,... | collective-permute-start | bytes 786440 | tf_op jit(solution)/shard_map/ppermute | solution.py:233
  17.9 11.6 %collective-permute-start.2 = (bf16[64,2048]{1,0:T(8,128)(2,1)S(1)}, bf16[64,2048]{1,0:T(8,128)(2,1)S(1)}, u32[]{:S(2)}, u32[]{:S(2)}) collective-permute-start(bf16[64,2048]{1,0:T(8,128)(2,1)S(1)} %bitcast.66), channel_id=1, source_target_pairs={{0,2},{2,0},{4,6},{6,4},{8,10},{10,8},{12,14},{14,12},{16,18},{18,... | collective-permute-start | bytes 786440 | tf_op jit(solution)/shard_map/ppermute | solution.py:230
  19.6 10.0 %collective-permute-start.3 = (bf16[64,2048]{1,0:T(8,128)(2,1)S(1)}, bf16[64,2048]{1,0:T(8,128)(2,1)S(1)}, u32[]{:S(2)}, u32[]{:S(2)}) collective-permute-start(bf16[64,2048]{1,0:T(8,128)(2,1)S(1)} %bitcast.67), channel_id=1, source_target_pairs={{0,4},{2,6},{4,0},{6,2},{8,12},{10,14},{12,8},{14,10},{16,20},{18,... | collective-permute-start | bytes 786440 | tf_op jit(solution)/shard_map/ppermute | solution.py:230
  25.0 61.3 %copy-start.11 = (bf16[64,2048]{1,0:T(8,128)(2,1)}, bf16[64,2048]{1,0:T(8,128)(2,1)S(1)}, u32[]{:S(2)}) copy-start(bf16[64,2048]{1,0:T(8,128)(2,1)S(1)} %collective-permute-done.refs_0_) | copy-start | bytes 786436
  29.5 56.7 %copy-start.10 = (bf16[64,2048]{1,0:T(8,128)(2,1)}, bf16[64,2048]{1,0:T(8,128)(2,1)S(1)}, u32[]{:S(2)}) copy-start(bf16[64,2048]{1,0:T(8,128)(2,1)S(1)} %collective-permute-done.1.refs_0_) | copy-start | bytes 786436
  29.5 46.1 %copy-start.13 = (bf16[64,2048]{1,0:T(8,128)(2,1)}, bf16[64,2048]{1,0:T(8,128)(2,1)S(1)}, u32[]{:S(2)}) copy-start(bf16[64,2048]{1,0:T(8,128)(2,1)S(1)} %collective-permute-done.2.refs_1_) | copy-start | bytes 786436
  30.3 45.4 %all-to-all-start.1 = ((bf16[16,288,128]{2,1,0:T(8,128)(2,1)}), bf16[16,288,128]{2,1,0:T(8,128)(2,1)S(1)}, u32[]{:S(2)}, u32[]{:S(2)}) async-start(bf16[16,288,128]{2,1,0:T(8,128)(2,1)} %shard_map.91), calls=%async_computation.1 | async-start | bytes 2359296 | tf_op jit(solution)/shard_map/all_to_all | solution.py:277
  35.9 18.6 %collective-permute-start.5 = (bf16[64,2048]{1,0:T(8,128)(2,1)S(1)}, bf16[64,2048]{1,0:T(8,128)(2,1)S(1)}, u32[]{:S(2)}, u32[]{:S(2)}) collective-permute-start(bf16[64,2048]{1,0:T(8,128)(2,1)S(1)} %collective-permute-done.refs_0_), channel_id=1, source_target_pairs={{0,2},{2,0},{4,6},{6,4},{8,10},{10,8},{12,14},{14,12},{16,18},{18,... | collective-permute-start | bytes 786440 | tf_op jit(solution)/shard_map/ppermute | solution.py:230
  37.8 16.7 %collective-permute-start.7 = (bf16[64,2048]{1,0:T(8,128)(2,1)S(1)}, bf16[64,2048]{1,0:T(8,128)(2,1)S(1)}, u32[]{:S(2)}, u32[]{:S(2)}) collective-permute-start(bf16[64,2048]{1,0:T(8,128)(2,1)S(1)} %collective-permute-done.refs_0_), channel_id=1, source_target_pairs={{0,4},{2,6},{4,0},{6,2},{8,12},{10,14},{12,8},{14,10},{16,20},{18,... | collective-permute-start | bytes 786440 | tf_op jit(solution)/shard_map/ppermute | solution.py:230
  39.3 35.6 %collective-permute-start.4 = (bf16[64,2048]{1,0:T(8,128)(2,1)S(1)}, bf16[64,2048]{1,0:T(8,128)(2,1)S(1)}, u32[]{:S(2)}, u32[]{:S(2)}) collective-permute-start(bf16[64,2048]{1,0:T(8,128)(2,1)S(1)} %bitcast.68), channel_id=1, source_target_pairs={{0,16},{2,18},{4,20},{6,22},{8,24},{10,26},{12,28},{14,30},{16,0},... | collective-permute-start | bytes 786440 | tf_op jit(solution)/shard_map/ppermute | solution.py:233
  41.7 33.3 %collective-permute-start.6 = (bf16[64,2048]{1,0:T(8,128)(2,1)S(1)}, bf16[64,2048]{1,0:T(8,128)(2,1)S(1)}, u32[]{:S(2)}, u32[]{:S(2)}) collective-permute-start(bf16[64,2048]{1,0:T(8,128)(2,1)S(1)} %collective-permute-done.1.refs_0_), channel_id=1, source_target_pairs={{0,2},{2,0},{4,6},{6,4},{8,10},{10,8},{12,14},{14,12},{16,18},{18,... | collective-permute-start | bytes 786440 | tf_op jit(solution)/shard_map/ppermute | solution.py:230
  42.2 33.4 %collective-permute-start.8 = (bf16[64,2048]{1,0:T(8,128)(2,1)S(1)}, bf16[64,2048]{1,0:T(8,128)(2,1)}, u32[]{:S(2)}, u32[]{:S(2)}) collective-permute-start(bf16[64,2048]{1,0:T(8,128)(2,1)S(1)} %collective-permute-done.2.refs_1_), channel_id=1, source_target_pairs={{0,4},{2,6},{4,0},{6,2},{8,12},{10,14},{12,8},{14,10},{16,20},{18,... | collective-permute-start | bytes 786440 | tf_op jit(solution)/shard_map/ppermute | solution.py:230
  54.5 20.4 %copy-start.16 = (bf16[64,2048]{1,0:T(8,128)(2,1)}, bf16[64,2048]{1,0:T(8,128)(2,1)S(1)}, u32[]{:S(2)}) copy-start(bf16[64,2048]{1,0:T(8,128)(2,1)S(1)} %collective-permute-done.5.refs_1_) | copy-start | bytes 786436
  54.5 20.4 %copy-start.17 = (bf16[64,2048]{1,0:T(8,128)(2,1)}, bf16[64,2048]{1,0:T(8,128)(2,1)S(1)}, u32[]{:S(2)}) copy-start(bf16[64,2048]{1,0:T(8,128)(2,1)S(1)} %collective-permute-done.7.refs_2_) | copy-start | bytes 786436
  75.6 22.0 %copy-start.12 = (bf16[64,2048]{1,0:T(8,128)(2,1)}, bf16[64,2048]{1,0:T(8,128)(2,1)S(1)}, u32[]{:S(2)}) copy-start(bf16[64,2048]{1,0:T(8,128)(2,1)S(1)} %collective-permute-done.6.refs_1_) | copy-start | bytes 786436
  75.6 7.0 %copy-start.1 = (bf16[16,288,128]{2,1,0:T(8,128)(2,1)}, bf16[16,288,128]{2,1,0:T(8,128)(2,1)S(1)}, u32[]{:S(2)}) copy-start(bf16[16,288,128]{2,1,0:T(8,128)(2,1)S(1)} %all-to-all-done.1.refs_0_) | copy-start | bytes 3538948
  75.7 5.1 %collective-permute-start.9 = (bf16[16,288,128]{2,1,0:T(8,128)(2,1)S(1)}, bf16[16,288,128]{2,1,0:T(8,128)(2,1)S(1)}, u32[]{:S(2)}, u32[]{:S(2)}) collective-permute-start(bf16[16,288,128]{2,1,0:T(8,128)(2,1)S(1)} %all-to-all-done.1.refs_0_), channel_id=1, source_target_pairs={{0,1},{1,0},{2,3},{3,2},{4,5},{5,4},{6,7},{7,6},{8,9},{9,8},{10,11... | collective-permute-start | bytes 3538952 | tf_op jit(solution)/shard_map/ppermute | solution.py:238
  75.8 21.8 %collective-permute-start.10 = (bf16[64,2048]{1,0:T(8,128)(2,1)}, bf16[64,2048]{1,0:T(8,128)(2,1)}, u32[]{:S(2)}, u32[]{:S(2)}) collective-permute-start(bf16[64,2048]{1,0:T(8,128)(2,1)} %copy-done.15), channel_id=1, source_target_pairs={{0,2},{2,0},{4,6},{6,4},{8,10},{10,8},{12,14},{14,12},{16,18},{18,... | collective-permute-start | bytes 786440 | tf_op jit(solution)/shard_map/ppermute | solution.py:230
  77.3 20.3 %collective-permute-start.11 = (bf16[64,2048]{1,0:T(8,128)(2,1)}, bf16[64,2048]{1,0:T(8,128)(2,1)}, u32[]{:S(2)}, u32[]{:S(2)}) collective-permute-start(bf16[64,2048]{1,0:T(8,128)(2,1)} %copy-done.15), channel_id=1, source_target_pairs={{0,4},{2,6},{4,0},{6,2},{8,12},{10,14},{12,8},{14,10},{16,20},{18,... | collective-permute-start | bytes 786440 | tf_op jit(solution)/shard_map/ppermute | solution.py:230
  80.1 17.6 %collective-permute-start.12 = (bf16[64,2048]{1,0:T(8,128)(2,1)S(1)}, bf16[64,2048]{1,0:T(8,128)(2,1)}, u32[]{:S(2)}, u32[]{:S(2)}) collective-permute-start(bf16[64,2048]{1,0:T(8,128)(2,1)S(1)} %collective-permute-done.1.refs_0_), channel_id=1, source_target_pairs={{0,4},{2,6},{4,0},{6,2},{8,12},{10,14},{12,8},{14,10},{16,20},{18,... | collective-permute-start | bytes 786440 | tf_op jit(solution)/shard_map/ppermute | solution.py:230
  80.2 17.4 %collective-permute-start.13 = (bf16[64,2048]{1,0:T(8,128)(2,1)}, bf16[64,2048]{1,0:T(8,128)(2,1)}, u32[]{:S(2)}, u32[]{:S(2)}) collective-permute-start(bf16[64,2048]{1,0:T(8,128)(2,1)} %copy-done.17), channel_id=1, source_target_pairs={{0,2},{2,0},{4,6},{6,4},{8,10},{10,8},{12,14},{14,12},{16,18},{18,... | collective-permute-start | bytes 786440 | tf_op jit(solution)/shard_map/ppermute | solution.py:230
  80.8 1.9 %copy-start.5 = (bf16[16,288,128]{2,1,0:T(8,128)(2,1)}, bf16[16,288,128]{2,1,0:T(8,128)(2,1)S(1)}, u32[]{:S(2)}) copy-start(bf16[16,288,128]{2,1,0:T(8,128)(2,1)S(1)} %collective-permute-done.9.refs_1_) | copy-start | bytes 3538948
  80.8 16.9 %collective-permute-start.14 = (bf16[64,2048]{1,0:T(8,128)(2,1)S(1)}, bf16[64,2048]{1,0:T(8,128)(2,1)}, u32[]{:S(2)}, u32[]{:S(2)}) collective-permute-start(bf16[64,2048]{1,0:T(8,128)(2,1)S(1)} %collective-permute-done.6.refs_1_), channel_id=1, source_target_pairs={{0,4},{2,6},{4,0},{6,2},{8,12},{10,14},{12,8},{14,10},{16,20},{18,... | collective-permute-start | bytes 786440 | tf_op jit(solution)/shard_map/ppermute | solution.py:230
  97.7 14.9 %copy-start.2 = (bf16[2,64,2048]{2,1,0:T(8,128)(2,1)S(1)}, bf16[2,64,2048]{2,1,0:T(8,128)(2,1)}, u32[]{:S(2)}) copy-start(bf16[2,64,2048]{2,1,0:T(8,128)(2,1)} %get-tuple-element.70.refs_9_) | copy-start | bytes 1572868
  97.7 14.9 %collective-permute-start.15 = (bf16[2,64,2048]{2,1,0:T(8,128)(2,1)}, bf16[2,64,2048]{2,1,0:T(8,128)(2,1)S(1)}, u32[]{:S(2)}, u32[]{:S(2)}) collective-permute-start(bf16[2,64,2048]{2,1,0:T(8,128)(2,1)} %get-tuple-element.71), channel_id=1, source_target_pairs={{0,2},{2,0},{4,6},{6,4},{8,10},{10,8},{12,14},{14,12},{16,18},{18,... | collective-permute-start | bytes 1572872 | tf_op jit(solution)/shard_map/ppermute | solution.py:230
  99.2 12.3 %collective-permute-start.16 = (bf16[64,2048]{1,0:T(8,128)(2,1)}, bf16[64,2048]{1,0:T(8,128)(2,1)S(1)}, u32[]{:S(2)}, u32[]{:S(2)}) collective-permute-start(bf16[64,2048]{1,0:T(8,128)(2,1)} %collective-permute-done.10.refs_1_), channel_id=1, source_target_pairs={{0,4},{2,6},{4,0},{6,2},{8,12},{10,14},{12,8},{14,10},{16,20},{18,... | collective-permute-start | bytes 786440 | tf_op jit(solution)/shard_map/ppermute | solution.py:230
  111.5 2.3 %copy-start.18 = (bf16[64,2048]{1,0:T(8,128)(2,1)}, bf16[64,2048]{1,0:T(8,128)(2,1)S(1)}, u32[]{:S(2)}) copy-start(bf16[64,2048]{1,0:T(8,128)(2,1)S(1)} %collective-permute-done.16.refs_3_) | copy-start | bytes 786436
  111.5 15.1 %collective-permute-start.18 = (bf16[2,64,2048]{2,1,0:T(8,128)(2,1)}, bf16[2,64,2048]{2,1,0:T(8,128)(2,1)S(1)}, u32[]{:S(2)}, u32[]{:S(2)}) collective-permute-start(bf16[2,64,2048]{2,1,0:T(8,128)(2,1)} %get-tuple-element.83), channel_id=1, source_target_pairs={{0,4},{2,6},{4,0},{6,2},{8,12},{10,14},{12,8},{14,10},{16,20},{18,... | collective-permute-start | bytes 1572872 | tf_op jit(solution)/shard_map/ppermute | solution.py:230
  112.7 14.0 %copy-start.4 = (bf16[2,64,2048]{2,1,0:T(8,128)(2,1)S(1)}, bf16[2,64,2048]{2,1,0:T(8,128)(2,1)}, u32[]{:S(2)}) copy-start(bf16[2,64,2048]{2,1,0:T(8,128)(2,1)} %get-tuple-element.82.refs_9_) | copy-start | bytes 1572868
  112.7 48.1 %collective-permute-start.17 = (bf16[64,2048]{1,0:T(8,128)(2,1)S(1)}, bf16[64,2048]{1,0:T(8,128)(2,1)S(1)}, u32[]{:S(2)}, u32[]{:S(2)}) collective-permute-start(bf16[64,2048]{1,0:T(8,128)(2,1)S(1)} %fusion.7.refs_10_), channel_id=1, source_target_pairs={{0,4},{2,6},{4,0},{6,2},{8,12},{10,14},{12,8},{14,10},{16,20},{18,... | collective-permute-start | bytes 786440 | tf_op jit(solution)/shard_map/ppermute | solution.py:230
  125.0 20.2 %collective-permute-start.21 = (bf16[2,64,2048]{2,1,0:T(8,128)(2,1)}, bf16[2,64,2048]{2,1,0:T(8,128)(2,1)S(1)}, u32[]{:S(2)}, u32[]{:S(2)}) collective-permute-start(bf16[2,64,2048]{2,1,0:T(8,128)(2,1)} %get-tuple-element.89), channel_id=1, source_target_pairs={{0,2},{2,0},{4,6},{6,4},{8,10},{10,8},{12,14},{14,12},{16,18},{18,... | collective-permute-start | bytes 1572872 | tf_op jit(solution)/shard_map/ppermute | solution.py:230
  126.7 18.4 %copy-start.3 = (bf16[2,64,2048]{2,1,0:T(8,128)(2,1)S(1)}, bf16[2,64,2048]{2,1,0:T(8,128)(2,1)}, u32[]{:S(2)}) copy-start(bf16[2,64,2048]{2,1,0:T(8,128)(2,1)} %get-tuple-element.88.refs_9_) | copy-start | bytes 1572868
  126.7 16.3 %collective-permute-start.19 = (bf16[64,2048]{1,0:T(8,128)(2,1)S(1)}, bf16[64,2048]{1,0:T(8,128)(2,1)}, u32[]{:S(2)}, u32[]{:S(2)}) collective-permute-start(bf16[64,2048]{1,0:T(8,128)(2,1)S(1)} %fusion.8.refs_10_), channel_id=1, source_target_pairs={{0,2},{2,0},{4,6},{6,4},{8,10},{10,8},{12,14},{14,12},{16,18},{18,... | collective-permute-start | bytes 786440 | tf_op jit(solution)/shard_map/ppermute | solution.py:230
  139.0 21.6 %copy-start.9 = (bf16[2,64,2048]{2,1,0:T(8,128)(2,1)S(1)}, bf16[2,64,2048]{2,1,0:T(8,128)(2,1)}, u32[]{:S(2)}) copy-start(bf16[2,64,2048]{2,1,0:T(8,128)(2,1)} %get-tuple-element.97) | copy-start | bytes 1572868
  139.0 14.1 %collective-permute-start.24 = (bf16[2,64,2048]{2,1,0:T(8,128)(2,1)}, bf16[2,64,2048]{2,1,0:T(8,128)(2,1)S(1)}, u32[]{:S(2)}, u32[]{:S(2)}) collective-permute-start(bf16[2,64,2048]{2,1,0:T(8,128)(2,1)} %get-tuple-element.95), channel_id=1, source_target_pairs={{0,4},{2,6},{4,0},{6,2},{8,12},{10,14},{12,8},{14,10},{16,20},{18,... | collective-permute-start | bytes 1572872 | tf_op jit(solution)/shard_map/ppermute | solution.py:230
  144.2 16.6 %collective-permute-start.20 = (bf16[64,2048]{1,0:T(8,128)(2,1)S(1)}, bf16[64,2048]{1,0:T(8,128)(2,1)S(1)}, u32[]{:S(2)}, u32[]{:S(2)}) collective-permute-start(bf16[64,2048]{1,0:T(8,128)(2,1)S(1)} %fusion.2), channel_id=1, source_target_pairs={{0,24},{2,26},{4,28},{6,30},{8,0},{10,2},{12,4},{14,6},{16,8},{18,... | collective-permute-start | bytes 786440 | tf_op jit(solution)/shard_map/ppermute | solution.py:233
  145.3 10.7 %collective-permute-start.22 = (bf16[64,2048]{1,0:T(8,128)(2,1)S(1)}, bf16[64,2048]{1,0:T(8,128)(2,1)S(1)}, u32[]{:S(2)}, u32[]{:S(2)}) collective-permute-start(bf16[64,2048]{1,0:T(8,128)(2,1)S(1)} %fusion.9), channel_id=1, source_target_pairs={{0,4},{2,6},{4,0},{6,2},{8,12},{10,14},{12,8},{14,10},{16,20},{18,... | collective-permute-start | bytes 786440 | tf_op jit(solution)/shard_map/ppermute | solution.py:230
  154.1 6.4 %collective-permute-start.25 = (bf16[64,2048]{1,0:T(8,128)(2,1)S(1)}, bf16[64,2048]{1,0:T(8,128)(2,1)S(1)}, u32[]{:S(2)}, u32[]{:S(2)}) collective-permute-start(bf16[64,2048]{1,0:T(8,128)(2,1)S(1)} %fusion.10), channel_id=1, source_target_pairs={{0,2},{2,0},{4,6},{6,4},{8,10},{10,8},{12,14},{14,12},{16,18},{18,... | collective-permute-start | bytes 786440 | tf_op jit(solution)/shard_map/ppermute | solution.py:230
  156.0 15.7 %collective-permute-start.23 = (bf16[64,2048]{1,0:T(8,128)(2,1)S(1)}, bf16[64,2048]{1,0:T(8,128)(2,1)S(1)}, u32[]{:S(2)}, u32[]{:S(2)}) collective-permute-start(bf16[64,2048]{1,0:T(8,128)(2,1)S(1)} %fusion.1), channel_id=1, source_target_pairs={{0,16},{2,18},{4,20},{6,22},{8,24},{10,26},{12,28},{14,30},{16,0},... | collective-permute-start | bytes 786440 | tf_op jit(solution)/shard_map/ppermute | solution.py:233
  160.7 11.1 %collective-permute-start.26 = (bf16[64,2048]{1,0:T(8,128)(2,1)S(1)}, bf16[64,2048]{1,0:T(8,128)(2,1)S(1)}, u32[]{:S(2)}, u32[]{:S(2)}) collective-permute-start(bf16[64,2048]{1,0:T(8,128)(2,1)S(1)} %fusion), channel_id=1, source_target_pairs={{0,8},{2,10},{4,12},{6,14},{8,16},{10,18},{12,20},{14,22},{16,24},... | collective-permute-start | bytes 786440 | tf_op jit(solution)/shard_map/ppermute | solution.py:233
  (4 other events, 3.6 us)
Sparse Core Ops, SparseCore 0:
  8.9 18.6 all-gather.6
  29.2 17.1 all-gather.8
  47.9 17.1 all-gather.10

commit v3 on v2

--- a/solution.py
+++ b/solution.py
@@ -265,7 +265,7 @@
         for e in range(local_experts)
     ]
 
-    near = sorted({1, lines - 1} - {0, lines})
+    near = [lines // 2]
     rest = [d for d in range(1, lines) if d not in near]
     planes = [0] + near[:1] + rest + near[1:]
     x_first = {d: n % 2 == 0 for n, d in enumerate(planes)}

time: 184 us -> 185 us (level)
  starting transfers between devices: 37.5 us -> 59.9 us
  waiting for transfers between devices: 66.4 us -> 45.5 us
    ppermute x20, waiting for transfers between devices: 27.8 us -> 8.06 us  [flip(): return lax.ppermute(value, 'wide', [(w, w ^ bits) for w in range(wide)])]
    ppermute x6, starting transfers between devices: 8.67 us -> 27.3 us  [shift(): lax.ppermute(value, 'wide', [(w, (w + PLANE * by) % wide) for w in range(...]
    ppermute x20, starting transfers between devices: 23.1 us -> 25.7 us  [flip(): return lax.ppermute(value, 'wide', [(w, w ^ bits) for w in range(wide)])]
  transfers between devices with their start and end apart: 31 -> 31, of which waited for: 10 -> 8; matrix products, arithmetic and copies ran while one was open for 2% -> 2% of each run, Pallas kernels for 28% -> 28%
where the time goes in v3:
time: 185 us; the launch traced here: 184 us
  starting transfers between devices  59.9 us (32%)
  Pallas kernels  51.2 us (28%)
  waiting for transfers between devices  45.5 us (25%)
  between operations  13.5 us (7%)
  blocking collectives  7.89 us (4%)
  local copies, waits for them, and re-layouts  3.31 us (2%)
  other arithmetic  3.08 us (2%)
    pallas_call x4, Pallas kernels, layer(): pl.pallas_call(functools.partial(layer_kernel, (experts, plane, x_first,...  45 us
    ppermute x6, waiting for transfers between devices, shift(): lax.ppermute(value, 'wide', [(w, (w + PLANE * by) % wide) for w in range(...  35.3 us
    ppermute x6, starting transfers between devices, shift(): lax.ppermute(value, 'wide', [(w, (w + PLANE * by) % wide) for w in range(...  27.3 us
    ppermute x20, starting transfers between devices, flip(): return lax.ppermute(value, 'wide', [(w, w ^ bits) for w in range(wide)])  25.7 us
    ppermute x20, waiting for transfers between devices, flip(): return lax.ppermute(value, 'wide', [(w, w ^ bits) for w in range(wide)])  8.06 us
    all_to_all x1, starting transfers between devices, body(): lax.all_to_all(stacked, 'wide', split_axis=0, concat_axis=0, tiled=True)  6.81 us
    all_to_all x1, blocking collectives, body(): lax.all_to_all(tokens, 'narrow', split_axis=0, concat_axis=1, tiled=True)  3.94 us
    all_to_all x1, blocking collectives, body(): lax.all_to_all(out.astype(jnp.bfloat16), 'narrow', split_axis=1, concat_a...  3.94 us
  transfers between devices with their start and end apart: 31, of which 8 were waited for; matrix products, arithmetic and copies ran while one was open for 2% of the time, Pallas kernels for 28%

profile of v3, /device:TPU:0, one launch (start us, length us, event | category | flops | bytes accessed | tf_op | source)
XLA Modules:
  0.0 184.4 jit_solution(3509632300910564886)
XLA Ops:
  6.5 0.7 all-gather.7.cloned.1.call-update
  7.3 0.7 all-gather.9.cloned.1.call-update
  8.1 0.7 all-gather.11.cloned.1.call-update
  8.8 3.9 %all_to_all.43 = bf16[2,64,1024]{2,1,0:T(8,128)(2,1)S(1)} all-to-all(bf16[2,64,1024]{2,1,0:T(8,128)(2,1)S(1)} %bitcast.74), channel_id=1, replica_groups=mesh['wide'=16,'narrow'=2] {'narrow'}, dimensions={0} | all-to-all | bytes 524288 | tf_op jit(solution)/shard_map/all_to_all | solution.py:240
  12.7 4.1 %collective-permute-start = (bf16[64,2048]{1,0:T(8,128)(2,1)S(1)}, bf16[64,2048]{1,0:T(8,128)(2,1)S(1)}, u32[]{:S(2)}, u32[]{:S(2)}) collective-permute-start(bf16[64,2048]{1,0:T(8,128)(2,1)S(1)} %bitcast.64), channel_id=1, source_target_pairs={{0,16},{2,18},{4,20},{6,22},{8,24},{10,26},{12,28},{14,30},{16,0},... | collective-permute-start | bytes 786440 | tf_op jit(solution)/shard_map/ppermute | solution.py:233
  16.9 1.5 collective-permute-start.1
  18.3 1.5 collective-permute-start.2
  20.1 0.6 copy.18
  20.7 2.6 %shard_map.91 = bf16[16,288,128]{2,1,0:T(8,128)(2,1)} custom-call(bf16[128,1408]{1,0:T(8,128)(2,1)} %gate.1, bf16[128,1408]{1,0:T(8,128)(2,1)} %up.1, bf16[1408,128]{1,0:T(8,128)(2,1)} %down.1, bf16[16,8,128]{2,1,0:T(8,128)(2,1)} %bitcast.75), custom_call_target="tpu_custom_call" | custom-call | bytes 2883584 | tf_op jit(solution)/shard_map/pallas_call | solution.py:161
  23.4 5.7 %collective-permute-done.refs_0_ = bf16[64,2048]{1,0:T(8,128)(2,1)S(1)} collective-permute-done((bf16[64,2048]{1,0:T(8,128)(2,1)S(1)}, bf16[64,2048]{1,0:T(8,128)(2,1)S(1)}, u32[]{:S(2)}, u32[]{:S(2)}) %collective-permute-start) | collective-permute-done | bytes 262176 | tf_op jit(solution)/shard_map/ppermute | solution.py:233
  29.1 6.8 %all-to-all-start.1 = ((bf16[16,288,128]{2,1,0:T(8,128)(2,1)}), bf16[16,288,128]{2,1,0:T(8,128)(2,1)S(1)}, u32[]{:S(2)}, u32[]{:S(2)}) async-start(bf16[16,288,128]{2,1,0:T(8,128)(2,1)} %shard_map.91), calls=%async_computation.1 | async-start | bytes 2359296 | tf_op jit(solution)/shard_map/all_to_all | solution.py:277
  35.9 2.0 %collective-permute-start.3 = (bf16[64,2048]{1,0:T(8,128)(2,1)S(1)}, bf16[64,2048]{1,0:T(8,128)(2,1)S(1)}, u32[]{:S(2)}, u32[]{:S(2)}) collective-permute-start(bf16[64,2048]{1,0:T(8,128)(2,1)S(1)} %bitcast.67), channel_id=1, source_target_pairs={{0,8},{2,10},{4,12},{6,14},{8,16},{10,18},{12,20},{14,22},{16,24},... | collective-permute-start | bytes 786440 | tf_op jit(solution)/shard_map/ppermute | solution.py:233
  37.9 1.9 %collective-permute-start.4 = (bf16[64,2048]{1,0:T(8,128)(2,1)S(1)}, bf16[64,2048]{1,0:T(8,128)(2,1)S(1)}, u32[]{:S(2)}, u32[]{:S(2)}) collective-permute-start(bf16[64,2048]{1,0:T(8,128)(2,1)S(1)} %bitcast.68), channel_id=1, source_target_pairs={{0,24},{2,26},{4,28},{6,30},{8,0},{10,2},{12,4},{14,6},{16,8},{18,... | collective-permute-start | bytes 786440 | tf_op jit(solution)/shard_map/ppermute | solution.py:233
  39.8 1.9 %collective-permute-start.5 = (bf16[64,2048]{1,0:T(8,128)(2,1)S(1)}, bf16[64,2048]{1,0:T(8,128)(2,1)S(1)}, u32[]{:S(2)}, u32[]{:S(2)}) collective-permute-start(bf16[64,2048]{1,0:T(8,128)(2,1)S(1)} %collective-permute-done.refs_0_), channel_id=1, source_target_pairs={{0,2},{2,0},{4,6},{6,4},{8,10},{10,8},{12,14},{14,12},{16,18},{18,... | collective-permute-start | bytes 786440 | tf_op jit(solution)/shard_map/ppermute | solution.py:230
  41.7 1.5 collective-permute-start.6
  43.8 22.4 %collective-permute-done.3.refs_0_ = bf16[64,2048]{1,0:T(8,128)(2,1)S(1)} collective-permute-done((bf16[64,2048]{1,0:T(8,128)(2,1)S(1)}, bf16[64,2048]{1,0:T(8,128)(2,1)S(1)}, u32[]{:S(2)}, u32[]{:S(2)}) %collective-permute-start.3) | collective-permute-done | bytes 262176 | tf_op jit(solution)/shard_map/ppermute | solution.py:233
  66.1 2.4 %collective-permute-done.4.refs_0_ = bf16[64,2048]{1,0:T(8,128)(2,1)S(1)} collective-permute-done((bf16[64,2048]{1,0:T(8,128)(2,1)S(1)}, bf16[64,2048]{1,0:T(8,128)(2,1)S(1)}, u32[]{:S(2)}, u32[]{:S(2)}) %collective-permute-start.4) | collective-permute-done | bytes 262176 | tf_op jit(solution)/shard_map/ppermute | solution.py:233
  68.6 0.7 copy-done.16
  69.6 1.5 collective-permute-start.10
  71.0 1.7 collective-permute-start.12
  73.8 0.7 reshape_transpose_reshape.3.refs_4_
  74.5 1.5 collective-permute-start.13
  76.0 3.6 %shard_map.92.refs_5_ = bf16[3,192,2048]{2,1,0:T(8,128)(2,1)} custom-call(bf16[16,288,128]{2,1,0:T(8,128)(2,1)} %copy-done.1, bf16[16,288,128]{2,1,0:T(8,128)(2,1)} %copy-done.5), custom_call_target="tpu_custom_call" | custom-call | bytes 4718592 | tf_op jit(solution)/shard_map/pallas_call | solution.py:195
  79.6 11.2 %shard_map.93 = (bf16[2,64,2048]{2,1,0:T(8,128)(2,1)}, bf16[2,64,2048]{2,1,0:T(8,128)(2,1)}) custom-call(bf16[64,2048]{1,0:T(8,128)(2,1)} %bitcast.69, bf16[64,2048]{1,0:T(8,128)(2,1)} %copy-done.13, bf16[64,2048]{1,0:T(8,128)(2,1)} %copy-done.14, bf16[64,2048]{1,0:T(8,128)(2,1)} %collective-permute-done.7.refs_3_, ...), custom_call_target="tpu_custom_call" | custom-call | flops 5033164800 | bytes 19660800 | tf_op jit(solution)/shard_map/pallas_call | solution.py:119
  91.0 1.1 collective-permute-start.14
  92.1 1.7 collective-permute-start.15
  93.8 1.0 collective-permute-start.16
  94.8 11.2 %shard_map.94 = (bf16[2,64,2048]{2,1,0:T(8,128)(2,1)}, bf16[2,64,2048]{2,1,0:T(8,128)(2,1)}) custom-call(bf16[64,2048]{1,0:T(8,128)(2,1)} %copy-done.10, bf16[64,2048]{1,0:T(8,128)(2,1)} %copy-done.15, bf16[64,2048]{1,0:T(8,128)(2,1)} %copy-done.16, bf16[64,2048]{1,0:T(8,128)(2,1)} %collective-permute-done.13.refs_3_, ...), custom_call_target="tpu_custom_call" | custom-call | flops 5033164800 | bytes 19660800 | tf_op jit(solution)/shard_map/pallas_call | solution.py:119
  106.1 3.7 %collective-permute-done.16.refs_3_ = bf16[64,2048]{1,0:T(8,128)(2,1)S(1)} collective-permute-done((bf16[64,2048]{1,0:T(8,128)(2,1)}, bf16[64,2048]{1,0:T(8,128)(2,1)S(1)}, u32[]{:S(2)}, u32[]{:S(2)}) %collective-permute-start.16) | collective-permute-done | bytes 262176 | tf_op jit(solution)/shard_map/ppermute | solution.py:230
  109.8 1.7 collective-permute-start.18
  112.3 11.2 %shard_map.95 = (bf16[2,64,2048]{2,1,0:T(8,128)(2,1)}, bf16[2,64,2048]{2,1,0:T(8,128)(2,1)}) custom-call(bf16[64,2048]{1,0:T(8,128)(2,1)} %copy-done.12, bf16[64,2048]{1,0:T(8,128)(2,1)} %collective-permute-done.9.refs_1_, bf16[64,2048]{1,0:T(8,128)(2,1)} %collective-permute-done.11.refs_2_, bf16[64,2048]{1,0:T(8,128)(2,1)} %copy-done.18, ...), custom_call_target="tpu_custom_call" | custom-call | flops 5033164800 | bytes 19660800 | tf_op jit(solution)/shard_map/pallas_call | solution.py:119
  123.5 1.4 collective-permute-start.21
  125.0 1.3 collective-permute-start.19
  126.3 11.3 %shard_map.96 = (bf16[2,64,2048]{2,1,0:T(8,128)(2,1)}, bf16[2,64,2048]{2,1,0:T(8,128)(2,1)}) custom-call(bf16[64,2048]{1,0:T(8,128)(2,1)} %copy-done.11, bf16[64,2048]{1,0:T(8,128)(2,1)} %collective-permute-done.10.refs_1_, bf16[64,2048]{1,0:T(8,128)(2,1)} %collective-permute-done.12.refs_2_, bf16[64,2048]{1,0:T(8,128)(2,1)} %copy-done.17, ...), custom_call_target="tpu_custom_call" | custom-call | flops 5033164800 | bytes 19660800 | tf_op jit(solution)/shard_map/pallas_call | solution.py:119
  137.6 1.8 collective-permute-start.24
  139.4 1.8 collective-permute-done.19
  141.2 7.7 %collective-permute-start.20 = (bf16[64,2048]{1,0:T(8,128)(2,1)S(1)}, bf16[64,2048]{1,0:T(8,128)(2,1)S(1)}, u32[]{:S(2)}, u32[]{:S(2)}) collective-permute-start(bf16[64,2048]{1,0:T(8,128)(2,1)S(1)} %fusion.2), channel_id=1, source_target_pairs={{0,16},{2,18},{4,20},{6,22},{8,24},{10,26},{12,28},{14,30},{16,0},... | collective-permute-start | bytes 786440 | tf_op jit(solution)/shard_map/ppermute | solution.py:233
  149.0 1.2 collective-permute-start.22
  150.2 1.0 fusion.10
  151.3 1.7 collective-permute-start.25
  152.9 2.6 %collective-permute-done.22 = bf16[64,2048]{1,0:T(8,128)(2,1)S(1)} collective-permute-done((bf16[64,2048]{1,0:T(8,128)(2,1)S(1)}, bf16[64,2048]{1,0:T(8,128)(2,1)S(1)}, u32[]{:S(2)}, u32[]{:S(2)}) %collective-permute-start.22) | collective-permute-done | bytes 262176 | tf_op jit(solution)/shard_map/ppermute | solution.py:230
  155.6 2.9 %collective-permute-start.23 = (bf16[64,2048]{1,0:T(8,128)(2,1)S(1)}, bf16[64,2048]{1,0:T(8,128)(2,1)S(1)}, u32[]{:S(2)}, u32[]{:S(2)}) collective-permute-start(bf16[64,2048]{1,0:T(8,128)(2,1)S(1)} %fusion.1), channel_id=1, source_target_pairs={{0,24},{2,26},{4,28},{6,30},{8,0},{10,2},{12,4},{14,6},{16,8},{18,... | collective-permute-start | bytes 786440 | tf_op jit(solution)/shard_map/ppermute | solution.py:233
  158.6 8.6 %collective-permute-start.26 = (bf16[64,2048]{1,0:T(8,128)(2,1)S(1)}, bf16[64,2048]{1,0:T(8,128)(2,1)S(1)}, u32[]{:S(2)}, u32[]{:S(2)}) collective-permute-start(bf16[64,2048]{1,0:T(8,128)(2,1)S(1)} %fusion), channel_id=1, source_target_pairs={{0,8},{2,10},{4,12},{6,14},{8,16},{10,18},{12,20},{14,22},{16,24},... | collective-permute-start | bytes 786440 | tf_op jit(solution)/shard_map/ppermute | solution.py:233
  167.2 1.9 %collective-permute-done.23 = bf16[64,2048]{1,0:T(8,128)(2,1)S(1)} collective-permute-done((bf16[64,2048]{1,0:T(8,128)(2,1)S(1)}, bf16[64,2048]{1,0:T(8,128)(2,1)S(1)}, u32[]{:S(2)}, u32[]{:S(2)}) %collective-permute-start.23) | collective-permute-done | bytes 262176 | tf_op jit(solution)/shard_map/ppermute | solution.py:233
  169.1 2.8 %collective-permute-done.26 = bf16[64,2048]{1,0:T(8,128)(2,1)S(1)} collective-permute-done((bf16[64,2048]{1,0:T(8,128)(2,1)S(1)}, bf16[64,2048]{1,0:T(8,128)(2,1)S(1)}, u32[]{:S(2)}, u32[]{:S(2)}) %collective-permute-start.26) | collective-permute-done | bytes 262176 | tf_op jit(solution)/shard_map/ppermute | solution.py:233
  172.0 1.2 fusion.6
  173.2 3.9 %all_to_all.44 = bf16[64,2,1024]{2,0,1:T(8,128)(2,1)S(1)} all-to-all(bf16[64,2,1024]{2,0,1:T(8,128)(2,1)S(1)} %bitcast.71), channel_id=1, replica_groups=mesh['wide'=16,'narrow'=2] {'narrow'}, dimensions={1} | all-to-all | bytes 524288 | tf_op jit(solution)/shard_map/all_to_all | solution.py:335
  177.2 0.7 copy.22
  (90 shorter events, 3.5 us)
Async XLA Ops:
  6.5 13.3 %copy-start = (f32[128,6]{0,1:T(8,128)S(1)}, f32[128,6]{0,1:T(8,128)}, u32[]{:S(2)}) copy-start(f32[128,6]{0,1:T(8,128)} %param.11) | copy-start | bytes 9220
  6.5 73.0 %all-gather.7.cloned.1.call-start = ((), (), s32[]{:S(2)}) async-start(), calls=%async_computation.3 | async-start | bytes 8650752 | tf_op jit(solution)/shard_map/all_gather | solution.py:262
  7.3 1.5 copy-start.19
  7.3 12.7 %copy-start.20 = (s32[128,6]{0,1:T(8,128)S(1)}, s32[128,6]{0,1:T(8,128)}, u32[]{:S(2)}) copy-start(s32[128,6]{0,1:T(8,128)} %param.10) | copy-start | bytes 9220
  7.3 72.3 %all-gather.9.cloned.1.call-start = ((), (), s32[]{:S(2)}) async-start(), calls=%async_computation.4 | async-start | bytes 8650752 | tf_op jit(solution)/shard_map/all_gather | solution.py:262
  8.0 71.6 %all-gather.11.cloned.1.call-start = ((), (), s32[]{:S(2)}) async-start(), calls=%async_computation.5 | async-start | bytes 8650752 | tf_op jit(solution)/shard_map/all_gather | solution.py:262
  12.7 66.8 %copy-start.8 = (bf16[2,8,8,1024]{3,2,0,1:T(8,128)(2,1)}, bf16[2,8,8,1024]{3,2,0,1:T(8,128)(2,1)S(1)}, u32[]{:S(2)}) copy-start(bf16[2,8,8,1024]{3,2,0,1:T(8,128)(2,1)S(1)} %copy.17) | copy-start | bytes 786436
  12.7 16.3 %collective-permute-start = (bf16[64,2048]{1,0:T(8,128)(2,1)S(1)}, bf16[64,2048]{1,0:T(8,128)(2,1)S(1)}, u32[]{:S(2)}, u32[]{:S(2)}) collective-permute-start(bf16[64,2048]{1,0:T(8,128)(2,1)S(1)} %bitcast.64), channel_id=1, source_target_pairs={{0,16},{2,18},{4,20},{6,22},{8,24},{10,26},{12,28},{14,30},{16,0},... | collective-permute-start | bytes 786440 | tf_op jit(solution)/shard_map/ppermute | solution.py:233
  16.9 12.2 %collective-permute-start.1 = (bf16[64,2048]{1,0:T(8,128)(2,1)S(1)}, bf16[64,2048]{1,0:T(8,128)(2,1)S(1)}, u32[]{:S(2)}, u32[]{:S(2)}) collective-permute-start(bf16[64,2048]{1,0:T(8,128)(2,1)S(1)} %bitcast.65), channel_id=1, source_target_pairs={{0,2},{2,0},{4,6},{6,4},{8,10},{10,8},{12,14},{14,12},{16,18},{18,... | collective-permute-start | bytes 786440 | tf_op jit(solution)/shard_map/ppermute | solution.py:230
  18.3 10.8 %collective-permute-start.2 = (bf16[64,2048]{1,0:T(8,128)(2,1)S(1)}, bf16[64,2048]{1,0:T(8,128)(2,1)S(1)}, u32[]{:S(2)}, u32[]{:S(2)}) collective-permute-start(bf16[64,2048]{1,0:T(8,128)(2,1)S(1)} %bitcast.66), channel_id=1, source_target_pairs={{0,4},{2,6},{4,0},{6,2},{8,12},{10,14},{12,8},{14,10},{16,20},{18,... | collective-permute-start | bytes 786440 | tf_op jit(solution)/shard_map/ppermute | solution.py:230
  29.1 50.5 %copy-start.10 = (bf16[64,2048]{1,0:T(8,128)(2,1)}, bf16[64,2048]{1,0:T(8,128)(2,1)S(1)}, u32[]{:S(2)}) copy-start(bf16[64,2048]{1,0:T(8,128)(2,1)S(1)} %collective-permute-done.refs_0_) | copy-start | bytes 786436
  29.1 40.3 %copy-start.13 = (bf16[64,2048]{1,0:T(8,128)(2,1)}, bf16[64,2048]{1,0:T(8,128)(2,1)S(1)}, u32[]{:S(2)}) copy-start(bf16[64,2048]{1,0:T(8,128)(2,1)S(1)} %collective-permute-done.1.refs_1_) | copy-start | bytes 786436
  29.1 6.8 %copy-start.14 = (bf16[64,2048]{1,0:T(8,128)(2,1)}, bf16[64,2048]{1,0:T(8,128)(2,1)S(1)}, u32[]{:S(2)}) copy-start(bf16[64,2048]{1,0:T(8,128)(2,1)S(1)} %collective-permute-done.2.refs_2_) | copy-start | bytes 786436
  29.1 40.3 %all-to-all-start.1 = ((bf16[16,288,128]{2,1,0:T(8,128)(2,1)}), bf16[16,288,128]{2,1,0:T(8,128)(2,1)S(1)}, u32[]{:S(2)}, u32[]{:S(2)}) async-start(bf16[16,288,128]{2,1,0:T(8,128)(2,1)} %shard_map.91), calls=%async_computation.1 | async-start | bytes 2359296 | tf_op jit(solution)/shard_map/all_to_all | solution.py:277
  35.9 30.2 %collective-permute-start.3 = (bf16[64,2048]{1,0:T(8,128)(2,1)S(1)}, bf16[64,2048]{1,0:T(8,128)(2,1)S(1)}, u32[]{:S(2)}, u32[]{:S(2)}) collective-permute-start(bf16[64,2048]{1,0:T(8,128)(2,1)S(1)} %bitcast.67), channel_id=1, source_target_pairs={{0,8},{2,10},{4,12},{6,14},{8,16},{10,18},{12,20},{14,22},{16,24},... | collective-permute-start | bytes 786440 | tf_op jit(solution)/shard_map/ppermute | solution.py:233
  37.9 30.7 %collective-permute-start.4 = (bf16[64,2048]{1,0:T(8,128)(2,1)S(1)}, bf16[64,2048]{1,0:T(8,128)(2,1)S(1)}, u32[]{:S(2)}, u32[]{:S(2)}) collective-permute-start(bf16[64,2048]{1,0:T(8,128)(2,1)S(1)} %bitcast.68), channel_id=1, source_target_pairs={{0,24},{2,26},{4,28},{6,30},{8,0},{10,2},{12,4},{14,6},{16,8},{18,... | collective-permute-start | bytes 786440 | tf_op jit(solution)/shard_map/ppermute | solution.py:233
  39.8 28.8 %collective-permute-start.5 = (bf16[64,2048]{1,0:T(8,128)(2,1)S(1)}, bf16[64,2048]{1,0:T(8,128)(2,1)S(1)}, u32[]{:S(2)}, u32[]{:S(2)}) collective-permute-start(bf16[64,2048]{1,0:T(8,128)(2,1)S(1)} %collective-permute-done.refs_0_), channel_id=1, source_target_pairs={{0,2},{2,0},{4,6},{6,4},{8,10},{10,8},{12,14},{14,12},{16,18},{18,... | collective-permute-start | bytes 786440 | tf_op jit(solution)/shard_map/ppermute | solution.py:230
  41.7 26.9 %collective-permute-start.6 = (bf16[64,2048]{1,0:T(8,128)(2,1)S(1)}, bf16[64,2048]{1,0:T(8,128)(2,1)S(1)}, u32[]{:S(2)}, u32[]{:S(2)}) collective-permute-start(bf16[64,2048]{1,0:T(8,128)(2,1)S(1)} %collective-permute-done.refs_0_), channel_id=1, source_target_pairs={{0,4},{2,6},{4,0},{6,2},{8,12},{10,14},{12,8},{14,10},{16,20},{18,... | collective-permute-start | bytes 786440 | tf_op jit(solution)/shard_map/ppermute | solution.py:230
  43.2 26.1 %collective-permute-start.7 = (bf16[64,2048]{1,0:T(8,128)(2,1)S(1)}, bf16[64,2048]{1,0:T(8,128)(2,1)}, u32[]{:S(2)}, u32[]{:S(2)}) collective-permute-start(bf16[64,2048]{1,0:T(8,128)(2,1)S(1)} %collective-permute-done.1.refs_1_), channel_id=1, source_target_pairs={{0,4},{2,6},{4,0},{6,2},{8,12},{10,14},{12,8},{14,10},{16,20},{18,... | collective-permute-start | bytes 786440 | tf_op jit(solution)/shard_map/ppermute | solution.py:230
  66.1 24.8 %copy-start.12 = (bf16[64,2048]{1,0:T(8,128)(2,1)}, bf16[64,2048]{1,0:T(8,128)(2,1)S(1)}, u32[]{:S(2)}) copy-start(bf16[64,2048]{1,0:T(8,128)(2,1)S(1)} %collective-permute-done.3.refs_0_) | copy-start | bytes 786436
  68.6 22.3 %copy-start.11 = (bf16[64,2048]{1,0:T(8,128)(2,1)}, bf16[64,2048]{1,0:T(8,128)(2,1)S(1)}, u32[]{:S(2)}) copy-start(bf16[64,2048]{1,0:T(8,128)(2,1)S(1)} %collective-permute-done.4.refs_0_) | copy-start | bytes 786436
  69.4 6.6 %copy-start.1 = (bf16[16,288,128]{2,1,0:T(8,128)(2,1)}, bf16[16,288,128]{2,1,0:T(8,128)(2,1)S(1)}, u32[]{:S(2)}) copy-start(bf16[16,288,128]{2,1,0:T(8,128)(2,1)S(1)} %all-to-all-done.1.refs_0_) | copy-start | bytes 3538948
  69.4 5.1 %collective-permute-start.8 = (bf16[16,288,128]{2,1,0:T(8,128)(2,1)S(1)}, bf16[16,288,128]{2,1,0:T(8,128)(2,1)S(1)}, u32[]{:S(2)}, u32[]{:S(2)}) collective-permute-start(bf16[16,288,128]{2,1,0:T(8,128)(2,1)S(1)} %all-to-all-done.1.refs_0_), channel_id=1, source_target_pairs={{0,1},{1,0},{2,3},{3,2},{4,5},{5,4},{6,7},{7,6},{8,9},{9,8},{10,11... | collective-permute-start | bytes 3538952 | tf_op jit(solution)/shard_map/ppermute | solution.py:238
  69.6 21.3 %collective-permute-start.10 = (bf16[64,2048]{1,0:T(8,128)(2,1)S(1)}, bf16[64,2048]{1,0:T(8,128)(2,1)}, u32[]{:S(2)}, u32[]{:S(2)}) collective-permute-start(bf16[64,2048]{1,0:T(8,128)(2,1)S(1)} %collective-permute-done.4.refs_0_), channel_id=1, source_target_pairs={{0,2},{2,0},{4,6},{6,4},{8,10},{10,8},{12,14},{14,12},{16,18},{18,... | collective-permute-start | bytes 786440 | tf_op jit(solution)/shard_map/ppermute | solution.py:230
  71.0 19.9 %collective-permute-start.12 = (bf16[64,2048]{1,0:T(8,128)(2,1)S(1)}, bf16[64,2048]{1,0:T(8,128)(2,1)}, u32[]{:S(2)}, u32[]{:S(2)}) collective-permute-start(bf16[64,2048]{1,0:T(8,128)(2,1)S(1)} %collective-permute-done.4.refs_0_), channel_id=1, source_target_pairs={{0,4},{2,6},{4,0},{6,2},{8,12},{10,14},{12,8},{14,10},{16,20},{18,... | collective-permute-start | bytes 786440 | tf_op jit(solution)/shard_map/ppermute | solution.py:230
  72.8 18.1 %collective-permute-start.11 = (bf16[64,2048]{1,0:T(8,128)(2,1)S(1)}, bf16[64,2048]{1,0:T(8,128)(2,1)}, u32[]{:S(2)}, u32[]{:S(2)}) collective-permute-start(bf16[64,2048]{1,0:T(8,128)(2,1)S(1)} %collective-permute-done.3.refs_0_), channel_id=1, source_target_pairs={{0,4},{2,6},{4,0},{6,2},{8,12},{10,14},{12,8},{14,10},{16,20},{18,... | collective-permute-start | bytes 786440 | tf_op jit(solution)/shard_map/ppermute | solution.py:230
  73.1 17.9 %collective-permute-start.9 = (bf16[64,2048]{1,0:T(8,128)(2,1)S(1)}, bf16[64,2048]{1,0:T(8,128)(2,1)}, u32[]{:S(2)}, u32[]{:S(2)}) collective-permute-start(bf16[64,2048]{1,0:T(8,128)(2,1)S(1)} %collective-permute-done.3.refs_0_), channel_id=1, source_target_pairs={{0,2},{2,0},{4,6},{6,4},{8,10},{10,8},{12,14},{14,12},{16,18},{18,... | collective-permute-start | bytes 786440 | tf_op jit(solution)/shard_map/ppermute | solution.py:230
  74.5 1.5 copy-start.5
  74.5 16.4 %collective-permute-start.13 = (bf16[64,2048]{1,0:T(8,128)(2,1)}, bf16[64,2048]{1,0:T(8,128)(2,1)}, u32[]{:S(2)}, u32[]{:S(2)}) collective-permute-start(bf16[64,2048]{1,0:T(8,128)(2,1)} %copy-done.16), channel_id=1, source_target_pairs={{0,2},{2,0},{4,6},{6,4},{8,10},{10,8},{12,14},{14,12},{16,18},{18,... | collective-permute-start | bytes 786440 | tf_op jit(solution)/shard_map/ppermute | solution.py:230
  91.0 20.5 %copy-start.2 = (bf16[2,64,2048]{2,1,0:T(8,128)(2,1)S(1)}, bf16[2,64,2048]{2,1,0:T(8,128)(2,1)}, u32[]{:S(2)}) copy-start(bf16[2,64,2048]{2,1,0:T(8,128)(2,1)} %get-tuple-element.65.refs_9_) | copy-start | bytes 1572868
  91.0 20.5 %collective-permute-start.14 = (bf16[2,64,2048]{2,1,0:T(8,128)(2,1)}, bf16[2,64,2048]{2,1,0:T(8,128)(2,1)S(1)}, u32[]{:S(2)}, u32[]{:S(2)}) collective-permute-start(bf16[2,64,2048]{2,1,0:T(8,128)(2,1)} %get-tuple-element.66), channel_id=1, source_target_pairs={{0,2},{2,0},{4,6},{6,4},{8,10},{10,8},{12,14},{14,12},{16,18},{18,... | collective-permute-start | bytes 1572872 | tf_op jit(solution)/shard_map/ppermute | solution.py:230
  92.1 14.0 %collective-permute-start.15 = (bf16[64,2048]{1,0:T(8,128)(2,1)}, bf16[64,2048]{1,0:T(8,128)(2,1)S(1)}, u32[]{:S(2)}, u32[]{:S(2)}) collective-permute-start(bf16[64,2048]{1,0:T(8,128)(2,1)} %collective-permute-done.9.refs_1_), channel_id=1, source_target_pairs={{0,4},{2,6},{4,0},{6,2},{8,12},{10,14},{12,8},{14,10},{16,20},{18,... | collective-permute-start | bytes 786440 | tf_op jit(solution)/shard_map/ppermute | solution.py:230
  93.8 16.0 %collective-permute-start.16 = (bf16[64,2048]{1,0:T(8,128)(2,1)}, bf16[64,2048]{1,0:T(8,128)(2,1)S(1)}, u32[]{:S(2)}, u32[]{:S(2)}) collective-permute-start(bf16[64,2048]{1,0:T(8,128)(2,1)} %collective-permute-done.12.refs_2_), channel_id=1, source_target_pairs={{0,2},{2,0},{4,6},{6,4},{8,10},{10,8},{12,14},{14,12},{16,18},{18,... | collective-permute-start | bytes 786440 | tf_op jit(solution)/shard_map/ppermute | solution.py:230
  106.1 5.9 %copy-start.18 = (bf16[64,2048]{1,0:T(8,128)(2,1)}, bf16[64,2048]{1,0:T(8,128)(2,1)S(1)}, u32[]{:S(2)}) copy-start(bf16[64,2048]{1,0:T(8,128)(2,1)S(1)} %collective-permute-done.15.refs_3_) | copy-start | bytes 786436
  109.8 13.7 %copy-start.17 = (bf16[64,2048]{1,0:T(8,128)(2,1)}, bf16[64,2048]{1,0:T(8,128)(2,1)S(1)}, u32[]{:S(2)}) copy-start(bf16[64,2048]{1,0:T(8,128)(2,1)S(1)} %collective-permute-done.16.refs_3_) | copy-start | bytes 786436
  109.8 15.1 %collective-permute-start.18 = (bf16[2,64,2048]{2,1,0:T(8,128)(2,1)}, bf16[2,64,2048]{2,1,0:T(8,128)(2,1)S(1)}, u32[]{:S(2)}, u32[]{:S(2)}) collective-permute-start(bf16[2,64,2048]{2,1,0:T(8,128)(2,1)} %get-tuple-element.78), channel_id=1, source_target_pairs={{0,4},{2,6},{4,0},{6,2},{8,12},{10,14},{12,8},{14,10},{16,20},{18,... | collective-permute-start | bytes 1572872 | tf_op jit(solution)/shard_map/ppermute | solution.py:230
  111.6 13.3 %copy-start.4 = (bf16[2,64,2048]{2,1,0:T(8,128)(2,1)S(1)}, bf16[2,64,2048]{2,1,0:T(8,128)(2,1)}, u32[]{:S(2)}) copy-start(bf16[2,64,2048]{2,1,0:T(8,128)(2,1)} %get-tuple-element.77.refs_9_) | copy-start | bytes 1572868
  111.6 55.6 %collective-permute-start.17 = (bf16[64,2048]{1,0:T(8,128)(2,1)S(1)}, bf16[64,2048]{1,0:T(8,128)(2,1)}, u32[]{:S(2)}, u32[]{:S(2)}) collective-permute-start(bf16[64,2048]{1,0:T(8,128)(2,1)S(1)} %fusion.7.refs_10_), channel_id=1, source_target_pairs={{0,4},{2,6},{4,0},{6,2},{8,12},{10,14},{12,8},{14,10},{16,20},{18,... | collective-permute-start | bytes 786440 | tf_op jit(solution)/shard_map/ppermute | solution.py:230
  123.5 25.4 %collective-permute-start.21 = (bf16[2,64,2048]{2,1,0:T(8,128)(2,1)}, bf16[2,64,2048]{2,1,0:T(8,128)(2,1)S(1)}, u32[]{:S(2)}, u32[]{:S(2)}) collective-permute-start(bf16[2,64,2048]{2,1,0:T(8,128)(2,1)} %get-tuple-element.84), channel_id=1, source_target_pairs={{0,2},{2,0},{4,6},{6,4},{8,10},{10,8},{12,14},{14,12},{16,18},{18,... | collective-permute-start | bytes 1572872 | tf_op jit(solution)/shard_map/ppermute | solution.py:230
  125.0 24.0 %copy-start.3 = (bf16[2,64,2048]{2,1,0:T(8,128)(2,1)S(1)}, bf16[2,64,2048]{2,1,0:T(8,128)(2,1)}, u32[]{:S(2)}) copy-start(bf16[2,64,2048]{2,1,0:T(8,128)(2,1)} %get-tuple-element.83.refs_9_) | copy-start | bytes 1572868
  125.0 16.1 %collective-permute-start.19 = (bf16[64,2048]{1,0:T(8,128)(2,1)S(1)}, bf16[64,2048]{1,0:T(8,128)(2,1)S(1)}, u32[]{:S(2)}, u32[]{:S(2)}) collective-permute-start(bf16[64,2048]{1,0:T(8,128)(2,1)S(1)} %fusion.8.refs_10_), channel_id=1, source_target_pairs={{0,2},{2,0},{4,6},{6,4},{8,10},{10,8},{12,14},{14,12},{16,18},{18,... | collective-permute-start | bytes 786440 | tf_op jit(solution)/shard_map/ppermute | solution.py:230
  137.6 20.9 %copy-start.9 = (bf16[2,64,2048]{2,1,0:T(8,128)(2,1)S(1)}, bf16[2,64,2048]{2,1,0:T(8,128)(2,1)}, u32[]{:S(2)}) copy-start(bf16[2,64,2048]{2,1,0:T(8,128)(2,1)} %get-tuple-element.91) | copy-start | bytes 1572868
  137.6 12.6 %collective-permute-start.24 = (bf16[2,64,2048]{2,1,0:T(8,128)(2,1)}, bf16[2,64,2048]{2,1,0:T(8,128)(2,1)S(1)}, u32[]{:S(2)}, u32[]{:S(2)}) collective-permute-start(bf16[2,64,2048]{2,1,0:T(8,128)(2,1)} %get-tuple-element.89), channel_id=1, source_target_pairs={{0,4},{2,6},{4,0},{6,2},{8,12},{10,14},{12,8},{14,10},{16,20},{18,... | collective-permute-start | bytes 1572872 | tf_op jit(solution)/shard_map/ppermute | solution.py:230
  141.2 26.0 %collective-permute-start.20 = (bf16[64,2048]{1,0:T(8,128)(2,1)S(1)}, bf16[64,2048]{1,0:T(8,128)(2,1)S(1)}, u32[]{:S(2)}, u32[]{:S(2)}) collective-permute-start(bf16[64,2048]{1,0:T(8,128)(2,1)S(1)} %fusion.2), channel_id=1, source_target_pairs={{0,16},{2,18},{4,20},{6,22},{8,24},{10,26},{12,28},{14,30},{16,0},... | collective-permute-start | bytes 786440 | tf_op jit(solution)/shard_map/ppermute | solution.py:233
  149.0 6.4 %collective-permute-start.22 = (bf16[64,2048]{1,0:T(8,128)(2,1)S(1)}, bf16[64,2048]{1,0:T(8,128)(2,1)S(1)}, u32[]{:S(2)}, u32[]{:S(2)}) collective-permute-start(bf16[64,2048]{1,0:T(8,128)(2,1)S(1)} %fusion.9), channel_id=1, source_target_pairs={{0,4},{2,6},{4,0},{6,2},{8,12},{10,14},{12,8},{14,10},{16,20},{18,... | collective-permute-start | bytes 786440 | tf_op jit(solution)/shard_map/ppermute | solution.py:230
  151.3 7.2 %collective-permute-start.25 = (bf16[64,2048]{1,0:T(8,128)(2,1)S(1)}, bf16[64,2048]{1,0:T(8,128)(2,1)S(1)}, u32[]{:S(2)}, u32[]{:S(2)}) collective-permute-start(bf16[64,2048]{1,0:T(8,128)(2,1)S(1)} %fusion.10), channel_id=1, source_target_pairs={{0,2},{2,0},{4,6},{6,4},{8,10},{10,8},{12,14},{14,12},{16,18},{18,... | collective-permute-start | bytes 786440 | tf_op jit(solution)/shard_map/ppermute | solution.py:230
  155.6 13.6 %collective-permute-start.23 = (bf16[64,2048]{1,0:T(8,128)(2,1)S(1)}, bf16[64,2048]{1,0:T(8,128)(2,1)S(1)}, u32[]{:S(2)}, u32[]{:S(2)}) collective-permute-start(bf16[64,2048]{1,0:T(8,128)(2,1)S(1)} %fusion.1), channel_id=1, source_target_pairs={{0,24},{2,26},{4,28},{6,30},{8,0},{10,2},{12,4},{14,6},{16,8},{18,... | collective-permute-start | bytes 786440 | tf_op jit(solution)/shard_map/ppermute | solution.py:233
  158.6 13.4 %collective-permute-start.26 = (bf16[64,2048]{1,0:T(8,128)(2,1)S(1)}, bf16[64,2048]{1,0:T(8,128)(2,1)S(1)}, u32[]{:S(2)}, u32[]{:S(2)}) collective-permute-start(bf16[64,2048]{1,0:T(8,128)(2,1)S(1)} %fusion), channel_id=1, source_target_pairs={{0,8},{2,10},{4,12},{6,14},{8,16},{10,18},{12,20},{14,22},{16,24},... | collective-permute-start | bytes 786440 | tf_op jit(solution)/shard_map/ppermute | solution.py:233
  (4 other events, 3.6 us)
Sparse Core Ops, SparseCore 0:
  8.9 18.6 all-gather.6
  29.2 17.1 all-gather.8
  47.9 17.1 all-gather.10

commit v4 on v1

--- a/solution.py
+++ b/solution.py
@@ -9,7 +9,7 @@
 PLANE = 4
 TILE = 256
 OUT_TILE = 512
-VMEM_BYTES = 60 * 1024 * 1024
+VMEM_BYTES = 44 * 1024 * 1024
 
 
 def dot_t(rows, weight):

time: 182 us -> 181 us (level)
  local copies, waits for them, and re-layouts: 3.99 us -> 19.8 us
  Pallas kernels: 51.1 us -> 37.3 us
  waiting for transfers between devices: 57.3 us -> 54.7 us
    unnamed x50 -> x80, local copies, waits for them, and re-layouts: 2.45 us -> 18.9 us
    pallas_call x4, Pallas kernels: 45 us -> 35.4 us  [layer(): pl.pallas_call(functools.partial(layer_kernel, (experts, plane, x_first,...]
    pallas_call x1, Pallas kernels: 3.6 us -> 0.55 us  [lay_out(): pl.pallas_call(functools.partial(lay_out_kernel, units), out_shape=jax.Sh...]
  transfers between devices with their start and end apart: 31 -> 31, of which waited for: 16 -> 16; matrix products, arithmetic and copies ran while one was open for 2% -> 1% of each run, Pallas kernels for 22% -> 16%
where the time goes in v4:
time: 181 us; the launch traced here: 180 us
  waiting for transfers between devices  54.7 us (30%)
  starting transfers between devices  44.6 us (25%)
  Pallas kernels  37.3 us (21%)
  local copies, waits for them, and re-layouts  19.8 us (11%)
  between operations  13.4 us (7%)
  blocking collectives  9.06 us (5%)
    ppermute x20, waiting for transfers between devices, flip(): return lax.ppermute(value, 'wide', [(w, w ^ bits) for w in range(wide)])  40.8 us
    pallas_call x4, Pallas kernels, layer(): pl.pallas_call(functools.partial(layer_kernel, (experts, plane, x_first,...  35.4 us
    ppermute x20, starting transfers between devices, flip(): return lax.ppermute(value, 'wide', [(w, w ^ bits) for w in range(wide)])  27.3 us
    unnamed x80, local copies, waits for them, and re-layouts  18.9 us
    ppermute x6, starting transfers between devices, shift(): lax.ppermute(value, 'wide', [(w, (w + PLANE * by) % wide) for w in range(...  11.9 us
    ppermute x6, waiting for transfers between devices, shift(): lax.ppermute(value, 'wide', [(w, (w + PLANE * by) % wide) for w in range(...  9.98 us
    all_to_all x1, starting transfers between devices, body(): lax.all_to_all(stacked, 'wide', split_axis=0, concat_axis=0, tiled=True)  5.27 us
    all_to_all x1, blocking collectives, body(): lax.all_to_all(tokens, 'narrow', split_axis=0, concat_axis=1, tiled=True)  5.11 us
  transfers between devices with their start and end apart: 31, of which 16 were waited for; matrix products, arithmetic and copies ran while one was open for 1% of the time, Pallas kernels for 16%

profile of v4, /device:TPU:0, one launch (start us, length us, event | category | flops | bytes accessed | tf_op | source)
XLA Modules:
  0.0 180.0 jit_solution(16034300457017558829)
XLA Ops:
  6.5 5.1 %all_to_all.43 = bf16[2,64,1024]{2,1,0:T(8,128)(2,1)S(1)} all-to-all(bf16[2,64,1024]{2,1,0:T(8,128)(2,1)} %bitcast.71), channel_id=1, replica_groups=mesh['wide'=16,'narrow'=2] {'narrow'}, dimensions={0} | all-to-all | bytes 524288 | tf_op jit(solution)/shard_map/all_to_all | solution.py:240
  11.7 3.1 %collective-permute-start = (bf16[64,2048]{1,0:T(8,128)(2,1)S(1)}, bf16[64,2048]{1,0:T(8,128)(2,1)S(1)}, u32[]{:S(2)}, u32[]{:S(2)}) collective-permute-start(bf16[64,2048]{1,0:T(8,128)(2,1)S(1)} %bitcast.52), channel_id=1, source_target_pairs={{0,8},{2,10},{4,12},{6,14},{8,16},{10,18},{12,20},{14,22},{16,24},... | collective-permute-start | bytes 786440 | tf_op jit(solution)/shard_map/ppermute | solution.py:233
  14.8 2.1 %collective-permute-start.1 = (bf16[64,2048]{1,0:T(8,128)(2,1)S(1)}, bf16[64,2048]{1,0:T(8,128)(2,1)S(1)}, u32[]{:S(2)}, u32[]{:S(2)}) collective-permute-start(bf16[64,2048]{1,0:T(8,128)(2,1)S(1)} %bitcast.53), channel_id=1, source_target_pairs={{0,24},{2,26},{4,28},{6,30},{8,0},{10,2},{12,4},{14,6},{16,8},{18,... | collective-permute-start | bytes 786440 | tf_op jit(solution)/shard_map/ppermute | solution.py:233
  16.9 1.6 collective-permute-start.2
  18.5 1.5 collective-permute-start.3
  21.0 1.0 copy-done.6
  22.0 1.0 copy-done.7
  22.9 1.0 copy-done.8
  23.9 1.3 shard_map.91
  25.2 3.3 %collective-permute-done.1.refs_0_ = bf16[64,2048]{1,0:T(8,128)(2,1)S(1)} collective-permute-done((bf16[64,2048]{1,0:T(8,128)(2,1)S(1)}, bf16[64,2048]{1,0:T(8,128)(2,1)S(1)}, u32[]{:S(2)}, u32[]{:S(2)}) %collective-permute-start.1) | collective-permute-done | bytes 262176 | tf_op jit(solution)/shard_map/ppermute | solution.py:233
  30.0 1.6 collective-permute-start.5
  31.6 1.5 collective-permute-start.7
  34.1 1.3 collective-permute-start.4
  35.4 3.9 %collective-permute-done.5.refs_1_ = bf16[64,2048]{1,0:T(8,128)(2,1)S(1)} collective-permute-done((bf16[64,2048]{1,0:T(8,128)(2,1)S(1)}, bf16[64,2048]{1,0:T(8,128)(2,1)S(1)}, u32[]{:S(2)}, u32[]{:S(2)}) %collective-permute-start.5) | collective-permute-done | bytes 262176 | tf_op jit(solution)/shard_map/ppermute | solution.py:230
  40.0 3.3 %collective-permute-done.6.refs_1_ = bf16[64,2048]{1,0:T(8,128)(2,1)S(1)} collective-permute-done((bf16[64,2048]{1,0:T(8,128)(2,1)S(1)}, bf16[64,2048]{1,0:T(8,128)(2,1)S(1)}, u32[]{:S(2)}, u32[]{:S(2)}) %collective-permute-start.6) | collective-permute-done | bytes 262176 | tf_op jit(solution)/shard_map/ppermute | solution.py:230
  43.3 1.2 collective-permute-done.8.refs_2_
  45.3 1.9 %collective-permute-done.4.refs_0_ = bf16[64,2048]{1,0:T(8,128)(2,1)S(1)} collective-permute-done((bf16[64,2048]{1,0:T(8,128)(2,1)S(1)}, bf16[64,2048]{1,0:T(8,128)(2,1)S(1)}, u32[]{:S(2)}, u32[]{:S(2)}) %collective-permute-start.4) | collective-permute-done | bytes 262176 | tf_op jit(solution)/shard_map/ppermute | solution.py:233
  47.2 5.3 %all-to-all-start.1 = ((bf16[16,288,128]{2,1,0:T(8,128)(2,1)}), bf16[16,288,128]{2,1,0:T(8,128)(2,1)S(1)}, u32[]{:S(2)}, u32[]{:S(2)}) async-start(bf16[16,288,128]{2,1,0:T(8,128)(2,1)} %shard_map.91), calls=%async_computation.1 | async-start | bytes 2359296 | tf_op jit(solution)/shard_map/all_to_all | solution.py:281
  52.5 1.9 %collective-permute-start.11 = (bf16[64,2048]{1,0:T(8,128)(2,1)S(1)}, bf16[64,2048]{1,0:T(8,128)(2,1)S(1)}, u32[]{:S(2)}, u32[]{:S(2)}) collective-permute-start(bf16[64,2048]{1,0:T(8,128)(2,1)S(1)} %collective-permute-done.4.refs_0_), channel_id=1, source_target_pairs={{0,2},{2,0},{4,6},{6,4},{8,10},{10,8},{12,14},{14,12},{16,18},{18,... | collective-permute-start | bytes 786440 | tf_op jit(solution)/shard_map/ppermute | solution.py:230
  54.4 1.5 collective-permute-start.12
  57.3 1.9 %collective-permute-start.9 = (bf16[64,2048]{1,0:T(8,128)(2,1)S(1)}, bf16[64,2048]{1,0:T(8,128)(2,1)S(1)}, u32[]{:S(2)}, u32[]{:S(2)}) collective-permute-start(bf16[64,2048]{1,0:T(8,128)(2,1)S(1)} %collective-permute-done.3.refs_2_), channel_id=1, source_target_pairs={{0,2},{2,0},{4,6},{6,4},{8,10},{10,8},{12,14},{14,12},{16,18},{18,... | collective-permute-start | bytes 786440 | tf_op jit(solution)/shard_map/ppermute | solution.py:230
  59.1 8.1 %collective-permute-done.11.refs_1_ = bf16[64,2048]{1,0:T(8,128)(2,1)S(1)} collective-permute-done((bf16[64,2048]{1,0:T(8,128)(2,1)S(1)}, bf16[64,2048]{1,0:T(8,128)(2,1)S(1)}, u32[]{:S(2)}, u32[]{:S(2)}) %collective-permute-start.11) | collective-permute-done | bytes 262176 | tf_op jit(solution)/shard_map/ppermute | solution.py:230
  67.2 5.5 %collective-permute-start.13 = (bf16[64,2048]{1,0:T(8,128)(2,1)S(1)}, bf16[64,2048]{1,0:T(8,128)(2,1)S(1)}, u32[]{:S(2)}, u32[]{:S(2)}) collective-permute-start(bf16[64,2048]{1,0:T(8,128)(2,1)S(1)} %collective-permute-done.11.refs_1_), channel_id=1, source_target_pairs={{0,4},{2,6},{4,0},{6,2},{8,12},{10,14},{12,8},{14,10},{16,20},{18,... | collective-permute-start | bytes 786440 | tf_op jit(solution)/shard_map/ppermute | solution.py:230
  73.4 6.6 %collective-permute-done.10.refs_3_ = bf16[64,2048]{1,0:T(8,128)(2,1)S(1)} collective-permute-done((bf16[64,2048]{1,0:T(8,128)(2,1)S(1)}, bf16[64,2048]{1,0:T(8,128)(2,1)S(1)}, u32[]{:S(2)}, u32[]{:S(2)}) %collective-permute-start.10) | collective-permute-done | bytes 262176 | tf_op jit(solution)/shard_map/ppermute | solution.py:230
  82.2 2.2 %collective-permute-done.9.refs_3_ = bf16[64,2048]{1,0:T(8,128)(2,1)S(1)} collective-permute-done((bf16[64,2048]{1,0:T(8,128)(2,1)S(1)}, bf16[64,2048]{1,0:T(8,128)(2,1)S(1)}, u32[]{:S(2)}, u32[]{:S(2)}) %collective-permute-start.9) | collective-permute-done | bytes 262176 | tf_op jit(solution)/shard_map/ppermute | solution.py:230
  86.2 2.5 %collective-permute-done.15.refs_1_ = bf16[16,288,128]{2,1,0:T(8,128)(2,1)S(1)} collective-permute-done((bf16[16,288,128]{2,1,0:T(8,128)(2,1)S(1)}, bf16[16,288,128]{2,1,0:T(8,128)(2,1)S(1)}, u32[]{:S(2)}, u32[]{:S(2)}) %collective-permute-start.15) | collective-permute-done | bytes 1179680 | tf_op jit(solution)/shard_map/ppermute | solution.py:238
  88.7 1.0 copy-done.2
  89.7 1.3 copy-done.3
  91.6 2.6 %copy-done.1 = bf16[1,1408,2048]{2,1,0:T(8,128)(2,1)S(1)} copy-done((bf16[1,1408,2048]{2,1,0:T(8,128)(2,1)S(1)}, bf16[1,1408,2048]{2,1,0:T(8,128)(2,1)}, u32[]{:S(2)}) %copy-start.1) | copy-done | bytes 5767192
  95.2 0.9 copy-done.34
  98.1 8.1 %shard_map.93 = (bf16[2,64,2048]{2,1,0:T(8,128)(2,1)S(1)}, bf16[2,64,2048]{2,1,0:T(8,128)(2,1)S(1)}) custom-call(bf16[64,2048]{1,0:T(8,128)(2,1)S(1)} %copy-done.28, bf16[64,2048]{1,0:T(8,128)(2,1)S(1)} %copy-done.34, bf16[64,2048]{1,0:T(8,128)(2,1)S(1)} %copy-done.36, bf16[64,2048]{1,0:T(8,128)(2,1)S(1)} %copy-done.38, ...), custom_call_target="tpu_custom_call" | custom-call | flops 5033164800 | bytes 19660800 | tf_op jit(solution)/shard_map/pallas_call | solution.py:119
  107.0 9.1 %shard_map.94 = (bf16[2,64,2048]{2,1,0:T(8,128)(2,1)S(1)}, bf16[2,64,2048]{2,1,0:T(8,128)(2,1)S(1)}) custom-call(bf16[64,2048]{1,0:T(8,128)(2,1)S(1)} %copy-done.16, bf16[64,2048]{1,0:T(8,128)(2,1)S(1)} %copy-done.22, bf16[64,2048]{1,0:T(8,128)(2,1)S(1)} %copy-done.24, bf16[64,2048]{1,0:T(8,128)(2,1)S(1)} %copy-done.32, ...), custom_call_target="tpu_custom_call" | custom-call | flops 5033164800 | bytes 19660800 | tf_op jit(solution)/shard_map/pallas_call | solution.py:119
  116.2 1.4 collective-permute-start.19
  117.6 2.7 %collective-permute-done.16 = bf16[2,64,2048]{2,1,0:T(8,128)(2,1)S(1)} collective-permute-done((bf16[2,64,2048]{2,1,0:T(8,128)(2,1)S(1)}, bf16[2,64,2048]{2,1,0:T(8,128)(2,1)S(1)}, u32[]{:S(2)}, u32[]{:S(2)}) %collective-permute-start.16) | collective-permute-done | bytes 524320 | tf_op jit(solution)/shard_map/ppermute | solution.py:230
  120.3 1.5 collective-permute-start.17
  121.9 9.1 %shard_map.95 = (bf16[2,64,2048]{2,1,0:T(8,128)(2,1)S(1)}, bf16[2,64,2048]{2,1,0:T(8,128)(2,1)S(1)}) custom-call(bf16[64,2048]{1,0:T(8,128)(2,1)S(1)} %copy-done.14, bf16[64,2048]{1,0:T(8,128)(2,1)S(1)} %copy-done.18, bf16[64,2048]{1,0:T(8,128)(2,1)S(1)} %copy-done.20, bf16[64,2048]{1,0:T(8,128)(2,1)S(1)} %copy-done.30, ...), custom_call_target="tpu_custom_call" | custom-call | flops 5033164800 | bytes 19660800 | tf_op jit(solution)/shard_map/pallas_call | solution.py:119
  131.1 1.4 collective-permute-start.20
  133.2 9.1 %shard_map.96 = (bf16[2,64,2048]{2,1,0:T(8,128)(2,1)S(1)}, bf16[2,64,2048]{2,1,0:T(8,128)(2,1)S(1)}) custom-call(bf16[64,2048]{1,0:T(8,128)(2,1)S(1)} %bitcast.57, bf16[64,2048]{1,0:T(8,128)(2,1)S(1)} %copy-done.10, bf16[64,2048]{1,0:T(8,128)(2,1)S(1)} %copy-done.12, bf16[64,2048]{1,0:T(8,128)(2,1)S(1)} %copy-done.26, ...), custom_call_target="tpu_custom_call" | custom-call | flops 5033164800 | bytes 19660800 | tf_op jit(solution)/shard_map/pallas_call | solution.py:119
  142.3 1.4 collective-permute-start.25
  143.8 2.4 %collective-permute-start.18 = (bf16[64,2048]{1,0:T(8,128)(2,1)S(1)}, bf16[64,2048]{1,0:T(8,128)(2,1)S(1)}, u32[]{:S(2)}, u32[]{:S(2)}) collective-permute-start(bf16[64,2048]{1,0:T(8,128)(2,1)S(1)} %fusion.4), channel_id=1, source_target_pairs={{0,16},{2,18},{4,20},{6,22},{8,24},{10,26},{12,28},{14,30},{16,0},... | collective-permute-start | bytes 786440 | tf_op jit(solution)/shard_map/ppermute | solution.py:233
  146.3 1.5 collective-permute-start.21
  147.8 1.8 collective-permute-done.22
  150.3 7.0 %collective-permute-done.25 = bf16[2,64,2048]{2,1,0:T(8,128)(2,1)S(1)} collective-permute-done((bf16[2,64,2048]{2,1,0:T(8,128)(2,1)S(1)}, bf16[2,64,2048]{2,1,0:T(8,128)(2,1)S(1)}, u32[]{:S(2)}, u32[]{:S(2)}) %collective-permute-start.25) | collective-permute-done | bytes 524320 | tf_op jit(solution)/shard_map/ppermute | solution.py:230
  158.1 2.1 %collective-permute-done.23 = bf16[64,2048]{1,0:T(8,128)(2,1)S(1)} collective-permute-done((bf16[64,2048]{1,0:T(8,128)(2,1)S(1)}, bf16[64,2048]{1,0:T(8,128)(2,1)S(1)}, u32[]{:S(2)}, u32[]{:S(2)}) %collective-permute-start.23) | collective-permute-done | bytes 262176 | tf_op jit(solution)/shard_map/ppermute | solution.py:230
  160.3 1.5 collective-permute-start.24
  161.8 1.9 %collective-permute-done.26 = bf16[64,2048]{1,0:T(8,128)(2,1)S(1)} collective-permute-done((bf16[64,2048]{1,0:T(8,128)(2,1)S(1)}, bf16[64,2048]{1,0:T(8,128)(2,1)S(1)}, u32[]{:S(2)}, u32[]{:S(2)}) %collective-permute-start.26) | collective-permute-done | bytes 262176 | tf_op jit(solution)/shard_map/ppermute | solution.py:230
  163.8 4.8 %collective-permute-done.24 = bf16[64,2048]{1,0:T(8,128)(2,1)S(1)} collective-permute-done((bf16[64,2048]{1,0:T(8,128)(2,1)S(1)}, bf16[64,2048]{1,0:T(8,128)(2,1)S(1)}, u32[]{:S(2)}, u32[]{:S(2)}) %collective-permute-start.24) | collective-permute-done | bytes 262176 | tf_op jit(solution)/shard_map/ppermute | solution.py:233
  168.8 3.9 %all_to_all.44 = bf16[64,2,1024]{2,0,1:T(8,128)(2,1)S(1)} all-to-all(bf16[64,2,1024]{2,0,1:T(8,128)(2,1)S(1)} %bitcast.68), channel_id=1, replica_groups=mesh['wide'=16,'narrow'=2] {'narrow'}, dimensions={1} | all-to-all | bytes 524288 | tf_op jit(solution)/shard_map/all_to_all | solution.py:325
  (126 shorter events, 19.1 us)
Async XLA Ops:
  6.5 13.5 %copy-start = (f32[128,6]{0,1:T(8,128)S(1)}, f32[128,6]{0,1:T(8,128)}, u32[]{:S(2)}) copy-start(f32[128,6]{0,1:T(8,128)} %param.11) | copy-start | bytes 9220
  6.5 85.0 %all-gather.7.cloned.1.call-start = ((), (), s32[]{:S(2)}) async-start(), calls=%async_computation.3 | async-start | bytes 8650752 | tf_op jit(solution)/shard_map/all_gather | solution.py:273
  11.7 22.5 %copy-start.4 = (bf16[2,8,8,1024]{3,2,0,1:T(8,128)(2,1)}, bf16[2,8,8,1024]{3,2,0,1:T(8,128)(2,1)S(1)}, u32[]{:S(2)}) copy-start(bf16[2,8,8,1024]{3,2,0,1:T(8,128)(2,1)S(1)} %copy.17) | copy-start | bytes 786436
  11.7 13.5 %collective-permute-start = (bf16[64,2048]{1,0:T(8,128)(2,1)S(1)}, bf16[64,2048]{1,0:T(8,128)(2,1)S(1)}, u32[]{:S(2)}, u32[]{:S(2)}) collective-permute-start(bf16[64,2048]{1,0:T(8,128)(2,1)S(1)} %bitcast.52), channel_id=1, source_target_pairs={{0,8},{2,10},{4,12},{6,14},{8,16},{10,18},{12,20},{14,22},{16,24},... | collective-permute-start | bytes 786440 | tf_op jit(solution)/shard_map/ppermute | solution.py:233
  14.8 13.7 %collective-permute-start.1 = (bf16[64,2048]{1,0:T(8,128)(2,1)S(1)}, bf16[64,2048]{1,0:T(8,128)(2,1)S(1)}, u32[]{:S(2)}, u32[]{:S(2)}) collective-permute-start(bf16[64,2048]{1,0:T(8,128)(2,1)S(1)} %bitcast.53), channel_id=1, source_target_pairs={{0,24},{2,26},{4,28},{6,30},{8,0},{10,2},{12,4},{14,6},{16,8},{18,... | collective-permute-start | bytes 786440 | tf_op jit(solution)/shard_map/ppermute | solution.py:233
  16.9 11.6 %collective-permute-start.2 = (bf16[64,2048]{1,0:T(8,128)(2,1)S(1)}, bf16[64,2048]{1,0:T(8,128)(2,1)S(1)}, u32[]{:S(2)}, u32[]{:S(2)}) collective-permute-start(bf16[64,2048]{1,0:T(8,128)(2,1)S(1)} %bitcast.54), channel_id=1, source_target_pairs={{0,2},{2,0},{4,6},{6,4},{8,10},{10,8},{12,14},{14,12},{16,18},{18,... | collective-permute-start | bytes 786440 | tf_op jit(solution)/shard_map/ppermute | solution.py:230
  18.5 10.0 %collective-permute-start.3 = (bf16[64,2048]{1,0:T(8,128)(2,1)S(1)}, bf16[64,2048]{1,0:T(8,128)(2,1)S(1)}, u32[]{:S(2)}, u32[]{:S(2)}) collective-permute-start(bf16[64,2048]{1,0:T(8,128)(2,1)S(1)} %bitcast.55), channel_id=1, source_target_pairs={{0,4},{2,6},{4,0},{6,2},{8,12},{10,14},{12,8},{14,10},{16,20},{18,... | collective-permute-start | bytes 786440 | tf_op jit(solution)/shard_map/ppermute | solution.py:230
  28.5 28.8 %copy-start.11 = (bf16[64,2048]{1,0:T(8,128)(2,1)}, bf16[64,2048]{1,0:T(8,128)(2,1)S(1)}, u32[]{:S(2)}) copy-start(bf16[64,2048]{1,0:T(8,128)(2,1)S(1)} %collective-permute-done.3.refs_2_) | copy-start | bytes 786436
  28.5 63.1 %all-gather.9.cloned.1.call-start = ((), (), s32[]{:S(2)}) async-start(), calls=%async_computation.4 | async-start | bytes 8650752 | tf_op jit(solution)/shard_map/all_gather | solution.py:273
  29.3 62.3 %all-gather.11.cloned.1.call-start = ((), (), s32[]{:S(2)}) async-start(), calls=%async_computation.5 | async-start | bytes 8650752 | tf_op jit(solution)/shard_map/all_gather | solution.py:273
  30.0 9.3 %collective-permute-start.5 = (bf16[64,2048]{1,0:T(8,128)(2,1)S(1)}, bf16[64,2048]{1,0:T(8,128)(2,1)S(1)}, u32[]{:S(2)}, u32[]{:S(2)}) collective-permute-start(bf16[64,2048]{1,0:T(8,128)(2,1)S(1)} %collective-permute-done.refs_0_), channel_id=1, source_target_pairs={{0,2},{2,0},{4,6},{6,4},{8,10},{10,8},{12,14},{14,12},{16,18},{18,... | collective-permute-start | bytes 786440 | tf_op jit(solution)/shard_map/ppermute | solution.py:230
  31.6 11.8 %collective-permute-start.7 = (bf16[64,2048]{1,0:T(8,128)(2,1)S(1)}, bf16[64,2048]{1,0:T(8,128)(2,1)S(1)}, u32[]{:S(2)}, u32[]{:S(2)}) collective-permute-start(bf16[64,2048]{1,0:T(8,128)(2,1)S(1)} %collective-permute-done.refs_0_), channel_id=1, source_target_pairs={{0,4},{2,6},{4,0},{6,2},{8,12},{10,14},{12,8},{14,10},{16,20},{18,... | collective-permute-start | bytes 786440 | tf_op jit(solution)/shard_map/ppermute | solution.py:230
  33.1 10.3 %collective-permute-start.6 = (bf16[64,2048]{1,0:T(8,128)(2,1)S(1)}, bf16[64,2048]{1,0:T(8,128)(2,1)S(1)}, u32[]{:S(2)}, u32[]{:S(2)}) collective-permute-start(bf16[64,2048]{1,0:T(8,128)(2,1)S(1)} %collective-permute-done.1.refs_0_), channel_id=1, source_target_pairs={{0,2},{2,0},{4,6},{6,4},{8,10},{10,8},{12,14},{14,12},{16,18},{18,... | collective-permute-start | bytes 786440 | tf_op jit(solution)/shard_map/ppermute | solution.py:230
  33.6 10.9 %collective-permute-start.8 = (bf16[64,2048]{1,0:T(8,128)(2,1)S(1)}, bf16[64,2048]{1,0:T(8,128)(2,1)S(1)}, u32[]{:S(2)}, u32[]{:S(2)}) collective-permute-start(bf16[64,2048]{1,0:T(8,128)(2,1)S(1)} %collective-permute-done.1.refs_0_), channel_id=1, source_target_pairs={{0,4},{2,6},{4,0},{6,2},{8,12},{10,14},{12,8},{14,10},{16,20},{18,... | collective-permute-start | bytes 786440 | tf_op jit(solution)/shard_map/ppermute | solution.py:230
  34.1 13.0 %collective-permute-start.4 = (bf16[64,2048]{1,0:T(8,128)(2,1)S(1)}, bf16[64,2048]{1,0:T(8,128)(2,1)S(1)}, u32[]{:S(2)}, u32[]{:S(2)}) collective-permute-start(bf16[64,2048]{1,0:T(8,128)(2,1)S(1)} %bitcast.56), channel_id=1, source_target_pairs={{0,16},{2,18},{4,20},{6,22},{8,24},{10,26},{12,28},{14,30},{16,0},... | collective-permute-start | bytes 786440 | tf_op jit(solution)/shard_map/ppermute | solution.py:233
  43.3 41.7 %copy-start.17 = (bf16[64,2048]{1,0:T(8,128)(2,1)}, bf16[64,2048]{1,0:T(8,128)(2,1)S(1)}, u32[]{:S(2)}) copy-start(bf16[64,2048]{1,0:T(8,128)(2,1)S(1)} %collective-permute-done.6.refs_1_) | copy-start | bytes 786436
  47.2 39.0 %copy-start.27 = (bf16[64,2048]{1,0:T(8,128)(2,1)}, bf16[64,2048]{1,0:T(8,128)(2,1)S(1)}, u32[]{:S(2)}) copy-start(bf16[64,2048]{1,0:T(8,128)(2,1)S(1)} %collective-permute-done.4.refs_0_) | copy-start | bytes 786436
  47.2 38.6 %all-to-all-start.1 = ((bf16[16,288,128]{2,1,0:T(8,128)(2,1)}), bf16[16,288,128]{2,1,0:T(8,128)(2,1)S(1)}, u32[]{:S(2)}, u32[]{:S(2)}) async-start(bf16[16,288,128]{2,1,0:T(8,128)(2,1)} %shard_map.91), calls=%async_computation.1 | async-start | bytes 2359296 | tf_op jit(solution)/shard_map/all_to_all | solution.py:281
  52.5 14.8 %collective-permute-start.11 = (bf16[64,2048]{1,0:T(8,128)(2,1)S(1)}, bf16[64,2048]{1,0:T(8,128)(2,1)S(1)}, u32[]{:S(2)}, u32[]{:S(2)}) collective-permute-start(bf16[64,2048]{1,0:T(8,128)(2,1)S(1)} %collective-permute-done.4.refs_0_), channel_id=1, source_target_pairs={{0,2},{2,0},{4,6},{6,4},{8,10},{10,8},{12,14},{14,12},{16,18},{18,... | collective-permute-start | bytes 786440 | tf_op jit(solution)/shard_map/ppermute | solution.py:230
  54.4 26.4 %collective-permute-start.12 = (bf16[64,2048]{1,0:T(8,128)(2,1)S(1)}, bf16[64,2048]{1,0:T(8,128)(2,1)S(1)}, u32[]{:S(2)}, u32[]{:S(2)}) collective-permute-start(bf16[64,2048]{1,0:T(8,128)(2,1)S(1)} %collective-permute-done.4.refs_0_), channel_id=1, source_target_pairs={{0,4},{2,6},{4,0},{6,2},{8,12},{10,14},{12,8},{14,10},{16,20},{18,... | collective-permute-start | bytes 786440 | tf_op jit(solution)/shard_map/ppermute | solution.py:230
  55.9 24.2 %collective-permute-start.10 = (bf16[64,2048]{1,0:T(8,128)(2,1)S(1)}, bf16[64,2048]{1,0:T(8,128)(2,1)S(1)}, u32[]{:S(2)}, u32[]{:S(2)}) collective-permute-start(bf16[64,2048]{1,0:T(8,128)(2,1)S(1)} %collective-permute-done.7.refs_2_), channel_id=1, source_target_pairs={{0,2},{2,0},{4,6},{6,4},{8,10},{10,8},{12,14},{14,12},{16,18},{18,... | collective-permute-start | bytes 786440 | tf_op jit(solution)/shard_map/ppermute | solution.py:230
  57.1 24.3 %collective-permute-start.14 = (bf16[64,2048]{1,0:T(8,128)(2,1)S(1)}, bf16[64,2048]{1,0:T(8,128)(2,1)S(1)}, u32[]{:S(2)}, u32[]{:S(2)}) collective-permute-start(bf16[64,2048]{1,0:T(8,128)(2,1)S(1)} %collective-permute-done.6.refs_1_), channel_id=1, source_target_pairs={{0,4},{2,6},{4,0},{6,2},{8,12},{10,14},{12,8},{14,10},{16,20},{18,... | collective-permute-start | bytes 786440 | tf_op jit(solution)/shard_map/ppermute | solution.py:230
  57.3 27.1 %collective-permute-start.9 = (bf16[64,2048]{1,0:T(8,128)(2,1)S(1)}, bf16[64,2048]{1,0:T(8,128)(2,1)S(1)}, u32[]{:S(2)}, u32[]{:S(2)}) collective-permute-start(bf16[64,2048]{1,0:T(8,128)(2,1)S(1)} %collective-permute-done.3.refs_2_), channel_id=1, source_target_pairs={{0,2},{2,0},{4,6},{6,4},{8,10},{10,8},{12,14},{14,12},{16,18},{18,... | collective-permute-start | bytes 786440 | tf_op jit(solution)/shard_map/ppermute | solution.py:230
  67.2 17.9 %collective-permute-start.13 = (bf16[64,2048]{1,0:T(8,128)(2,1)S(1)}, bf16[64,2048]{1,0:T(8,128)(2,1)S(1)}, u32[]{:S(2)}, u32[]{:S(2)}) collective-permute-start(bf16[64,2048]{1,0:T(8,128)(2,1)S(1)} %collective-permute-done.11.refs_1_), channel_id=1, source_target_pairs={{0,4},{2,6},{4,0},{6,2},{8,12},{10,14},{12,8},{14,10},{16,20},{18,... | collective-permute-start | bytes 786440 | tf_op jit(solution)/shard_map/ppermute | solution.py:230
  85.8 2.8 %collective-permute-start.15 = (bf16[16,288,128]{2,1,0:T(8,128)(2,1)S(1)}, bf16[16,288,128]{2,1,0:T(8,128)(2,1)S(1)}, u32[]{:S(2)}, u32[]{:S(2)}) collective-permute-start(bf16[16,288,128]{2,1,0:T(8,128)(2,1)S(1)} %all-to-all-done.1.refs_0_), channel_id=1, source_target_pairs={{0,1},{1,0},{2,3},{3,2},{4,5},{5,4},{6,7},{7,6},{8,9},{9,8},{10,11... | collective-permute-start | bytes 3538952 | tf_op jit(solution)/shard_map/ppermute | solution.py:238
  98.0 8.9 %copy-start.16 = (bf16[64,2048]{1,0:T(8,128)(2,1)S(1)}, bf16[64,2048]{1,0:T(8,128)(2,1)}, u32[]{:S(2)}) copy-start(bf16[64,2048]{1,0:T(8,128)(2,1)} %copy-done.15) | copy-start | bytes 786436
  98.0 8.9 %copy-start.22 = (bf16[64,2048]{1,0:T(8,128)(2,1)S(1)}, bf16[64,2048]{1,0:T(8,128)(2,1)}, u32[]{:S(2)}) copy-start(bf16[64,2048]{1,0:T(8,128)(2,1)} %copy-done.21) | copy-start | bytes 786436
  98.0 9.0 %copy-start.24 = (bf16[64,2048]{1,0:T(8,128)(2,1)S(1)}, bf16[64,2048]{1,0:T(8,128)(2,1)}, u32[]{:S(2)}) copy-start(bf16[64,2048]{1,0:T(8,128)(2,1)} %copy-done.23) | copy-start | bytes 786436
  98.0 9.0 %copy-start.32 = (bf16[64,2048]{1,0:T(8,128)(2,1)S(1)}, bf16[64,2048]{1,0:T(8,128)(2,1)}, u32[]{:S(2)}) copy-start(bf16[64,2048]{1,0:T(8,128)(2,1)} %copy-done.31) | copy-start | bytes 786436
  106.2 14.0 %collective-permute-start.16 = (bf16[2,64,2048]{2,1,0:T(8,128)(2,1)S(1)}, bf16[2,64,2048]{2,1,0:T(8,128)(2,1)S(1)}, u32[]{:S(2)}, u32[]{:S(2)}) collective-permute-start(bf16[2,64,2048]{2,1,0:T(8,128)(2,1)S(1)} %get-tuple-element.84), channel_id=1, source_target_pairs={{0,2},{2,0},{4,6},{6,4},{8,10},{10,8},{12,14},{14,12},{16,18},{18,... | collective-permute-start | bytes 1572872 | tf_op jit(solution)/shard_map/ppermute | solution.py:230
  107.0 14.9 %copy-start.14 = (bf16[64,2048]{1,0:T(8,128)(2,1)S(1)}, bf16[64,2048]{1,0:T(8,128)(2,1)}, u32[]{:S(2)}) copy-start(bf16[64,2048]{1,0:T(8,128)(2,1)} %copy-done.13) | copy-start | bytes 786436
  107.0 14.9 %copy-start.18 = (bf16[64,2048]{1,0:T(8,128)(2,1)S(1)}, bf16[64,2048]{1,0:T(8,128)(2,1)}, u32[]{:S(2)}) copy-start(bf16[64,2048]{1,0:T(8,128)(2,1)} %copy-done.17) | copy-start | bytes 786436
  107.0 14.8 %copy-start.20 = (bf16[64,2048]{1,0:T(8,128)(2,1)S(1)}, bf16[64,2048]{1,0:T(8,128)(2,1)}, u32[]{:S(2)}) copy-start(bf16[64,2048]{1,0:T(8,128)(2,1)} %copy-done.19) | copy-start | bytes 786436
  107.0 14.8 %copy-start.30 = (bf16[64,2048]{1,0:T(8,128)(2,1)S(1)}, bf16[64,2048]{1,0:T(8,128)(2,1)}, u32[]{:S(2)}) copy-start(bf16[64,2048]{1,0:T(8,128)(2,1)} %copy-done.29) | copy-start | bytes 786436
  116.2 14.9 %collective-permute-start.19 = (bf16[2,64,2048]{2,1,0:T(8,128)(2,1)S(1)}, bf16[2,64,2048]{2,1,0:T(8,128)(2,1)S(1)}, u32[]{:S(2)}, u32[]{:S(2)}) collective-permute-start(bf16[2,64,2048]{2,1,0:T(8,128)(2,1)S(1)} %get-tuple-element.92), channel_id=1, source_target_pairs={{0,4},{2,6},{4,0},{6,2},{8,12},{10,14},{12,8},{14,10},{16,20},{18,... | collective-permute-start | bytes 1572872 | tf_op jit(solution)/shard_map/ppermute | solution.py:230
  120.3 12.9 %copy-start.5 = (bf16[2,8,8,1024]{3,2,0,1:T(8,128)(2,1)S(1)}, bf16[2,8,8,1024]{3,2,0,1:T(8,128)(2,1)}, u32[]{:S(2)}) copy-start(bf16[2,8,8,1024]{3,2,0,1:T(8,128)(2,1)} %copy-done.4) | copy-start | bytes 786436
  120.3 12.9 %copy-start.10 = (bf16[64,2048]{1,0:T(8,128)(2,1)S(1)}, bf16[64,2048]{1,0:T(8,128)(2,1)}, u32[]{:S(2)}) copy-start(bf16[64,2048]{1,0:T(8,128)(2,1)} %copy-done.9) | copy-start | bytes 786436
  120.3 12.9 %copy-start.12 = (bf16[64,2048]{1,0:T(8,128)(2,1)S(1)}, bf16[64,2048]{1,0:T(8,128)(2,1)}, u32[]{:S(2)}) copy-start(bf16[64,2048]{1,0:T(8,128)(2,1)} %copy-done.11) | copy-start | bytes 786436
  120.3 12.9 %copy-start.26 = (bf16[64,2048]{1,0:T(8,128)(2,1)S(1)}, bf16[64,2048]{1,0:T(8,128)(2,1)}, u32[]{:S(2)}) copy-start(bf16[64,2048]{1,0:T(8,128)(2,1)} %copy-done.25) | copy-start | bytes 786436
  120.3 23.4 %collective-permute-start.17 = (bf16[64,2048]{1,0:T(8,128)(2,1)S(1)}, bf16[64,2048]{1,0:T(8,128)(2,1)S(1)}, u32[]{:S(2)}, u32[]{:S(2)}) collective-permute-start(bf16[64,2048]{1,0:T(8,128)(2,1)S(1)} %fusion.5.refs_10_), channel_id=1, source_target_pairs={{0,4},{2,6},{4,0},{6,2},{8,12},{10,14},{12,8},{14,10},{16,20},{18,... | collective-permute-start | bytes 786440 | tf_op jit(solution)/shard_map/ppermute | solution.py:230
  131.1 15.1 %collective-permute-start.20 = (bf16[64,2048]{1,0:T(8,128)(2,1)S(1)}, bf16[64,2048]{1,0:T(8,128)(2,1)S(1)}, u32[]{:S(2)}, u32[]{:S(2)}) collective-permute-start(bf16[64,2048]{1,0:T(8,128)(2,1)S(1)} %fusion.6.refs_10_), channel_id=1, source_target_pairs={{0,2},{2,0},{4,6},{6,4},{8,10},{10,8},{12,14},{14,12},{16,18},{18,... | collective-permute-start | bytes 786440 | tf_op jit(solution)/shard_map/ppermute | solution.py:230
  132.5 17.1 %collective-permute-start.22 = (bf16[2,64,2048]{2,1,0:T(8,128)(2,1)S(1)}, bf16[2,64,2048]{2,1,0:T(8,128)(2,1)S(1)}, u32[]{:S(2)}, u32[]{:S(2)}) collective-permute-start(bf16[2,64,2048]{2,1,0:T(8,128)(2,1)S(1)} %get-tuple-element.100), channel_id=1, source_target_pairs={{0,2},{2,0},{4,6},{6,4},{8,10},{10,8},{12,14},{14,12},{16,18},{18,... | collective-permute-start | bytes 1572872 | tf_op jit(solution)/shard_map/ppermute | solution.py:230
  142.3 14.9 %collective-permute-start.25 = (bf16[2,64,2048]{2,1,0:T(8,128)(2,1)S(1)}, bf16[2,64,2048]{2,1,0:T(8,128)(2,1)S(1)}, u32[]{:S(2)}, u32[]{:S(2)}) collective-permute-start(bf16[2,64,2048]{2,1,0:T(8,128)(2,1)S(1)} %get-tuple-element.107), channel_id=1, source_target_pairs={{0,4},{2,6},{4,0},{6,2},{8,12},{10,14},{12,8},{14,10},{16,20},{18,... | collective-permute-start | bytes 1572872 | tf_op jit(solution)/shard_map/ppermute | solution.py:230
  143.8 18.0 %collective-permute-start.18 = (bf16[64,2048]{1,0:T(8,128)(2,1)S(1)}, bf16[64,2048]{1,0:T(8,128)(2,1)S(1)}, u32[]{:S(2)}, u32[]{:S(2)}) collective-permute-start(bf16[64,2048]{1,0:T(8,128)(2,1)S(1)} %fusion.4), channel_id=1, source_target_pairs={{0,16},{2,18},{4,20},{6,22},{8,24},{10,26},{12,28},{14,30},{16,0},... | collective-permute-start | bytes 786440 | tf_op jit(solution)/shard_map/ppermute | solution.py:233
  146.3 15.5 %collective-permute-start.21 = (bf16[64,2048]{1,0:T(8,128)(2,1)S(1)}, bf16[64,2048]{1,0:T(8,128)(2,1)S(1)}, u32[]{:S(2)}, u32[]{:S(2)}) collective-permute-start(bf16[64,2048]{1,0:T(8,128)(2,1)S(1)} %fusion.3), channel_id=1, source_target_pairs={{0,24},{2,26},{4,28},{6,30},{8,0},{10,2},{12,4},{14,6},{16,8},{18,... | collective-permute-start | bytes 786440 | tf_op jit(solution)/shard_map/ppermute | solution.py:233
  149.7 10.6 %collective-permute-start.23 = (bf16[64,2048]{1,0:T(8,128)(2,1)S(1)}, bf16[64,2048]{1,0:T(8,128)(2,1)S(1)}, u32[]{:S(2)}, u32[]{:S(2)}) collective-permute-start(bf16[64,2048]{1,0:T(8,128)(2,1)S(1)} %fusion.7), channel_id=1, source_target_pairs={{0,4},{2,6},{4,0},{6,2},{8,12},{10,14},{12,8},{14,10},{16,20},{18,... | collective-permute-start | bytes 786440 | tf_op jit(solution)/shard_map/ppermute | solution.py:230
  157.3 6.4 %collective-permute-start.26 = (bf16[64,2048]{1,0:T(8,128)(2,1)S(1)}, bf16[64,2048]{1,0:T(8,128)(2,1)S(1)}, u32[]{:S(2)}, u32[]{:S(2)}) collective-permute-start(bf16[64,2048]{1,0:T(8,128)(2,1)S(1)} %fusion.8), channel_id=1, source_target_pairs={{0,2},{2,0},{4,6},{6,4},{8,10},{10,8},{12,14},{14,12},{16,18},{18,... | collective-permute-start | bytes 786440 | tf_op jit(solution)/shard_map/ppermute | solution.py:230
  160.3 8.2 %collective-permute-start.24 = (bf16[64,2048]{1,0:T(8,128)(2,1)S(1)}, bf16[64,2048]{1,0:T(8,128)(2,1)S(1)}, u32[]{:S(2)}, u32[]{:S(2)}) collective-permute-start(bf16[64,2048]{1,0:T(8,128)(2,1)S(1)} %fusion.2), channel_id=1, source_target_pairs={{0,8},{2,10},{4,12},{6,14},{8,16},{10,18},{12,20},{14,22},{16,24},... | collective-permute-start | bytes 786440 | tf_op jit(solution)/shard_map/ppermute | solution.py:233
  (22 other events, 30.4 us)
Sparse Core Ops, SparseCore 0:
  28.6 15.9 all-gather.6
  46.2 17.1 all-gather.8
  64.9 17.1 all-gather.10
